TPU v7x, 32 devices: a whole 2x2x4 slice. The times are simulated.
32 devices in a mesh: users: 8 (over z, y), items: 4 (over x, core).
Axes of the slice: x: 2, y: 2, z: 4, core: 2. Of those that a mesh axis runs over, the one named last changes fastest.
Arguments:
- user_factor: bfloat16 [16384, 256], P('users'), may hold values from -2.390625 to 2.390625
- hot_factor: bfloat16 [512, 256], replicated, may hold values from -2.390625 to 2.390625
- cold_factor: bfloat16 [8192, 256], P(('users', 'items')), may hold values from -2.390625 to 2.390625
- hour_factor: bfloat16 [168, 256], replicated, may hold values from -2.390625 to 2.390625
- block_user: int32 [32, 512], P(('users', 'items')), may hold values from 0 to 2047
- block_slot: int32 [32, 512], P(('users', 'items')), may hold values from 0 to 47
- block_hour: int32 [32, 512], P(('users', 'items')), may hold values from 0 to 20
- block_count: int32 [32], P(('users', 'items')), may hold values from 128 to 512, as said below
- need_rows: int32 [32, 8, 2], P(('users', 'items')), may hold values from 0 to 15
- observed: bfloat16 [32, 512, 128], P(('users', 'items')), may hold values from 0 to 1, as said below
Outputs:
- user_grad: float32 [16384, 256], P(('users', 'items'))
- cold_grad: float32 [8192, 256], P(('users', 'items'))
- hot_grad: float32 [512, 256], P(('users', 'items'))
- hour_grad: float32 [168, 256], replicated
Inputs may be any that keep to these rules, and one draw needn't show every extreme that they name: `block_count`: some device has all 512 slots live. `observed`: every entry is 0 or 1.
All inputs are finite; a program needn't handle non-finite values.
Results may differ from a plain program's by a relative error of at most 0.0029.
Values may be sent and summed in bfloat16 or wider, within the bound.
No kernel may reach another device: no remote copies, remote signals or barrier semaphores. Data moves between devices by JAX's collectives and lax.ppermute only.
A program may use at most 128 MiB of HBM per device.

v0:
```python
import jax
import jax.numpy as jnp
from jax import lax
from jax.sharding import PartitionSpec as P

IB = 16
HB = 8


def body(
    user_factor,
    hot_factor,
    cold_factor,
    hour_factor,
    block_user,
    block_slot,
    block_hour,
    block_count,
    need_rows,
    observed,
):
    rank_size = user_factor.shape[1]
    hour_count = hour_factor.shape[0]
    hour_blocks = hour_count // HB
    hot_rows = hot_factor.shape[0]
    shard_len = cold_factor.shape[0]
    peer_count = lax.axis_size("users")
    requests = need_rows[0]
    req_count = requests.shape[1]
    offsets = jnp.arange(IB, dtype=jnp.int32)
    asked_rows = lax.all_to_all(requests, "users", split_axis=0, concat_axis=0, tiled=True)
    served_rows = (asked_rows[:, :, None] * IB + offsets).reshape(peer_count, req_count * IB)
    fetched = lax.all_to_all(
        cold_factor[served_rows], "users", split_axis=0, concat_axis=0, tiled=True
    ).reshape(-1, rank_size)
    item_table = jnp.concatenate([hot_factor, fetched], axis=0)
    hour_table = hour_factor.reshape(hour_blocks, HB * rank_size)
    block_total = block_user.shape[1]
    group_len = min(block_total, 512)
    groups = block_total // group_len
    live_count = block_count[0]
    data = (
        block_user[0].reshape(groups, group_len),
        block_slot[0].reshape(groups, group_len),
        block_hour[0].reshape(groups, group_len),
        jnp.arange(block_total, dtype=jnp.int32).reshape(groups, group_len),
        observed[0].reshape(groups, group_len, IB, HB),
    )
    block_ids = jnp.arange(hour_blocks, dtype=jnp.int32)

    def one_group(carry, group_data):
        grad_user, grad_item, grad_hour = carry
        users_idx, slots_idx, hours_idx, position, obs = group_data
        user_rows = user_factor[users_idx]
        item_idx = slots_idx[:, None] * IB + offsets
        item_rows = item_table[item_idx]
        hour_onehot = (hours_idx[:, None] == block_ids).astype(jnp.bfloat16)
        hour_rows = jnp.dot(hour_onehot, hour_table, preferred_element_type=jnp.float32)
        hour_rows = hour_rows.astype(jnp.bfloat16).reshape(group_len, HB, rank_size)
        user_item = (
            user_rows.astype(jnp.float32)[:, None, :] * item_rows.astype(jnp.float32)
        ).astype(jnp.bfloat16)
        model = jnp.einsum("gar,gbr->gab", user_item, hour_rows, preferred_element_type=jnp.float32)
        live_mask = position < live_count
        residual = jnp.where(
            live_mask[:, None, None], jax.nn.sigmoid(model) - obs.astype(jnp.float32), 0.0
        )
        residual = residual.astype(jnp.bfloat16)
        weighted = jnp.einsum(
            "gab,gbr->gar", residual, hour_rows, preferred_element_type=jnp.float32
        )
        item_terms = weighted * user_rows.astype(jnp.float32)[:, None, :]
        user_terms = jnp.sum(weighted * item_rows.astype(jnp.float32), axis=1)
        hour_terms = jnp.einsum(
            "gab,gar->gbr", residual, user_item, preferred_element_type=jnp.float32
        )
        grad_user = grad_user.at[users_idx].add(user_terms)
        grad_item = grad_item.at[item_idx.reshape(-1)].add(item_terms.reshape(-1, rank_size))
        grad_hour = grad_hour.at[hours_idx].add(hour_terms.reshape(group_len, HB * rank_size))
        return ((grad_user, grad_item, grad_hour), None)

    start = (
        jnp.zeros((user_factor.shape[0], rank_size), jnp.float32),
        jnp.zeros((item_table.shape[0], rank_size), jnp.float32),
        jnp.zeros((hour_blocks, HB * rank_size), jnp.float32),
    )
    (grad_user, grad_item, grad_hour), _ = lax.scan(one_group, start, data)
    cold_part = grad_item[hot_rows:]
    returned = lax.all_to_all(
        cold_part.reshape(peer_count, req_count * IB, rank_size),
        "users",
        split_axis=0,
        concat_axis=0,
        tiled=True,
    )
    cold_grad = (
        jnp.zeros((shard_len, rank_size), jnp.float32)
        .at[served_rows.reshape(-1)]
        .add(returned.reshape(-1, rank_size))
    )
    hot_grad = lax.psum_scatter(
        grad_item[:hot_rows], ("users", "items"), scatter_dimension=0, tiled=True
    )
    user_grad = lax.psum_scatter(grad_user, "items", scatter_dimension=0, tiled=True)
    hour_grad = lax.psum(grad_hour, ("users", "items")).reshape(hour_count, rank_size)
    return (user_grad, cold_grad, hot_grad, hour_grad)


def solution(mesh):
    in_specs = (
        P("users", None),
        P(),
        P(("users", "items"), None),
        P(),
        P(("users", "items"), None),
        P(("users", "items"), None),
        P(("users", "items"), None),
        P(("users", "items")),
        P(("users", "items"), None, None),
        P(("users", "items"), None, None),
    )
    out_specs = (
        P(("users", "items"), None),
        P(("users", "items"), None),
        P(("users", "items"), None),
        P(),
    )
    return jax.shard_map(body, mesh=mesh, in_specs=in_specs, out_specs=out_specs, check_vma=False)
```

profile of v0, /device:TPU:0, one launch (start us, length us, event | category | flops | bytes accessed | tf_op | source)
XLA Modules:
  0.0 399.0 jit_solution(18010390556952559091)
XLA Ops:
  7.2 1.5 copy.23
  8.6 7.3 %all-to-all-start = ((s32[8,1,2]{2,1,0:T(1,128)}), s32[8,1,2]{2,1,0:T(1,128)S(1)}, u32[]{:S(2)}, u32[]{:S(2)}) async-start(s32[8,1,2]{2,1,0:T(1,128)} %copy.23), calls=%async_computation | async-start | bytes 8192 | tf_op jit(solution)/shard_map/all_to_all | solution.py:31
  19.5 1.6 reshape.275
  24.2 1.7 convolution_convert_fusion
  27.5 1.8 gather_fusion.1
  29.3 6.0 %all-to-all-start.1 = ((bf16[8,32,256]{2,1,0:T(8,128)(2,1)}), bf16[8,32,256]{2,1,0:T(8,128)(2,1)}, u32[]{:S(2)}, u32[]{:S(2)}) async-start(bf16[8,32,256]{2,1,0:T(8,128)(2,1)} %bitcast.47), calls=%async_computation.1 | async-start | bytes 262144 | tf_op jit(solution)/shard_map/all_to_all | solution.py:33
  36.5 2.7 gather_fusion
  39.2 1.8 convert_element_type.35
  41.0 2.0 copy.28
  43.0 2.0 copy.27
  46.1 32.9 %gather_fusion.2 = bf16[8192,256]{1,0:T(8,128)(2,1)} fusion(bf16[768,256]{1,0:T(8,128)(2,1)S(1)} %pad_maximum_fusion, s32[8192]{0:T(1024)S(1)} %broadcast_clamp_fusion), kind=kCustom, calls=%fused_computation.2 | custom fusion | bytes 8421376 | tf_op jit(solution)/shard_map/while/body/eval_jaxpr/gather | solution.py:56
  79.0 5.0 %select_convert_fusion = bf16[512,16,8]{1,2,0:T(8,128)(2,1)S(1)} fusion(f32[512,16,8]{1,2,0:T(8,128)} %copy.27, bf16[512,8,256]{2,1,0:T(8,128)(2,1)} %bitcast.44, bf16[512,16,256]{2,1,0:T(8,128)(2,1)} %bitcast.39, f32[512,256]{1,0:T(8,128)S(1)} %copy-done.4, pred[512]{0:T(512)(128)(4,1)S(1)} %iota_compare_fusion.2), kind=kOutput, calls=%fused_computation.15 | convolution fusion | flops 40239104 | bytes 7209472 | tf_op jit(solution)/shard_map/while/body/eval_jaxpr/gar,gbr->gab/dot_general | solution.py:63
  85.1 3.9 copy.29
  89.0 8.7 %scatter_custom_fusion.3 = f32[21,2048]{1,0:T(8,128)S(1)} fusion(s32[512]{0:T(512)} %bitcast.55, f32[512,2048]{1,0:T(8,128)} %bitcast.46, f32[]{:T(128)} %constant.13.clone.1), kind=kCustom, calls=%fused_computation.29 | custom fusion | flops 1048576 | bytes 172544 | tf_op jit(solution)/shard_map/while/body/eval_jaxpr/scatter-add | solution.py:79
  98.5 9.2 %broadcast_multiply_fusion = (f32[512,16,256]{2,1,0:T(8,128)}, f32[512,256]{1,0:T(8,128)}) fusion(f32[512,256]{1,0:T(8,128)} %convert_element_type.35, bf16[8192,256]{1,0:T(8,128)(2,1)} %gather_fusion.2, bf16[512,16,8]{1,2,0:T(8,128)(2,1)} %copy-done.5, bf16[512,8,256]{2,1,0:T(8,128)(2,1)S(1)} %bitcast.45), kind=kOutput, calls=%fused_computation.11 | convolution fusion | flops 41811968 | bytes 15859712 | tf_op jit(solution)/shard_map/while/body/eval_jaxpr/gab,gbr->gar/dot_general | solution.py:69
  107.6 44.8 %scatter_custom_fusion.1 = f32[768,256]{1,0:T(8,128)S(1)} fusion(s32[8192]{0:T(1024)} %bitcast.49, f32[8192,256]{1,0:T(8,128)} %bitcast.42, f32[]{:T(128)} %constant.13.clone.1), kind=kCustom, calls=%fused_computation.20 | custom fusion | flops 2097152 | bytes 786944 | tf_op jit(solution)/shard_map/while/body/eval_jaxpr/scatter-add | solution.py:78
  153.4 5.5 %scatter_custom_fusion = f32[2048,256]{1,0:T(8,128)} fusion(s32[512]{0:T(512)} %bitcast.54, f32[512,256]{1,0:T(8,128)} %get-tuple-element.35, f32[]{:T(128)} %constant.13.clone.1), kind=kCustom, calls=%fused_computation.16 | custom fusion | flops 131072 | bytes 2097664 | tf_op jit(solution)/shard_map/while/body/eval_jaxpr/scatter-add | solution.py:77
  159.6 5.9 %all-to-all-start.2 = ((f32[8,32,256]{2,1,0:T(8,128)}), f32[8,32,256]{2,1,0:T(8,128)S(1)}, u32[]{:S(2)}, u32[]{:S(2)}) async-start(f32[8,32,256]{2,1,0:T(8,128)} %bitcast.14), calls=%async_computation.3 | async-start | bytes 524288 | tf_op jit(solution)/shard_map/all_to_all | solution.py:89
  165.7 8.1 %all-to-all-done.2 = f32[8,32,256]{2,1,0:T(8,128)S(1)} async-done(((f32[8,32,256]{2,1,0:T(8,128)}), f32[8,32,256]{2,1,0:T(8,128)S(1)}, u32[]{:S(2)}, u32[]{:S(2)}) %all-to-all-start.2) | async-done | bytes 262176 | tf_op jit(solution)/shard_map/all_to_all | solution.py:89
  173.8 2.6 scatter_custom_fusion.2
  176.4 45.4 %all-reduce.2.cloned.1.call-done = f32[168,256]{1,0:T(8,128)} async-done(((f32[168,256]{1,0:T(8,128)}), f32[168,256]{1,0:T(8,128)}) %all-reduce.2.cloned.1.call-update) | async-done | bytes 172048 | tf_op jit(solution)/shard_map/psum | solution.py:105
  221.8 138.5 %reduce-scatter.5.cloned.1.call-done = f32[16,256]{1,0:T(8,128)} async-done(((f32[512,256]{1,0:T(8,128)}), f32[16,256]{1,0:T(8,128)}) %reduce-scatter.5.cloned.1.call-update) | async-done | bytes 16400 | tf_op jit(solution)/shard_map/reduce_scatter | solution.py:101
  360.3 30.6 %reduce-scatter.3.cloned.1.call-done = f32[512,256]{1,0:T(8,128)} async-done(((f32[2048,256]{1,0:T(8,128)}), f32[512,256]{1,0:T(8,128)}) %reduce-scatter.3.cloned.1.call-update) | async-done | bytes 524304 | tf_op jit(solution)/shard_map/reduce_scatter | solution.py:104
  390.9 1.6 copy.32
  (53 shorter events, 13.4 us)
Async XLA Ops:
  7.2 29.3 %copy-start = (bf16[2048,256]{1,0:T(8,128)(2,1)S(1)}, bf16[2048,256]{1,0:T(8,128)(2,1)}, u32[]{:S(2)}) copy-start(bf16[2048,256]{1,0:T(8,128)(2,1)} %param.10) | copy-start | bytes 3145732
  7.2 20.3 %copy-start.2 = (bf16[256,256]{1,0:T(8,128)(2,1)S(1)}, bf16[256,256]{1,0:T(8,128)(2,1)}, u32[]{:S(2)}) copy-start(bf16[256,256]{1,0:T(8,128)(2,1)} %param.12) | copy-start | bytes 393220
  8.6 17.8 %all-to-all-start = ((s32[8,1,2]{2,1,0:T(1,128)}), s32[8,1,2]{2,1,0:T(1,128)S(1)}, u32[]{:S(2)}, u32[]{:S(2)}) async-start(s32[8,1,2]{2,1,0:T(1,128)} %copy.23), calls=%async_computation | async-start | bytes 8192 | tf_op jit(solution)/shard_map/all_to_all | solution.py:31
  18.9 0.6 copy-start.6
  29.3 15.7 %all-to-all-start.1 = ((bf16[8,32,256]{2,1,0:T(8,128)(2,1)}), bf16[8,32,256]{2,1,0:T(8,128)(2,1)}, u32[]{:S(2)}, u32[]{:S(2)}) async-start(bf16[8,32,256]{2,1,0:T(8,128)(2,1)} %bitcast.47), calls=%async_computation.1 | async-start | bytes 262144 | tf_op jit(solution)/shard_map/all_to_all | solution.py:33
  35.3 186.5 %all-reduce.2.cloned.1.call-start = ((), (), s32[]{:S(2)}) async-start(), calls=%async_computation.7 | async-start | bytes 344064 | tf_op jit(solution)/shard_map/psum | solution.py:105
  46.1 32.9 %copy-start.4 = (f32[512,256]{1,0:T(8,128)S(1)}, f32[512,256]{1,0:T(8,128)}, u32[]{:S(2)}) copy-start(f32[512,256]{1,0:T(8,128)} %convert_element_type.35) | copy-start | bytes 1572868
  79.0 5.0 %copy-start.1 = (bf16[8192,256]{1,0:T(8,128)(2,1)S(1)}, bf16[8192,256]{1,0:T(8,128)(2,1)}, u32[]{:S(2)}) copy-start(bf16[8192,256]{1,0:T(8,128)(2,1)} %gather_fusion.2) | copy-start | bytes 12582916
  84.1 1.1 copy-start.5
  85.1 13.3 %copy-start.3 = (bf16[64,8,8,256]{3,2,1,0:T(8,128)(2,1)S(1)}, bf16[64,8,8,256]{3,2,1,0:T(8,128)(2,1)}, u32[]{:S(2)}) copy-start(bf16[64,8,8,256]{3,2,1,0:T(8,128)(2,1)} %copy.28) | copy-start | bytes 6291460
  98.4 261.8 %reduce-scatter.5.cloned.1.call-start = ((), (), s32[]{:S(2)}) async-start(), calls=%async_computation.6 | async-start | bytes 540672 | tf_op jit(solution)/shard_map/reduce_scatter | solution.py:101
  153.3 237.6 %reduce-scatter.3.cloned.1.call-start = ((), (), s32[]{:S(2)}) async-start(), calls=%async_computation.5 | async-start | bytes 2621440 | tf_op jit(solution)/shard_map/reduce_scatter | solution.py:104
  159.6 14.2 %all-to-all-start.2 = ((f32[8,32,256]{2,1,0:T(8,128)}), f32[8,32,256]{2,1,0:T(8,128)S(1)}, u32[]{:S(2)}, u32[]{:S(2)}) async-start(f32[8,32,256]{2,1,0:T(8,128)} %bitcast.14), calls=%async_computation.3 | async-start | bytes 524288 | tf_op jit(solution)/shard_map/all_to_all | solution.py:89
Sparse Core Ops, SparseCore 0:
  98.5 123.2 all-reduce.1
  224.6 135.6 reduce-scatter.4
  363.5 27.3 reduce-scatter.2
where the time goes:
time: 400 us; the launch traced here: 399 us
  waiting for transfers between devices  223 us (56%)
  other arithmetic  69.9 us (17%)
  local copies, waits for them, and re-layouts  55.7 us (14%)
  starting transfers between devices  19.3 us (5%)
  matrix products  16.8 us (4%)
  between operations  14.6 us (4%)
    reduce_scatter x1, waiting for transfers between devices, body(): lax.psum_scatter(grad_item[:hot_rows], ('users', 'items'), scatter_dimens...  138 us
    psum x1, waiting for transfers between devices, body(): lax.psum(grad_hour, ('users', 'items')).reshape(hour_count, rank_size)  45.4 us
    scatter-add x1, other arithmetic, one_group(): grad_item.at[item_idx.reshape(-1)].add(item_terms.reshape(-1, rank_size))  44.8 us
    gather x1, local copies, waits for them, and re-layouts, one_group(): item_rows = item_table[item_idx]  32.9 us
    reduce_scatter x1, waiting for transfers between devices, body(): lax.psum_scatter(grad_user, 'items', scatter_dimension=0, tiled=True)  30.6 us
    dot_general x1, matrix products, one_group(): jnp.einsum('gab,gbr->gar', residual, hour_rows, preferred_element_type=jn...  9.17 us
    scatter-add x1, other arithmetic, one_group(): grad_hour.at[hours_idx].add(hour_terms.reshape(group_len, HB * rank_size))  8.67 us
    unnamed x18, local copies, waits for them, and re-layouts  8.63 us
  transfers between devices with their start and end apart: 6, of which 4 were waited for; matrix products, arithmetic and copies ran while one was open for 21% of the time, Pallas kernels for 0%

commit v1 on v0

v1 whole, which is shorter than its diff:
```python
import functools

import jax
import jax.numpy as jnp
from jax import lax
from jax.experimental import pallas as pl
from jax.experimental.pallas import tpu as pltpu
from jax.sharding import PartitionSpec as P

IB = 16
HB = 8
HALF = 128
F32 = jnp.float32
BF16 = jnp.bfloat16


def bits_of(size):
    return size.bit_length() - 1


def flip(value, bits):
    out = jnp.zeros_like(value)
    for k in range(bits):
        out = out | (((value >> k) & 1) << (bits - 1 - k))
    return out


def hour_of(lane, split, hours):
    half = hours // 2
    inside = lane & (HALF - 1)
    hour = ((lane >> 7) ^ split) * half + inside
    return hour, inside < half


def kernel(
    sizes, ids, count, user, slot, hour, user_tab, hot, cold, hours_tab, observed,
    grad_user, grad_item, grad_hour,
    table, item_sums, user_rows, user_terms, obs, live_hour,
):
    peers, items, hot_slots, reqs, hours, permute_hot = sizes
    p, q = ids[0], ids[1]
    blocks = user.shape[1]
    users = user_tab.shape[0]
    slots = table.shape[1] // IB
    user_chunk = users // items
    parts = range(table.shape[0])

    for part in parts:
        lanes = slice(part * 128, part * 128 + 128)
        table[part, : hot.shape[0], :] = hot[:, lanes].astype(F32)
        table[part, hot.shape[0] :, :] = cold[:, lanes].astype(F32)

    def column(row):
        parts = [
            jnp.transpose(jnp.broadcast_to(row[:, k : k + 128], (128, 128))) for k in range(0, blocks, 128)
        ]
        return jnp.concatenate(parts, axis=0)

    def spread(col, lanes):
        return jnp.concatenate([col] * (-(-lanes // 128)), axis=1)[:, :lanes]

    user_row, slot_row = user[...], slot[...]
    place = lax.broadcasted_iota(jnp.int32, (1, blocks), 1)
    hour_row = jnp.where(place < count[0], hour[...], -1)
    user_col, slot_col = column(user_row), column(slot_row)
    hour_col = column(hour_row)

    step = 512
    acc = jnp.zeros((blocks, user_tab.shape[1]), F32)
    for k in range(0, users, step):
        lane = lax.broadcasted_iota(jnp.int32, (blocks, step), 1) + k
        hit = (spread(user_col, step) == lane).astype(F32).astype(BF16)
        acc += jnp.dot(hit, user_tab[k : k + step, :], preferred_element_type=F32)
    user_rows[...] = acc
    user_terms[...] = jnp.zeros_like(user_terms)
    grad_hour[...] = jnp.zeros_like(grad_hour)

    pick = (spread(slot_col, slots) == lax.broadcasted_iota(jnp.int32, (blocks, slots), 1)).astype(F32).astype(BF16)
    user_bits, all_bits = bits_of(peers), bits_of(peers * items)
    cold_slot = slot_row - hot_slots
    cold_pos = hot_slots + flip((cold_slot // reqs) ^ p, user_bits) * reqs + cold_slot % reqs
    hot_pos = flip(slot_row ^ (p * items + q), all_bits) if permute_hot else slot_row
    put_pos = jnp.where(slot_row < hot_slots, hot_pos, cold_pos)
    put = (put_pos == lax.broadcasted_iota(jnp.int32, (slots, blocks), 0)).astype(F32).astype(BF16)

    lane = lax.broadcasted_iota(jnp.int32, (blocks, 2 * HALF), 1)
    lane_hour, used = hour_of(lane, q & 1, hours)
    mask = used & ((lane_hour // HB) == spread(hour_col, 2 * HALF))
    live_hour[...] = mask.astype(F32)
    obs[...] = 0.5 - observed[...].astype(F32)
    lane_hour, used = hour_of(lax.broadcasted_iota(jnp.int32, (IB * HB, 2 * HALF), 1), q & 1, hours)
    cell = lax.broadcasted_iota(jnp.int32, (IB * HB, 2 * HALF), 0)
    tile = (used & ((cell & (HB - 1)) == (lane_hour & (HB - 1)))).astype(F32).astype(BF16)

    cell_item = lax.broadcasted_iota(jnp.int32, (blocks, IB * HB), 1) // HB
    hours_half = hours_tab[...] * jnp.asarray(0.5, BF16)

    def one(a):
        of_place = pl.ds(a, slots, stride=IB)
        choice = jnp.concatenate([table[part, of_place, :] for part in parts], axis=1).astype(BF16)
        rows = jnp.dot(pick, choice, preferred_element_type=F32)
        users_f = user_rows[...]
        user_item = (users_f * rows).astype(BF16)
        half_model = lax.dot_general(
            user_item, hours_half, (((1,), (1,)), ((), ())), preferred_element_type=F32
        )
        seen = jnp.dot(
            jnp.where(cell_item == a, obs[...], 0.0).astype(BF16), tile, preferred_element_type=F32
        )
        residual = ((0.5 * jnp.tanh(half_model) + seen) * live_hour[...]).astype(BF16)
        weighted = jnp.dot(residual, hours_tab[...], preferred_element_type=F32)
        grad_hour[...] += lax.dot_general(
            residual, user_item, (((0,), (0,)), ((), ())), preferred_element_type=F32
        )
        user_terms[...] += weighted * rows
        terms = weighted * users_f
        high = terms.astype(BF16)
        low = (terms - high.astype(F32)).astype(BF16)
        total = jnp.dot(put, high, preferred_element_type=F32) + jnp.dot(put, low, preferred_element_type=F32)
        for part in parts:
            item_sums[part, of_place, :] = total[:, part * 128 : part * 128 + 128]

    def loop(a, carry):
        one(a)
        return carry

    lax.fori_loop(0, IB, loop, 0)

    for part in parts:
        grad_item[:, part * 128 : part * 128 + 128] = item_sums[part]

    terms = user_terms[...]
    high = terms.astype(BF16)
    low = (terms - high.astype(F32)).astype(BF16)
    item_bits = bits_of(items)
    user_pos = flip((user_row // user_chunk) ^ q, item_bits) * user_chunk + user_row % user_chunk
    for k in range(0, users, step):
        hit = (user_pos == lax.broadcasted_iota(jnp.int32, (step, blocks), 0) + k).astype(F32).astype(BF16)
        grad_user[k : k + step, :] = jnp.dot(hit, high, preferred_element_type=F32) + jnp.dot(
            hit, low, preferred_element_type=F32
        )


def hop(values, axis, size, bit):
    return lax.ppermute(values, axis, [(i, i ^ (1 << bit)) for i in range(size)])


def halves(values):
    rows = values.shape[0] // 2
    return values[:rows], values[rows:]


def body(
    user_factor,
    hot_factor,
    cold_factor,
    hour_factor,
    block_user,
    block_slot,
    block_hour,
    block_count,
    need_rows,
    observed,
):
    rank_size = user_factor.shape[1]
    hours = hour_factor.shape[0]
    hot_rows = hot_factor.shape[0]
    shard_len = cold_factor.shape[0]
    peers, items = lax.axis_size("users"), lax.axis_size("items")
    p, q = lax.axis_index("users"), lax.axis_index("items")
    requests = need_rows[0]
    reqs = requests.shape[1]
    offsets = jnp.arange(IB, dtype=jnp.int32)
    asked = lax.all_to_all(requests, "users", split_axis=0, concat_axis=0, tiled=True)
    served_rows = (asked[:, :, None] * IB + offsets).reshape(-1)
    fetched = lax.all_to_all(
        cold_factor[served_rows].reshape(peers, reqs * IB, rank_size), "users", split_axis=0, concat_axis=0, tiled=True
    ).reshape(-1, rank_size)

    half = hours // 2
    pad = jnp.zeros((HALF - half, rank_size), BF16)
    low, high = halves(hour_factor)
    swap = (q & 1) == 1
    hour_table = jnp.concatenate([jnp.where(swap, high, low), pad, jnp.where(swap, low, high), pad], axis=0)

    blocks = block_user.shape[1]
    hot_slots = hot_rows // IB
    slots = hot_slots + peers * reqs
    permute_hot = hot_rows == IB * peers * items
    sizes = (peers, items, hot_slots, reqs, hours, permute_hot)
    vmem = pl.BlockSpec(memory_space=pltpu.VMEM)
    smem = pl.BlockSpec(memory_space=pltpu.SMEM)
    grad_user, grad_item, grad_hour = pl.pallas_call(
        functools.partial(kernel, sizes),
        out_shape=(
            jax.ShapeDtypeStruct(user_factor.shape, F32),
            jax.ShapeDtypeStruct((slots * IB, rank_size), F32),
            jax.ShapeDtypeStruct((2 * HALF, rank_size), F32),
        ),
        in_specs=[smem, smem] + [vmem] * 8,
        out_specs=(vmem, vmem, vmem),
        scratch_shapes=[
            pltpu.VMEM((rank_size // 128, slots * IB, 128), F32),
            pltpu.VMEM((rank_size // 128, slots * IB, 128), F32),
            pltpu.VMEM((blocks, rank_size), F32),
            pltpu.VMEM((blocks, rank_size), F32),
            pltpu.VMEM((blocks, IB * HB), F32),
            pltpu.VMEM((blocks, 2 * HALF), F32),
        ],
        compiler_params=pltpu.CompilerParams(vmem_limit_bytes=48 * 1024 * 1024),
        name="blocks",
    )(
        jnp.stack([p, q]).astype(jnp.int32),
        block_count,
        block_user,
        block_slot,
        block_hour,
        user_factor,
        hot_factor,
        fetched,
        hour_table,
        observed[0],
    )

    returned = grad_item[hot_rows:].astype(BF16).reshape(-1, reqs * IB, rank_size)
    hot = grad_item[:hot_rows]
    user = grad_user
    mine, other = halves(grad_hour)
    mine, other = mine[:half], other[:half]

    for bit in range(bits_of(items)):
        keep, send = halves(user)
        user = keep + hop(send.astype(BF16), "items", items, bit).astype(F32)
        if permute_hot:
            keep, send = halves(hot)
            hot = keep + hop(send.astype(BF16), "items", items, bit).astype(F32)
        if bit == 0:
            mine = mine + hop(other, "items", items, bit)
        else:
            mine = mine + hop(mine, "items", items, bit)
    for bit in range(bits_of(peers)):
        if permute_hot:
            keep, send = halves(hot)
            hot = keep + hop(send, "users", peers, bit)
        mine = mine + hop(mine, "users", peers, bit)
        size = returned.shape[0] // 2
        keep, send = returned[:size], returned[size:]
        returned = jnp.concatenate([keep, hop(send, "users", peers, bit)], axis=1)
    other = hop(mine, "items", items, 0)
    hour_grad = jnp.concatenate([jnp.where(swap, other, mine), jnp.where(swap, mine, other)], axis=0)
    if not permute_hot:
        hot = lax.psum_scatter(hot, ("users", "items"), scatter_dimension=0, tiled=True)

    returned = returned.reshape(peers, reqs, IB, rank_size)
    source = jnp.arange(peers, dtype=jnp.int32) ^ p
    wanted = asked[source].reshape(-1)
    shard_blocks = shard_len // IB
    hit = (jnp.arange(shard_blocks, dtype=jnp.int32)[:, None] == wanted[None, :]).astype(BF16)
    cold_grad = jnp.dot(hit, returned.reshape(peers * reqs, IB * rank_size), preferred_element_type=F32)
    return (user, cold_grad.reshape(shard_len, rank_size), hot, hour_grad)


def solution(mesh):
    in_specs = (
        P("users", None),
        P(),
        P(("users", "items"), None),
        P(),
        P(("users", "items"), None),
        P(("users", "items"), None),
        P(("users", "items"), None),
        P(("users", "items")),
        P(("users", "items"), None, None),
        P(("users", "items"), None, None),
    )
    out_specs = (
        P(("users", "items"), None),
        P(("users", "items"), None),
        P(("users", "items"), None),
        P(),
    )
    return jax.shard_map(body, mesh=mesh, in_specs=in_specs, out_specs=out_specs, check_vma=False)
```

time: 400 us -> 89.9 us (0.22)
  waiting for transfers between devices: 223 us -> 26.7 us
  other arithmetic: 69.9 us -> 6.14 us
  local copies, waits for them, and re-layouts: 55.7 us -> 13.6 us
  matrix products: 16.8 us -> 0.16 us
  Pallas kernels: 0 us -> 15 us
  between operations: 14.6 us -> 1.51 us
  starting transfers between devices: 19.3 us -> 26.2 us
    reduce_scatter x2 -> x0, waiting for transfers between devices: 169 us -> none  [the longest x1 138 us: body(): lax.psum_scatter(grad_item[:hot_rows], ('users', 'items'), scatter_dimens...]
    scatter-add x4 -> x0, other arithmetic: 61.5 us -> none  [the longest x1 44.8 us: one_group(): grad_item.at[item_idx.reshape(-1)].add(item_terms.reshape(-1, rank_size))]
    psum x1 -> x0, waiting for transfers between devices: 45.4 us -> none  [body(): lax.psum(grad_hour, ('users', 'items')).reshape(hour_count, rank_size)]
    gather x3 -> x2, local copies, waits for them, and re-layouts: 37.5 us -> 2.36 us  [the longest x1 1.81 us: body(): cold_factor[served_rows].reshape(peers, reqs * IB, rank_size)]
    dot_general x4 -> x1, matrix products: 16.8 us -> 0.16 us  [body(): jnp.dot(hit, returned.reshape(peers * reqs, IB * rank_size), preferred_el...]
    ppermute x0 -> x16, starting transfers between devices: none -> 15.5 us  [hop(): return lax.ppermute(values, axis, [(i, i ^ 1 << bit) for i in range(size)])]
    pallas_call x0 -> x1, Pallas kernels: none -> 15 us  [body(): pl.pallas_call(functools.partial(kernel, sizes), out_shape=(jax.ShapeDtyp...]
    ppermute x0 -> x16, waiting for transfers between devices: none -> 14.7 us  [hop(): return lax.ppermute(values, axis, [(i, i ^ 1 << bit) for i in range(size)])]
  transfers between devices with their start and end apart: 6 -> 18, of which waited for: 4 -> 11; matrix products, arithmetic and copies ran while one was open for 21% -> 10% of each run, Pallas kernels for 0% -> 0%
where the time goes in v1:
time: 89.9 us; the launch traced here: 89.3 us
  waiting for transfers between devices  26.7 us (30%)
  starting transfers between devices  26.2 us (29%)
  Pallas kernels  15 us (17%)
  local copies, waits for them, and re-layouts  13.6 us (15%)
  other arithmetic  6.14 us (7%)
  between operations  1.51 us (2%)
    ppermute x16, starting transfers between devices, hop(): return lax.ppermute(values, axis, [(i, i ^ 1 << bit) for i in range(size)])  15.5 us
    pallas_call x1, Pallas kernels, body(): pl.pallas_call(functools.partial(kernel, sizes), out_shape=(jax.ShapeDtyp...  15 us
    ppermute x16, waiting for transfers between devices, hop(): return lax.ppermute(values, axis, [(i, i ^ 1 << bit) for i in range(size)])  14.7 us
    all_to_all x1, starting transfers between devices, body(): lax.all_to_all(requests, 'users', split_axis=0, concat_axis=0, tiled=True)  7.28 us
    all_to_all x1, waiting for transfers between devices, body(): lax.all_to_all(cold_factor[served_rows].reshape(peers, reqs * IB, rank_si...  6.51 us
    all_to_all x1, waiting for transfers between devices, body(): lax.all_to_all(requests, 'users', split_axis=0, concat_axis=0, tiled=True)  5.51 us
    unnamed x16, local copies, waits for them, and re-layouts  4.88 us
    all_to_all x1, starting transfers between devices, body(): lax.all_to_all(cold_factor[served_rows].reshape(peers, reqs * IB, rank_si...  3.37 us
  transfers between devices with their start and end apart: 18, of which 11 were waited for; matrix products, arithmetic and copies ran while one was open for 10% of the time, Pallas kernels for 0%

profile of v1, /device:TPU:0, one launch (start us, length us, event | category | flops | bytes accessed | tf_op | source)
XLA Modules:
  0.0 89.3 jit_solution(12643083759978133792)
XLA Ops:
  0.7 1.4 %copy.18 = s32[8,1,2]{2,1,0:T(1,128)} copy(s32[8,1,2]{0,2,1:T(2,128)} %bitcast.19) | data formatting | bytes 128 | tf_op jit(solution)/shard_map/all_to_all | solution.py:174
  2.1 7.3 %all-to-all-start = ((s32[8,1,2]{2,1,0:T(1,128)}), s32[8,1,2]{2,1,0:T(1,128)S(1)}, u32[]{:S(2)}, u32[]{:S(2)}) async-start(s32[8,1,2]{2,1,0:T(1,128)} %copy.18), calls=%async_computation | async-start | bytes 8192 | tf_op jit(solution)/shard_map/all_to_all | solution.py:174
  10.2 5.5 %all-to-all-done = s32[8,1,2]{2,1,0:T(1,128)S(1)} async-done(((s32[8,1,2]{2,1,0:T(1,128)}), s32[8,1,2]{2,1,0:T(1,128)S(1)}, u32[]{:S(2)}, u32[]{:S(2)}) %all-to-all-start) | async-done | bytes 96 | tf_op jit(solution)/shard_map/all_to_all | solution.py:174
  16.1 1.8 %gather_fusion = bf16[256,256]{1,0:T(8,128)(2,1)} fusion(bf16[256,256]{1,0:T(8,128)(2,1)S(1)} %copy-done, s32[1024]{0:T(1024)S(1)} %pad_clamp_fusion.1), kind=kCustom, calls=%fused_computation | custom fusion | bytes 263168 | tf_op jit(solution)/shard_map/gather | solution.py:177
  17.9 3.4 %all-to-all-start.1 = ((bf16[8,32,256]{2,1,0:T(8,128)(2,1)}), bf16[8,32,256]{2,1,0:T(8,128)(2,1)S(1)}, u32[]{:S(2)}, u32[]{:S(2)}) async-start(bf16[8,32,256]{2,1,0:T(8,128)(2,1)} %bitcast.5), calls=%async_computation.1 | async-start | bytes 262144 | tf_op jit(solution)/shard_map/all_to_all | solution.py:176
  22.0 6.5 %all-to-all-done.1 = bf16[8,32,256]{2,1,0:T(8,128)(2,1)S(1)} async-done(((bf16[8,32,256]{2,1,0:T(8,128)(2,1)}), bf16[8,32,256]{2,1,0:T(8,128)(2,1)S(1)}, u32[]{:S(2)}, u32[]{:S(2)}) %all-to-all-start.1) | async-done | bytes 131104 | tf_op jit(solution)/shard_map/all_to_all | solution.py:176
  28.6 1.2 %copy-done.1 = bf16[2048,256]{1,0:T(8,128)(2,1)S(1)} copy-done((bf16[2048,256]{1,0:T(8,128)(2,1)S(1)}, bf16[2048,256]{1,0:T(8,128)(2,1)}, u32[]{:S(2)}) %copy-start.1) | copy-done | bytes 1048600
  29.8 0.9 %copy-done.3 = bf16[1,512,128]{2,1,0:T(8,128)(2,1)S(1)} copy-done((bf16[1,512,128]{2,1,0:T(8,128)(2,1)S(1)}, bf16[1,512,128]{2,1,0:T(8,128)(2,1)}, u32[]{:S(2)}) %copy-start.3) | copy-done | bytes 131096
  32.7 15.0 %blocks.1 = (f32[2048,256]{1,0:T(8,128)S(1)}, f32[768,256]{1,0:T(8,128)S(1)}, f32[256,256]{1,0:T(8,128)S(1)}) custom-call(s32[2]{0:T(128)S(1)} %pad_add_fusion.ids, s32[1]{0:T(128)S(6)} %copy.22.count, s32[1,512]{1,0:T(1,128)S(1)} %copy-done.5, s32[1,512]{1,0:T(1,128)S(1)} %copy-done.6, s32[1,512]{1,0:T(1,128)S(1)} %copy-done.7, ...), custom_call_target="tpu_custom_call" | custom-call | tf_op jit(solution)/shard_map/blocks/pallas_call | solution.py:193
  53.0 1.4 %collective-permute-done.2 = bf16[4,32,256]{2,1,0:T(8,128)(2,1)} collective-permute-done((bf16[4,32,256]{2,1,0:T(8,128)(2,1)}, bf16[4,32,256]{2,1,0:T(8,128)(2,1)}, u32[]{:S(2)}, u32[]{:S(2)}) %collective-permute-start.2) | collective-permute-done | bytes 65568 | tf_op jit(solution)/shard_map/ppermute | solution.py:145
  55.3 0.9 %convert_add_fusion.1 = f32[256,256]{1,0:T(8,128)S(1)} fusion(bf16[256,256]{1,0:T(8,128)(2,1)} %collective-permute-done.5, f32[768,256]{1,0:T(8,128)S(1)} %get-tuple-element.8), kind=kLoop, calls=%fused_computation.6 | loop fusion | flops 131072 | bytes 655360 | tf_op jit(solution)/shard_map/add | solution.py:236
  56.2 1.6 %collective-permute-start.6 = (bf16[128,256]{1,0:T(8,128)(2,1)S(1)}, bf16[128,256]{1,0:T(8,128)(2,1)S(1)}, u32[]{:S(2)}, u32[]{:S(2)}) collective-permute-start(bf16[128,256]{1,0:T(8,128)(2,1)S(1)} %slice.170), channel_id=1, source_target_pairs={{0,2},{1,3},{2,0},{3,1},{4,6},{5,7},{6,4},{7,5},{8,10},{9,11},{10,... | collective-permute-start | bytes 196616 | tf_op jit(solution)/shard_map/ppermute | solution.py:145
  57.8 0.9 %slice_add_fusion.2 = f32[84,256]{1,0:T(8,128)S(1)} fusion(f32[84,256]{1,0:T(8,128)S(1)} %collective-permute-done.10, f32[256,256]{1,0:T(8,128)} %copy-done.4), kind=kLoop, calls=%fused_computation.16 | loop fusion | flops 21504 | bytes 258048 | tf_op jit(solution)/shard_map/add | solution.py:238
  59.3 1.3 %collective-permute-done.6 = bf16[128,256]{1,0:T(8,128)(2,1)S(1)} collective-permute-done((bf16[128,256]{1,0:T(8,128)(2,1)S(1)}, bf16[128,256]{1,0:T(8,128)(2,1)S(1)}, u32[]{:S(2)}, u32[]{:S(2)}) %collective-permute-start.6) | collective-permute-done | bytes 65568 | tf_op jit(solution)/shard_map/ppermute | solution.py:145
  60.6 1.4 %collective-permute-start.7 = (f32[64,256]{1,0:T(8,128)S(1)}, f32[64,256]{1,0:T(8,128)S(1)}, u32[]{:S(2)}, u32[]{:S(2)}) collective-permute-start(f32[64,256]{1,0:T(8,128)S(1)} %slice.136), channel_id=1, source_target_pairs={{0,4},{4,0},{8,12},{12,8},{16,20},{20,16},{24,28},{28,24},{1,5},{5... | collective-permute-start | bytes 196616 | tf_op jit(solution)/shard_map/ppermute | solution.py:145
  62.0 0.9 %collective-permute-start.4 = (bf16[1,128,256]{2,1,0:T(8,128)(2,1)S(1)}, bf16[1,128,256]{2,1,0:T(8,128)(2,1)S(1)}, u32[]{:S(2)}, u32[]{:S(2)}) collective-permute-start(bf16[1,128,256]{2,1,0:T(8,128)(2,1)S(1)} %get-tuple-element.15), channel_id=1, source_target_pairs={{0,16},{4,20},{8,24},{12,28},{16,0},{20,4},{24,8},{28,12},{1,17},{... | collective-permute-start | bytes 196616 | tf_op jit(solution)/shard_map/ppermute | solution.py:145
  63.3 1.3 %collective-permute-start.12 = (f32[84,256]{1,0:T(8,128)S(1)}, f32[84,256]{1,0:T(8,128)S(1)}, u32[]{:S(2)}, u32[]{:S(2)}) collective-permute-start(f32[84,256]{1,0:T(8,128)S(1)} %add.98), channel_id=1, source_target_pairs={{0,4},{4,0},{8,12},{12,8},{16,20},{20,16},{24,28},{28,24},{1,5},{5... | collective-permute-start | bytes 258056 | tf_op jit(solution)/shard_map/ppermute | solution.py:145
  66.0 2.3 %collective-permute-start.8 = (f32[32,256]{1,0:T(8,128)}, f32[32,256]{1,0:T(8,128)S(1)}, u32[]{:S(2)}, u32[]{:S(2)}) collective-permute-start(f32[32,256]{1,0:T(8,128)} %slice.138), channel_id=1, source_target_pairs={{0,8},{4,12},{8,0},{12,4},{16,24},{20,28},{24,16},{28,20},{1,9},{5... | collective-permute-start | bytes 98312 | tf_op jit(solution)/shard_map/ppermute | solution.py:145
  68.4 1.5 %collective-permute-start.13 = (f32[84,256]{1,0:T(8,128)S(1)}, f32[84,256]{1,0:T(8,128)S(1)}, u32[]{:S(2)}, u32[]{:S(2)}) collective-permute-start(f32[84,256]{1,0:T(8,128)S(1)} %add.99), channel_id=1, source_target_pairs={{0,8},{4,12},{8,0},{12,4},{16,24},{20,28},{24,16},{28,20},{1,9},{5... | collective-permute-start | bytes 258056 | tf_op jit(solution)/shard_map/ppermute | solution.py:145
  70.4 1.0 %collective-permute-start.9 = (f32[16,256]{1,0:T(8,128)S(1)}, f32[16,256]{1,0:T(8,128)S(1)}, u32[]{:S(2)}, u32[]{:S(2)}) collective-permute-start(f32[16,256]{1,0:T(8,128)S(1)} %slice.140), channel_id=1, source_target_pairs={{0,16},{4,20},{8,24},{12,28},{16,0},{20,4},{24,8},{28,12},{1,17},{... | collective-permute-start | bytes 49160 | tf_op jit(solution)/shard_map/ppermute | solution.py:145
  73.0 1.4 %collective-permute-start.14 = (f32[84,256]{1,0:T(8,128)S(1)}, f32[84,256]{1,0:T(8,128)S(1)}, u32[]{:S(2)}, u32[]{:S(2)}) collective-permute-start(f32[84,256]{1,0:T(8,128)S(1)} %add.100), channel_id=1, source_target_pairs={{0,16},{4,20},{8,24},{12,28},{16,0},{20,4},{24,8},{28,12},{1,17},{... | collective-permute-start | bytes 258056 | tf_op jit(solution)/shard_map/ppermute | solution.py:145
  75.8 2.7 %collective-permute-done.14 = f32[84,256]{1,0:T(8,128)S(1)} collective-permute-done((f32[84,256]{1,0:T(8,128)S(1)}, f32[84,256]{1,0:T(8,128)S(1)}, u32[]{:S(2)}, u32[]{:S(2)}) %collective-permute-start.14) | collective-permute-done | bytes 86048 | tf_op jit(solution)/shard_map/ppermute | solution.py:145
  78.8 2.7 %collective-permute-start.1 = (bf16[512,256]{1,0:T(8,128)(2,1)S(1)}, bf16[512,256]{1,0:T(8,128)(2,1)S(1)}, u32[]{:S(2)}, u32[]{:S(2)}) collective-permute-start(bf16[512,256]{1,0:T(8,128)(2,1)S(1)} %slice.169), channel_id=1, source_target_pairs={{0,2},{1,3},{2,0},{3,1},{4,6},{5,7},{6,4},{7,5},{8,10},{9,11},{10,... | collective-permute-start | bytes 786440 | tf_op jit(solution)/shard_map/ppermute | solution.py:145
  82.2 6.2 %collective-permute-done.1 = bf16[512,256]{1,0:T(8,128)(2,1)S(1)} collective-permute-done((bf16[512,256]{1,0:T(8,128)(2,1)S(1)}, bf16[512,256]{1,0:T(8,128)(2,1)S(1)}, u32[]{:S(2)}, u32[]{:S(2)}) %collective-permute-start.1) | collective-permute-done | bytes 262176 | tf_op jit(solution)/shard_map/ppermute | solution.py:145
  (77 shorter events, 17.3 us)
Async XLA Ops:
  0.6 15.5 %copy-start = (bf16[256,256]{1,0:T(8,128)(2,1)S(1)}, bf16[256,256]{1,0:T(8,128)(2,1)}, u32[]{:S(2)}) copy-start(bf16[256,256]{1,0:T(8,128)(2,1)} %param.12) | copy-start | bytes 393220
  0.6 27.9 %copy-start.2 = (bf16[512,256]{1,0:T(8,128)(2,1)S(1)}, bf16[512,256]{1,0:T(8,128)(2,1)}, u32[]{:S(2)}) copy-start(bf16[512,256]{1,0:T(8,128)(2,1)} %hot.1) | copy-start | bytes 786436
  2.1 13.7 %all-to-all-start = ((s32[8,1,2]{2,1,0:T(1,128)}), s32[8,1,2]{2,1,0:T(1,128)S(1)}, u32[]{:S(2)}, u32[]{:S(2)}) async-start(s32[8,1,2]{2,1,0:T(1,128)} %copy.18), calls=%async_computation | async-start | bytes 8192 | tf_op jit(solution)/shard_map/all_to_all | solution.py:174
  17.9 10.7 %all-to-all-start.1 = ((bf16[8,32,256]{2,1,0:T(8,128)(2,1)}), bf16[8,32,256]{2,1,0:T(8,128)(2,1)S(1)}, u32[]{:S(2)}, u32[]{:S(2)}) async-start(bf16[8,32,256]{2,1,0:T(8,128)(2,1)} %bitcast.5), calls=%async_computation.1 | async-start | bytes 262144 | tf_op jit(solution)/shard_map/all_to_all | solution.py:176
  28.6 1.2 %copy-start.1 = (bf16[2048,256]{1,0:T(8,128)(2,1)S(1)}, bf16[2048,256]{1,0:T(8,128)(2,1)}, u32[]{:S(2)}) copy-start(bf16[2048,256]{1,0:T(8,128)(2,1)} %user_tab.1) | copy-start | bytes 3145732
  29.8 0.9 %copy-start.3 = (bf16[1,512,128]{2,1,0:T(8,128)(2,1)S(1)}, bf16[1,512,128]{2,1,0:T(8,128)(2,1)}, u32[]{:S(2)}) copy-start(bf16[1,512,128]{2,1,0:T(8,128)(2,1)} %param.19) | copy-start | bytes 393220
  30.7 0.7 copy-start.5
  47.7 0.7 copy-start.4
  49.8 4.6 %collective-permute-start.2 = (bf16[4,32,256]{2,1,0:T(8,128)(2,1)}, bf16[4,32,256]{2,1,0:T(8,128)(2,1)}, u32[]{:S(2)}, u32[]{:S(2)}) collective-permute-start(bf16[4,32,256]{2,1,0:T(8,128)(2,1)} %bitcast.10), channel_id=1, source_target_pairs={{0,4},{4,0},{8,12},{12,8},{16,20},{20,16},{24,28},{28,24},{1,5},{5... | collective-permute-start | bytes 196616 | tf_op jit(solution)/shard_map/ppermute | solution.py:145
  50.0 5.3 %collective-permute-start.5 = (bf16[256,256]{1,0:T(8,128)(2,1)}, bf16[256,256]{1,0:T(8,128)(2,1)}, u32[]{:S(2)}, u32[]{:S(2)}) collective-permute-start(bf16[256,256]{1,0:T(8,128)(2,1)} %slice.132), channel_id=1, source_target_pairs={{0,1},{1,0},{2,3},{3,2},{4,5},{5,4},{6,7},{7,6},{8,9},{9,8},{10,11... | collective-permute-start | bytes 393224 | tf_op jit(solution)/shard_map/ppermute | solution.py:145
  51.6 6.2 %collective-permute-start.10 = (f32[84,256]{1,0:T(8,128)S(1)}, f32[84,256]{1,0:T(8,128)S(1)}, u32[]{:S(2)}, u32[]{:S(2)}) collective-permute-start(f32[84,256]{1,0:T(8,128)S(1)} %slice.118), channel_id=1, source_target_pairs={{0,1},{1,0},{2,3},{3,2},{4,5},{5,4},{6,7},{7,6},{8,9},{9,8},{10,11... | collective-permute-start | bytes 258056 | tf_op jit(solution)/shard_map/ppermute | solution.py:145
  53.0 25.7 %collective-permute-start = (bf16[1024,256]{1,0:T(8,128)(2,1)}, bf16[1024,256]{1,0:T(8,128)(2,1)S(1)}, u32[]{:S(2)}, u32[]{:S(2)}) collective-permute-start(bf16[1024,256]{1,0:T(8,128)(2,1)} %slice.168), channel_id=1, source_target_pairs={{0,1},{1,0},{2,3},{3,2},{4,5},{5,4},{6,7},{7,6},{8,9},{9,8},{10,11... | collective-permute-start | bytes 1572872 | tf_op jit(solution)/shard_map/ppermute | solution.py:145
  55.2 6.8 %collective-permute-start.3 = (bf16[2,64,256]{2,1,0:T(8,128)(2,1)S(1)}, bf16[2,64,256]{2,1,0:T(8,128)(2,1)S(1)}, u32[]{:S(2)}, u32[]{:S(2)}) collective-permute-start(bf16[2,64,256]{2,1,0:T(8,128)(2,1)S(1)} %get-tuple-element.17), channel_id=1, source_target_pairs={{0,8},{4,12},{8,0},{12,4},{16,24},{20,28},{24,16},{28,20},{1,9},{5... | collective-permute-start | bytes 196616 | tf_op jit(solution)/shard_map/ppermute | solution.py:145
  56.2 4.3 %collective-permute-start.6 = (bf16[128,256]{1,0:T(8,128)(2,1)S(1)}, bf16[128,256]{1,0:T(8,128)(2,1)S(1)}, u32[]{:S(2)}, u32[]{:S(2)}) collective-permute-start(bf16[128,256]{1,0:T(8,128)(2,1)S(1)} %slice.170), channel_id=1, source_target_pairs={{0,2},{1,3},{2,0},{3,1},{4,6},{5,7},{6,4},{7,5},{8,10},{9,11},{10,... | collective-permute-start | bytes 196616 | tf_op jit(solution)/shard_map/ppermute | solution.py:145
  58.7 4.6 %collective-permute-start.11 = (f32[84,256]{1,0:T(8,128)S(1)}, f32[84,256]{1,0:T(8,128)S(1)}, u32[]{:S(2)}, u32[]{:S(2)}) collective-permute-start(f32[84,256]{1,0:T(8,128)S(1)} %slice_add_fusion.2), channel_id=1, source_target_pairs={{0,2},{1,3},{2,0},{3,1},{4,6},{5,7},{6,4},{7,5},{8,10},{9,11},{10,... | collective-permute-start | bytes 258056 | tf_op jit(solution)/shard_map/ppermute | solution.py:145
  60.6 4.8 %collective-permute-start.7 = (f32[64,256]{1,0:T(8,128)S(1)}, f32[64,256]{1,0:T(8,128)S(1)}, u32[]{:S(2)}, u32[]{:S(2)}) collective-permute-start(f32[64,256]{1,0:T(8,128)S(1)} %slice.136), channel_id=1, source_target_pairs={{0,4},{4,0},{8,12},{12,8},{16,20},{20,16},{24,28},{28,24},{1,5},{5... | collective-permute-start | bytes 196616 | tf_op jit(solution)/shard_map/ppermute | solution.py:145
  62.0 6.4 %collective-permute-start.4 = (bf16[1,128,256]{2,1,0:T(8,128)(2,1)S(1)}, bf16[1,128,256]{2,1,0:T(8,128)(2,1)S(1)}, u32[]{:S(2)}, u32[]{:S(2)}) collective-permute-start(bf16[1,128,256]{2,1,0:T(8,128)(2,1)S(1)} %get-tuple-element.15), channel_id=1, source_target_pairs={{0,16},{4,20},{8,24},{12,28},{16,0},{20,4},{24,8},{28,12},{1,17},{... | collective-permute-start | bytes 196616 | tf_op jit(solution)/shard_map/ppermute | solution.py:145
  63.3 5.1 %collective-permute-start.12 = (f32[84,256]{1,0:T(8,128)S(1)}, f32[84,256]{1,0:T(8,128)S(1)}, u32[]{:S(2)}, u32[]{:S(2)}) collective-permute-start(f32[84,256]{1,0:T(8,128)S(1)} %add.98), channel_id=1, source_target_pairs={{0,4},{4,0},{8,12},{12,8},{16,20},{20,16},{24,28},{28,24},{1,5},{5... | collective-permute-start | bytes 258056 | tf_op jit(solution)/shard_map/ppermute | solution.py:145
  66.0 4.4 %collective-permute-start.8 = (f32[32,256]{1,0:T(8,128)}, f32[32,256]{1,0:T(8,128)S(1)}, u32[]{:S(2)}, u32[]{:S(2)}) collective-permute-start(f32[32,256]{1,0:T(8,128)} %slice.138), channel_id=1, source_target_pairs={{0,8},{4,12},{8,0},{12,4},{16,24},{20,28},{24,16},{28,20},{1,9},{5... | collective-permute-start | bytes 98312 | tf_op jit(solution)/shard_map/ppermute | solution.py:145
  68.4 4.6 %collective-permute-start.13 = (f32[84,256]{1,0:T(8,128)S(1)}, f32[84,256]{1,0:T(8,128)S(1)}, u32[]{:S(2)}, u32[]{:S(2)}) collective-permute-start(f32[84,256]{1,0:T(8,128)S(1)} %add.99), channel_id=1, source_target_pairs={{0,8},{4,12},{8,0},{12,4},{16,24},{20,28},{24,16},{28,20},{1,9},{5... | collective-permute-start | bytes 258056 | tf_op jit(solution)/shard_map/ppermute | solution.py:145
  70.4 4.8 %collective-permute-start.9 = (f32[16,256]{1,0:T(8,128)S(1)}, f32[16,256]{1,0:T(8,128)S(1)}, u32[]{:S(2)}, u32[]{:S(2)}) collective-permute-start(f32[16,256]{1,0:T(8,128)S(1)} %slice.140), channel_id=1, source_target_pairs={{0,16},{4,20},{8,24},{12,28},{16,0},{20,4},{24,8},{28,12},{1,17},{... | collective-permute-start | bytes 49160 | tf_op jit(solution)/shard_map/ppermute | solution.py:145
  73.0 5.5 %collective-permute-start.14 = (f32[84,256]{1,0:T(8,128)S(1)}, f32[84,256]{1,0:T(8,128)S(1)}, u32[]{:S(2)}, u32[]{:S(2)}) collective-permute-start(f32[84,256]{1,0:T(8,128)S(1)} %add.100), channel_id=1, source_target_pairs={{0,16},{4,20},{8,24},{12,28},{16,0},{20,4},{24,8},{28,12},{1,17},{... | collective-permute-start | bytes 258056 | tf_op jit(solution)/shard_map/ppermute | solution.py:145
  78.6 2.9 %collective-permute-start.15 = (f32[84,256]{1,0:T(8,128)S(1)}, f32[84,256]{1,0:T(8,128)S(1)}, u32[]{:S(2)}, u32[]{:S(2)}) collective-permute-start(f32[84,256]{1,0:T(8,128)S(1)} %add.101), channel_id=1, source_target_pairs={{0,1},{1,0},{2,3},{3,2},{4,5},{5,4},{6,7},{7,6},{8,9},{9,8},{10,11... | collective-permute-start | bytes 258056 | tf_op jit(solution)/shard_map/ppermute | solution.py:145
  78.8 9.6 %collective-permute-start.1 = (bf16[512,256]{1,0:T(8,128)(2,1)S(1)}, bf16[512,256]{1,0:T(8,128)(2,1)S(1)}, u32[]{:S(2)}, u32[]{:S(2)}) collective-permute-start(bf16[512,256]{1,0:T(8,128)(2,1)S(1)} %slice.169), channel_id=1, source_target_pairs={{0,2},{1,3},{2,0},{3,1},{4,6},{5,7},{6,4},{7,5},{8,10},{9,11},{10,... | collective-permute-start | bytes 786440 | tf_op jit(solution)/shard_map/ppermute | solution.py:145
  (2 other events, 1.4 us)

commit v2 on v0

v2 whole, which is shorter than its diff:
```python
import collections
import functools

import jax
import jax.numpy as jnp
from jax import lax
from jax.experimental import pallas as pl
from jax.experimental.pallas import tpu as pltpu
from jax.sharding import PartitionSpec as P

IB = 16
HB = 8
HALF = 128
F32 = jnp.float32
BF16 = jnp.bfloat16

Sizes = collections.namedtuple(
    "Sizes",
    ("peers", "items", "hot_slots", "reqs", "hours", "permute_hot", "split_hot", "hot_blocks", "cold_blocks"),
)


def bits_of(size):
    return size.bit_length() - 1


def padded(rows):
    return -(-rows // 16) * 16


def flip(value, bits):
    out = jnp.zeros_like(value)
    for k in range(bits):
        out = out | (((value >> k) & 1) << (bits - 1 - k))
    return out


def hour_of(lane, split, hours):
    half = hours // 2
    inside = lane & (HALF - 1)
    hour = ((lane >> 7) ^ split) * half + inside
    return hour, inside < half


def one_hot(mask):
    return mask.astype(F32).astype(BF16)


def column(row):
    parts = [jnp.transpose(jnp.broadcast_to(row[:, k : k + 128], (128, 128))) for k in range(0, row.shape[1], 128)]
    return jnp.concatenate(parts, axis=0)


def spread(col, lanes):
    return jnp.concatenate([col] * (-(-lanes // 128)), axis=1)[:, :lanes]


def load_table(table, rows, at=0):
    for part in range(table.shape[0]):
        table[part, at : at + rows.shape[0], :] = rows[:, part * 128 : part * 128 + 128].astype(F32)


def chosen_blocks(sizes, hot, count, slot_row):
    place = lax.broadcasted_iota(jnp.int32, slot_row.shape, 1)
    of_kind = (slot_row < sizes.hot_slots) if hot else (slot_row >= sizes.hot_slots)
    chosen = (place < count) & of_kind
    return chosen, jnp.sum(chosen.astype(F32))


def prepare(sizes, hot, m, p, q, chosen, user, slot, hour, user_tab, observed, out):
    obs, live_hour, user_rows, pick, put, user_pos = out
    blocks = slot.shape[1]
    users = user_tab.shape[0]
    user_chunk = users // sizes.items

    kind = jnp.broadcast_to(chosen.astype(F32), (8, blocks)).astype(BF16)
    before = one_hot(
        lax.broadcasted_iota(jnp.int32, (blocks, blocks), 0) < lax.broadcasted_iota(jnp.int32, (blocks, blocks), 1)
    )
    rank = jnp.dot(kind, before, preferred_element_type=F32)[:1]
    rank = jnp.where(chosen, rank, -1.0).astype(jnp.int32)
    order = one_hot(rank == lax.broadcasted_iota(jnp.int32, (m, blocks), 0))
    user_in = user[...]
    rows = [user_in >> 4, user_in & 15, slot[...], hour[...] + 1]
    rows = jnp.concatenate([row.astype(F32) for row in rows] + [jnp.zeros((4, blocks), F32)], axis=0).astype(BF16)
    rows = lax.dot_general(rows, order, (((1,), (1,)), ((), ())), preferred_element_type=F32).astype(jnp.int32)
    user_row, slot_row, hour_row = rows[0:1] * 16 + rows[1:2], rows[2:3], rows[3:4] - 1
    obs[:m, :] = jnp.dot(order, 0.5 - observed[...], preferred_element_type=F32)

    user_col, hour_col = column(user_row), column(hour_row)
    step = 512
    total = jnp.zeros((m, user_tab.shape[1]), F32)
    for k in range(0, users, step):
        lane = lax.broadcasted_iota(jnp.int32, (m, step), 1) + k
        total += jnp.dot(one_hot(spread(user_col, step) == lane), user_tab[k : k + step, :], preferred_element_type=F32)
    user_rows[:m, :] = total

    slots = pick.shape[1]
    if hot:
        put_pos = flip(slot_row ^ (p * sizes.items + q), bits_of(sizes.peers * sizes.items)) if sizes.permute_hot else slot_row
    else:
        owner, request = (slot_row - sizes.hot_slots) // sizes.reqs, (slot_row - sizes.hot_slots) % sizes.reqs
        put_pos = (owner ^ p) * sizes.reqs + request
        slot_row = (owner ^ (p & ~1)) * sizes.reqs + request
    pick[:m, :] = one_hot(spread(column(slot_row), slots) == lax.broadcasted_iota(jnp.int32, (m, slots), 1))
    put[:, :m] = one_hot(put_pos == lax.broadcasted_iota(jnp.int32, (slots, m), 0))
    user_pos[:, :m] = flip((user_row // user_chunk) ^ q, bits_of(sizes.items)) * user_chunk + user_row % user_chunk

    lane = lax.broadcasted_iota(jnp.int32, (m, 2 * HALF), 1)
    lane_hour, used = hour_of(lane, q & 1, sizes.hours)
    live_hour[:m, :] = (used & ((lane_hour // HB) == spread(hour_col, 2 * HALF))).astype(F32)


def work(sizes, m, first, last, q, state, table, hours_tab, user_terms, item_sums, grad_hour, stack=4):
    obs, live_hour, user_rows, pick, put, _ = state
    slots = pick.shape[1]
    parts = range(table.shape[0])
    lane_hour, used = hour_of(lax.broadcasted_iota(jnp.int32, (IB * HB, 2 * HALF), 1), q & 1, sizes.hours)
    cell = lax.broadcasted_iota(jnp.int32, (IB * HB, 2 * HALF), 0)
    tile = one_hot(used & ((cell & (HB - 1)) == (lane_hour & (HB - 1))))
    cell_item = lax.broadcasted_iota(jnp.int32, (m, IB * HB), 1) // HB

    def one(group, carry):
        places = [group * stack + j for j in range(stack)]
        rows, cells = [], []
        for a in places:
            of_place = pl.ds(a, slots, stride=IB)
            choice = jnp.concatenate([table[part, of_place, :] for part in parts], axis=1).astype(BF16)
            rows.append(jnp.dot(pick[:m, :], choice, preferred_element_type=F32))
            cells.append(jnp.where(cell_item == a, obs[:m, :], 0.0).astype(BF16))
        users_f = user_rows[:m, :]
        user_item = jnp.concatenate([(users_f * row).astype(BF16) for row in rows], axis=0)
        half_model = lax.dot_general(
            user_item, hours_tab[...] * jnp.asarray(0.5, BF16), (((1,), (1,)), ((), ())), preferred_element_type=F32
        )
        seen = jnp.dot(jnp.concatenate(cells, axis=0), tile, preferred_element_type=F32)
        live = jnp.concatenate([live_hour[:m, :]] * stack, axis=0)
        residual = ((0.5 * jnp.tanh(half_model) + seen) * live).astype(BF16)
        weighted = jnp.dot(residual, hours_tab[...], preferred_element_type=F32)
        grad_hour[...] += lax.dot_general(
            residual, user_item, (((0,), (0,)), ((), ())), preferred_element_type=F32
        )
        into = put[:, :m]
        total = user_terms[:m, :]
        for j, a in enumerate(places):
            mine = weighted[j * m : j * m + m]
            total += mine * rows[j]
            terms = mine * users_f
            high = terms.astype(BF16)
            low = (terms - high.astype(F32)).astype(BF16)
            sums = jnp.dot(into, high, preferred_element_type=F32) + jnp.dot(into, low, preferred_element_type=F32)
            for part in parts:
                item_sums[part, pl.ds(a, slots, stride=IB), :] = sums[:, part * 128 : part * 128 + 128]
        user_terms[:m, :] = total
        return carry

    lax.fori_loop(first // stack, last // stack, one, 0)


def in_size(number, small, whole, run):
    pl.when(number <= small)(lambda: run(small))
    pl.when(number > small)(lambda: run(whole))


def serve(sizes, *refs):
    turns = sizes.peers // 2
    needs, (mine, theirs), outs, table = refs[: -turns - 3], refs[-turns - 3 : -turns - 1], refs[-turns - 1 : -1], refs[-1]
    p = lax.axis_index("users")
    rows = mine.shape[0]
    table[pl.ds(pl.multiple_of((p & 1) * rows, rows), rows), :] = mine[...]
    table[pl.ds(pl.multiple_of((1 - (p & 1)) * rows, rows), rows), :] = theirs[...]
    for m, out in enumerate(outs):
        for which in range(2):
            for r in range(sizes.reqs):
                owner = (p & ~1) + which
                block = needs[m][0, r, owner] if len(needs) == turns else needs[0][m, r * sizes.peers + owner]
                at = pl.multiple_of(which * rows + block * IB, IB)
                to = (which * sizes.reqs + r) * IB
                out[to : to + IB, :] = table[pl.ds(at, IB), :]


def start_copies(pairs, sems):
    copies = [pltpu.make_async_copy(source, target, sems.at[k]) for k, (source, target) in enumerate(pairs)]
    for copy in copies:
        copy.start()
    return copies


def first_kernel(
    sizes, count, user_in, slot_in, hour_in, user_tab_in, hot_in, hour_factor_in, observed_in,
    obs, live_hour, user_rows, pick, put, user_pos, user_terms, item_sums, grad_hour,
    table, hours_tab, user, slot, hour,
    user_tab, hot, hour_factor, observed, sems,
):
    state = (obs, live_hour, user_rows, pick, put, user_pos)
    p, q = lax.axis_index("users"), lax.axis_index("items")
    sources = (slot_in, user_in, hour_in, observed_in.at[0], user_tab_in, hour_factor_in, hot_in)
    copies = start_copies(zip(sources, (slot, user, hour, observed, user_tab, hour_factor, hot)), sems)
    user_terms[...] = jnp.zeros_like(user_terms)
    grad_hour[...] = jnp.zeros_like(grad_hour)
    for copy in copies[:3]:
        copy.wait()
    chosen, number = chosen_blocks(sizes, True, count[0], slot[...])
    for copy in copies[3:]:
        copy.wait()
    load_table(table, hot)
    row_hour, used = hour_of(lax.broadcasted_iota(jnp.int32, (2 * HALF, sizes.hours), 0), q & 1, sizes.hours)
    hit = one_hot(used & (row_hour == lax.broadcasted_iota(jnp.int32, (2 * HALF, sizes.hours), 1)))
    hours_tab[...] = jnp.dot(hit, hour_factor[...], preferred_element_type=F32).astype(BF16)

    def run(m):
        prepare(sizes, True, m, p, q, chosen, user, slot, hour, user_tab, observed, state)
        work(sizes, m, 0, IB // 2, q, state, table, hours_tab, user_terms, item_sums, grad_hour)

    in_size(number, sizes.hot_blocks, slot.shape[1], run)


def second_kernel(
    sizes, count, user_tab_in, observed_in,
    obs, live_hour, user_rows, pick, put, user_pos, user_terms_in, item_sums_in, grad_hour_in,
    table, hours_tab, user, slot, hour,
    obs_2, live_hour_2, user_rows_2, pick_2, put_2, user_pos_2, user_terms, item_sums, grad_hour,
    user_tab, observed, sems,
):
    state = (obs, live_hour, user_rows, pick, put, user_pos)
    state_2 = (obs_2, live_hour_2, user_rows_2, pick_2, put_2, user_pos_2)
    p, q = lax.axis_index("users"), lax.axis_index("items")
    copies = start_copies(zip((observed_in.at[0], user_tab_in), (observed, user_tab)), sems)
    user_terms[...] = user_terms_in[...]
    item_sums[...] = item_sums_in[...]
    grad_hour[...] = grad_hour_in[...]
    _, number = chosen_blocks(sizes, True, count[0], slot[...])

    def run(m):
        work(sizes, m, IB // 2, IB, q, state, table, hours_tab, user_terms, item_sums, grad_hour)

    in_size(number, sizes.hot_blocks, slot.shape[1], run)
    chosen, number = chosen_blocks(sizes, False, count[0], slot[...])
    for copy in copies:
        copy.wait()

    def make(m):
        prepare(sizes, False, m, p, q, chosen, user, slot, hour, user_tab, observed, state_2)

    in_size(number, sizes.cold_blocks, slot.shape[1], make)


def third_kernel(
    sizes, count, slot, hours_tab,
    obs, live_hour, user_rows, pick, put, user_pos, hot_sums, grad_hour_in,
    *refs,
):
    fetched, (send, keep, cold_send, user_terms, table, item_sums, grad_hour) = refs[:-7], refs[-7:]
    state = (obs, live_hour, user_rows, pick, put, user_pos)
    q = lax.axis_index("items")
    rows = fetched[0].shape[0]
    for m, block in enumerate(fetched):
        load_table(table, block, m * rows)
    user_terms[...] = jnp.zeros_like(user_terms)
    grad_hour[...] = grad_hour_in[...]
    _, number = chosen_blocks(sizes, False, count[0], slot[...])

    def run(m):
        work(sizes, m, 0, IB, q, state, table, hours_tab, user_terms, item_sums, grad_hour)

    in_size(number, sizes.cold_blocks, slot.shape[1], run)

    high_rows = padded(sizes.hours // 2)
    at = sizes.split_hot
    for part in range(table.shape[0]):
        lanes = slice(part * 128, part * 128 + 128)
        if at:
            keep[:at, lanes] = hot_sums[part, :at, :]
            send[:at, lanes] = hot_sums[part, at : 2 * at, :].astype(BF16)
        cold_send[:, lanes] = item_sums[part].astype(BF16)
    keep[at : at + high_rows, :] = grad_hour[:high_rows, :]
    other = grad_hour[HALF : HALF + high_rows, :]
    high = other.astype(BF16)
    send[at : at + high_rows, :] = high
    send[at + high_rows : at + 2 * high_rows, :] = (other - high.astype(F32)).astype(BF16)


def users_kernel(sizes, count, slot, pos, terms, pos_2, terms_2, send, keep, step=256):
    _, number = chosen_blocks(sizes, True, count[0], slot[...])
    _, number_2 = chosen_blocks(sizes, False, count[0], slot[...])

    def add(m, m_2):
        total = jnp.concatenate([terms[:m, :], terms_2[:m_2, :]], axis=0)
        high = total.astype(BF16)
        low = (total - high.astype(F32)).astype(BF16)
        row = jnp.concatenate([pos[:, :m], pos_2[:, :m_2]], axis=1)
        within = one_hot((row & (step - 1)) == lax.broadcasted_iota(jnp.int32, (step, m + m_2), 0))
        for k in range(0, 2 * keep.shape[0], step):
            hit = within * one_hot((row // step) == k // step)
            sums = jnp.dot(hit, high, preferred_element_type=F32) + jnp.dot(hit, low, preferred_element_type=F32)
            if k < keep.shape[0]:
                keep[k : k + step, :] = sums
            else:
                send[k - keep.shape[0] : k - keep.shape[0] + step, :] = sums.astype(BF16)

    def hot(m):
        in_size(number_2, sizes.cold_blocks, slot.shape[1], lambda m_2: add(m, m_2))

    in_size(number, sizes.hot_blocks, slot.shape[1], hot)


def finish(sizes, needs, returned, mine, other, hot, got, cold_grad, hot_grad, hour_grad):
    p, q = lax.axis_index("users"), lax.axis_index("items")
    hot_grad[...] = hot[...] + got[...].astype(F32)
    half = mine.shape[0]
    swap = (q & 1) == 1
    hour_grad[:half, :] = jnp.where(swap, other[...], mine[...])
    hour_grad[half:, :] = jnp.where(swap, mine[...], other[...])
    asked, rows = needs.shape[0], returned.shape[0]
    lane = lax.broadcasted_iota(jnp.int32, needs.shape, 1)
    mask = jnp.where(lane == p, needs[...], 0).astype(F32)
    wanted = jnp.broadcast_to(jnp.sum(mask, axis=1, keepdims=True), (asked, 128)).astype(BF16)
    number = lax.broadcasted_iota(jnp.int32, (asked, rows), 1) // IB
    source = flip(number // sizes.reqs, bits_of(sizes.peers)) * sizes.reqs + number % sizes.reqs
    place = one_hot(source == lax.broadcasted_iota(jnp.int32, (asked, rows), 0))
    block = lax.dot_general(wanted, place, (((0,), (0,)), ((), ())), preferred_element_type=F32)[:1].astype(jnp.int32)
    size = (cold_grad.shape[0], rows)
    row, column = lax.broadcasted_iota(jnp.int32, size, 0), lax.broadcasted_iota(jnp.int32, size, 1)
    hit = one_hot((row // IB == block) & (row % IB == column % IB))
    cold_grad[...] = jnp.dot(hit, returned[...], preferred_element_type=F32)


def hop(values, axis, size, bit):
    return lax.ppermute(values, axis, [(i, i ^ (1 << bit)) for i in range(size)])


def turn(values, axis, size, change):
    return lax.ppermute(values, axis, [(i, i ^ change) for i in range(size)])


def halves(values):
    rows = values.shape[0] // 2
    return values[:rows], values[rows:]


def body(
    user_factor,
    hot_factor,
    cold_factor,
    hour_factor,
    block_user,
    block_slot,
    block_hour,
    block_count,
    need_rows,
    observed,
):
    rank_size = user_factor.shape[1]
    hours = hour_factor.shape[0]
    hot_rows = hot_factor.shape[0]
    shard_len = cold_factor.shape[0]
    peers, items = lax.axis_size("users"), lax.axis_size("items")
    reqs = need_rows.shape[2]
    half = hours // 2
    blocks = block_user.shape[1]
    users = user_factor.shape[0]
    hot_slots, cold_slots = hot_rows // IB, peers * reqs
    permute_hot = hot_rows == IB * peers * items
    high_rows = padded(half)
    split_hot = hot_rows // 2 if permute_hot else 0
    sizes = Sizes(
        peers, items, hot_slots, reqs, hours, permute_hot, split_hot, blocks // 4 * 3, blocks // 2
    )
    vmem = pl.BlockSpec(memory_space=pltpu.VMEM)
    smem = pl.BlockSpec(memory_space=pltpu.SMEM)
    hbm = pl.BlockSpec(memory_space=pltpu.HBM)

    def shape(*dims, dtype=F32):
        return jax.ShapeDtypeStruct(dims, dtype)

    def state_of(slots):
        return (
            shape(blocks, IB * HB),
            shape(blocks, 2 * HALF),
            shape(blocks, rank_size),
            shape(blocks, slots, dtype=BF16),
            shape(slots, blocks, dtype=BF16),
            shape(1, blocks, dtype=jnp.int32),
        )

    def table_of(slots):
        return (rank_size // 128, slots * IB, 128)

    def call(function, scalar, far, near, out_shape, scratch, flops):
        return pl.pallas_call(
            functools.partial(function, sizes),
            out_shape=out_shape,
            in_specs=[smem] * len(scalar) + [hbm] * len(far) + [vmem] * len(near),
            out_specs=(vmem,) * len(out_shape),
            scratch_shapes=scratch,
            compiler_params=pltpu.CompilerParams(vmem_limit_bytes=24 * 1024 * 1024),
            cost_estimate=pl.CostEstimate(flops=flops, bytes_accessed=4 << 20, transcendentals=0),
            name=function.__name__,
        )(*scalar, *[pltpu.with_memory_space_constraint(value, pltpu.HBM) for value in far], *near)

    turns = peers // 2
    theirs = hop(cold_factor, "users", peers, 0)
    need = jnp.transpose(need_rows, (0, 2, 1))
    needs = [need] + [turn(need, "users", peers, 2 * m) for m in range(1, turns)]

    def room(*dims, dtype=F32):
        return pltpu.VMEM(dims, dtype)

    row = shape(1, blocks, dtype=jnp.int32)
    sums = (shape(*table_of(hot_slots)), shape(2 * HALF, rank_size))
    users_room = room(*user_factor.shape, dtype=BF16)
    observed_room = room(*observed.shape[1:], dtype=BF16)
    hot_state = call(
        first_kernel,
        (block_count,),
        (block_user, block_slot, block_hour, user_factor, hot_factor, hour_factor, observed),
        (),
        state_of(hot_slots)
        + (shape(blocks, rank_size),)
        + sums
        + (shape(*table_of(hot_slots)), shape(2 * HALF, rank_size, dtype=BF16), row, row, row),
        [
            users_room,
            room(*hot_factor.shape, dtype=BF16),
            room(*hour_factor.shape, dtype=BF16),
            observed_room,
            pltpu.SemaphoreType.DMA((7,)),
        ],
        5 * 10**9,
    )
    hours_tab, slot_row = hot_state[-4], hot_state[-2]
    served = call(
        serve,
        needs if turns <= 8 else [jnp.concatenate(needs, axis=0).reshape(turns, -1)],
        (),
        (cold_factor, theirs),
        (shape(2 * reqs * IB, rank_size, dtype=BF16),) * turns,
        [room(2 * shard_len, rank_size, dtype=BF16)],
        10**6,
    )
    hot_state, served = lax.optimization_barrier((hot_state, served))
    fetched = [served[0]] + [turn(served[m], "users", peers, 2 * m) for m in range(1, turns)]
    needs = jnp.concatenate(needs, axis=0)
    cold_state = call(
        second_kernel,
        (block_count,),
        (user_factor, observed),
        hot_state,
        state_of(cold_slots) + (shape(blocks, rank_size),) + sums,
        [users_room, observed_room, pltpu.SemaphoreType.DMA((2,))],
        5 * 10**9,
    )
    *cold_state, hot_terms, hot_whole, hour_whole = cold_state
    send, keep, returned, cold_terms = call(
        third_kernel,
        (block_count,),
        (),
        (slot_row, hours_tab, *cold_state, hot_whole, hour_whole, *fetched),
        (
            shape(split_hot + 2 * high_rows, rank_size, dtype=BF16),
            shape(split_hot + high_rows, rank_size),
            shape(cold_slots * IB, rank_size, dtype=BF16),
            shape(blocks, rank_size),
        ),
        [room(*table_of(cold_slots)), room(*table_of(cold_slots)), room(2 * HALF, rank_size)],
        5 * 10**9,
    )
    returned = returned.reshape(peers, reqs * IB, rank_size)
    send_user, user = call(
        users_kernel,
        (block_count,),
        (),
        (slot_row, hot_state[5], hot_terms, cold_state[5], cold_terms),
        (shape(users // 2, rank_size, dtype=BF16), shape(users // 2, rank_size)),
        [],
        10**9,
    )

    got = hop(send, "items", items, 0)
    hot = keep[:split_hot] + got[:split_hot].astype(F32)
    hour = keep[split_hot:] + got[split_hot : split_hot + high_rows].astype(F32)
    hour += got[split_hot + high_rows :].astype(F32)
    user += hop(send_user, "items", items, 0).astype(F32)

    steps = [("items", items, bit) for bit in range(1, bits_of(items))]
    steps += [("users", peers, bit) for bit in range(bits_of(peers))]

    def send_back(returned, bit):
        size = returned.shape[0] // 2
        return jnp.concatenate([returned[:size], hop(returned[size:], "users", peers, bit)], axis=1)

    bits = list(range(bits_of(peers)))
    returned = send_back(returned, bits.pop())
    first = bits_of(items) - 1
    for place, step in enumerate(steps):
        last = place == len(steps) - 1
        rows = hot.shape[0] // 2
        high = lax.reduce_precision(hour, 8, 7)
        parts = [hot[rows:].astype(BF16), high.astype(BF16)]
        exact = step[0] == "items"
        if exact:
            parts.append((hour - high).astype(BF16))
        else:
            hour = high
        parts = jnp.concatenate(parts, axis=0)
        if place == first:
            parts, user = lax.optimization_barrier((parts, user))
        if place == first:
            needs = jnp.stack([needs, hop(needs, "users", peers, 0)], axis=1)
        got = hop(parts, *step)
        if place == first:
            for other in steps[:first]:
                rows_user = user.shape[0] // 2
                got_user = hop(user[rows_user:].astype(BF16), *other)
                if other != steps[first - 1]:
                    user = user[:rows_user] + got_user.astype(F32)
        if place % 2 and bits:
            returned = send_back(returned, bits.pop())
        elif not last:
            got, returned = lax.optimization_barrier((got, returned))
        if place == len(steps) - 2:
            got, got_user, needs = lax.optimization_barrier((got, got_user, needs))
        if last:
            got_hot = got[:rows]
            hot = hot[:rows]
            hour = hour + got[rows : rows + high_rows].astype(F32)
            break
        hot = hot[:rows] + got[:rows].astype(F32)
        hour = hour + got[rows : rows + high_rows].astype(F32)
        if exact:
            hour = hour + got[rows + high_rows :].astype(F32)
    while bits:
        returned = send_back(returned, bits.pop())
    user = user[:rows_user] + got_user.astype(F32)
    mine = hour[:half]
    other = hop(mine, "items", items, 0)
    if not permute_hot:
        hot, got_hot = jnp.zeros((IB, rank_size), F32), jnp.zeros((IB, rank_size), BF16)
    cold_grad, hot, hour_grad = call(
        finish,
        (),
        (),
        (needs.reshape(-1, peers), returned.reshape(-1, rank_size), mine, other, hot, got_hot),
        (shape(shard_len, rank_size), shape(hot.shape[0], rank_size), shape(hours, rank_size)),
        [],
        10**8,
    )
    if not permute_hot:
        hot_whole = jnp.concatenate([hot_whole[part] for part in range(hot_whole.shape[0])], axis=1)
        hot = lax.psum_scatter(hot_whole, ("users", "items"), scatter_dimension=0, tiled=True)
    return (user, cold_grad, hot, hour_grad)


def solution(mesh):
    in_specs = (
        P("users", None),
        P(),
        P(("users", "items"), None),
        P(),
        P(("users", "items"), None),
        P(("users", "items"), None),
        P(("users", "items"), None),
        P(("users", "items")),
        P(("users", "items"), None, None),
        P(("users", "items"), None, None),
    )
    out_specs = (
        P(("users", "items"), None),
        P(("users", "items"), None),
        P(("users", "items"), None),
        P(),
    )
    return jax.shard_map(body, mesh=mesh, in_specs=in_specs, out_specs=out_specs, check_vma=False)
```

time: 400 us -> 57.4 us (0.14)
  waiting for transfers between devices: 223 us -> 12.2 us
  other arithmetic: 69.9 us -> 1.25 us
  local copies, waits for them, and re-layouts: 55.7 us -> 0.77 us
  Pallas kernels: 0 us -> 18.2 us
  matrix products: 16.8 us -> 0 us
  between operations: 14.6 us -> 1.6 us
    reduce_scatter x2 -> x0, waiting for transfers between devices: 169 us -> none  [the longest x1 138 us: body(): lax.psum_scatter(grad_item[:hot_rows], ('users', 'items'), scatter_dimens...]
    scatter-add x4 -> x0, other arithmetic: 61.5 us -> none  [the longest x1 44.8 us: one_group(): grad_item.at[item_idx.reshape(-1)].add(item_terms.reshape(-1, rank_size))]
    psum x1 -> x0, waiting for transfers between devices: 45.4 us -> none  [body(): lax.psum(grad_hour, ('users', 'items')).reshape(hour_count, rank_size)]
    gather x3 -> x0, local copies, waits for them, and re-layouts: 37.5 us -> none  [the longest x1 32.9 us: one_group(): item_rows = item_table[item_idx]]
    ppermute x0 -> x19, starting transfers between devices: none -> 23.2 us  [the longest x13 13.1 us: hop(): return lax.ppermute(values, axis, [(i, i ^ 1 << bit) for i in range(size)])]
    all_to_all x3 -> x0, starting transfers between devices: 19.2 us -> none  [the longest x1 7.28 us: body(): lax.all_to_all(requests, 'users', split_axis=0, concat_axis=0, tiled=True)]
    pallas_call x0 -> x6, Pallas kernels: none -> 18.2 us  [call(): pl.pallas_call(functools.partial(function, sizes), out_shape=out_shape, i...]
    dot_general x4 -> x0, matrix products: 16.8 us -> none  [the longest x1 9.17 us: one_group(): jnp.einsum('gab,gbr->gar', residual, hour_rows, preferred_element_type=jn...]
  transfers between devices with their start and end apart: 6 -> 19, of which waited for: 4 -> 8; matrix products, arithmetic and copies ran while one was open for 21% -> 2% of each run, Pallas kernels for 0% -> 30%
where the time goes in v2:
time: 57.4 us; the launch traced here: 57.2 us
  starting transfers between devices  23.2 us (40%)
  Pallas kernels  18.2 us (32%)
  waiting for transfers between devices  12.2 us (21%)
  between operations  1.6 us (3%)
  other arithmetic  1.25 us (2%)
  local copies, waits for them, and re-layouts  0.77 us (1%)
    pallas_call x6, Pallas kernels, call(): pl.pallas_call(functools.partial(function, sizes), out_shape=out_shape, i...  18.2 us
    ppermute x13, starting transfers between devices, hop(): return lax.ppermute(values, axis, [(i, i ^ 1 << bit) for i in range(size)])  13.1 us
    ppermute x13, waiting for transfers between devices, hop(): return lax.ppermute(values, axis, [(i, i ^ 1 << bit) for i in range(size)])  10.8 us
    ppermute x6, starting transfers between devices, turn(): return lax.ppermute(values, axis, [(i, i ^ change) for i in range(size)])  10.1 us
    ppermute x6, waiting for transfers between devices, turn(): return lax.ppermute(values, axis, [(i, i ^ change) for i in range(size)])  1.43 us
  transfers between devices with their start and end apart: 19, of which 8 were waited for; matrix products, arithmetic and copies ran while one was open for 2% of the time, Pallas kernels for 30%

profile of v2, /device:TPU:0, one launch (start us, length us, event | category | flops | bytes accessed | tf_op | source)
XLA Modules:
  0.0 57.2 jit_solution(4665733520142896512)
XLA Ops:
  1.3 3.0 %collective-permute-start = (s32[1,2,8]{2,1,0:T(2,128)S(1)}, s32[1,2,8]{2,1,0:T(2,128)S(1)}, u32[]{:S(2)}, u32[]{:S(2)}) collective-permute-start(s32[1,2,8]{2,1,0:T(2,128)S(1)} %bitcast.9), channel_id=1, source_target_pairs={{0,8},{4,12},{8,0},{12,4},{16,24},{20,28},{24,16},{28,20},{1,9},{5... | collective-permute-start | bytes 200 | tf_op jit(solution)/shard_map/ppermute | solution.py:333
  4.3 2.6 %collective-permute-start.1 = (s32[1,2,8]{2,1,0:T(2,128)S(1)}, s32[1,2,8]{2,1,0:T(2,128)S(1)}, u32[]{:S(2)}, u32[]{:S(2)}) collective-permute-start(s32[1,2,8]{2,1,0:T(2,128)S(1)} %bitcast.10), channel_id=1, source_target_pairs={{0,16},{4,20},{8,24},{12,28},{16,0},{20,4},{24,8},{28,12},{1,17},{... | collective-permute-start | bytes 200 | tf_op jit(solution)/shard_map/ppermute | solution.py:333
  6.9 1.7 %collective-permute-start.3 = (bf16[256,256]{1,0:T(8,128)(2,1)}, bf16[256,256]{1,0:T(8,128)(2,1)S(1)}, u32[]{:S(2)}, u32[]{:S(2)}) collective-permute-start(bf16[256,256]{1,0:T(8,128)(2,1)} %refs_4_.1), channel_id=1, source_target_pairs={{0,4},{4,0},{8,12},{12,8},{16,20},{20,16},{24,28},{28,24},{1,5},{5... | collective-permute-start | bytes 393224 | tf_op jit(solution)/shard_map/ppermute | solution.py:329
  9.3 5.8 %first_kernel.1 = (f32[512,128]{1,0:T(8,128)S(1)}, f32[512,256]{1,0:T(8,128)S(1)}, f32[512,256]{1,0:T(8,128)S(1)}, bf16[512,32]{1,0:T(8,128)(2,1)S(1)}, bf16[32,...) custom-call(s32[1]{0:T(128)S(6)} %copy.15.count, ...), custom_call_target="tpu_custom_call" | custom-call | flops 5000000000 | bytes 4194304 | tf_op jit(solution)/shard_map/first_kernel/pallas_call | solution.py:390
  16.2 1.0 %collective-permute-start.4 = (bf16[64,256]{1,0:T(8,128)(2,1)S(1)}, bf16[64,256]{1,0:T(8,128)(2,1)S(1)}, u32[]{:S(2)}, u32[]{:S(2)}) collective-permute-start(bf16[64,256]{1,0:T(8,128)(2,1)S(1)} %get-tuple-element.108), channel_id=1, source_target_pairs={{0,8},{4,12},{8,0},{12,4},{16,24},{20,28},{24,16},{28,20},{1,9},{5... | collective-permute-start | bytes 98312 | tf_op jit(solution)/shard_map/ppermute | solution.py:333
  17.2 3.5 %collective-permute-start.5 = (bf16[64,256]{1,0:T(8,128)(2,1)S(1)}, bf16[64,256]{1,0:T(8,128)(2,1)S(1)}, u32[]{:S(2)}, u32[]{:S(2)}) collective-permute-start(bf16[64,256]{1,0:T(8,128)(2,1)S(1)} %get-tuple-element.109), channel_id=1, source_target_pairs={{0,16},{4,20},{8,24},{12,28},{16,0},{20,4},{24,8},{28,12},{1,17},{... | collective-permute-start | bytes 98312 | tf_op jit(solution)/shard_map/ppermute | solution.py:333
  20.6 4.3 %second_kernel.1 = (f32[512,128]{1,0:T(8,128)S(1)}, f32[512,256]{1,0:T(8,128)S(1)}, f32[512,256]{1,0:T(8,128)S(1)}, bf16[512,16]{1,0:T(8,128)(2,1)S(1)}, bf16[16...) custom-call(s32[1]{0:T(128)S(6)} %copy.15.count, ...), custom_call_target="tpu_custom_call" | custom-call | flops 5000000000 | bytes 4194304 | tf_op jit(solution)/shard_map/second_kernel/pallas_call | solution.py:390
  24.9 1.4 %collective-permute-done.6.refs_3_ = bf16[64,256]{1,0:T(8,128)(2,1)S(1)} collective-permute-done((bf16[64,256]{1,0:T(8,128)(2,1)S(1)}, bf16[64,256]{1,0:T(8,128)(2,1)S(1)}, u32[]{:S(2)}, u32[]{:S(2)}) %collective-permute-start.6) | collective-permute-done | bytes 32800 | tf_op jit(solution)/shard_map/ppermute | solution.py:333
  26.4 4.4 %third_kernel.1 = (bf16[448,256]{1,0:T(8,128)(2,1)S(1)}, f32[352,256]{1,0:T(8,128)S(1)}, bf16[256,256]{1,0:T(8,128)(2,1)S(1)}, f32[512,256]{1,0:T(8,128)S(1)}) custom-call(s32[1]{0:T(128)S(6)} %copy.15.count, s32[1,512]{1,0:T(1,128)S(1)} %get-tuple-element.97.slot, bf16[256,256]{1,0:T(8,128)(2,1)S(1)} %get-tuple-element.95.hours_tab, ...), custom_call_target="tpu_custom_call" | custom-call | flops 5000000000 | bytes 4194304 | tf_op jit(solution)/shard_map/third_kernel/pallas_call | solution.py:390
  31.1 1.2 %collective-permute-done.7 = bf16[448,256]{1,0:T(8,128)(2,1)S(1)} collective-permute-done((bf16[448,256]{1,0:T(8,128)(2,1)S(1)}, bf16[448,256]{1,0:T(8,128)(2,1)S(1)}, u32[]{:S(2)}, u32[]{:S(2)}) %collective-permute-start.7) | collective-permute-done | bytes 229408 | tf_op jit(solution)/shard_map/ppermute | solution.py:329
  32.5 1.6 %collective-permute-start.8 = (bf16[320,256]{1,0:T(8,128)(2,1)S(1)}, bf16[320,256]{1,0:T(8,128)(2,1)S(1)}, u32[]{:S(2)}, u32[]{:S(2)}) collective-permute-start(bf16[320,256]{1,0:T(8,128)(2,1)S(1)} %pad_maximum_fusion), channel_id=1, source_target_pairs={{0,2},{1,3},{2,0},{3,1},{4,6},{5,7},{6,4},{7,5},{8,10},{9,11},{10,... | collective-permute-start | bytes 491528 | tf_op jit(solution)/shard_map/ppermute | solution.py:329
  34.0 1.9 %users_kernel.1 = (bf16[1024,256]{1,0:T(8,128)(2,1)S(1)}, f32[1024,256]{1,0:T(8,128)S(1)}) custom-call(s32[1]{0:T(128)S(6)} %copy.15.count, s32[1,512]{1,0:T(1,128)S(1)} %get-tuple-element.97.slot, s32[1,512]{1,0:T(1,128)S(1)} %get-tuple-element.90.user_pos.pos, f32[512,256]{1,0:T(8,128)S(1)} %get-tuple-element.115.terms, ...), custom_call_target="tpu_custom_call" | custom-call | flops 1000000000 | bytes 4194304 | tf_op jit(solution)/shard_map/users_kernel/pallas_call | solution.py:390
  36.1 1.5 %collective-permute-done.9 = bf16[4,32,256]{2,1,0:T(8,128)(2,1)S(1)} collective-permute-done((bf16[4,32,256]{2,1,0:T(8,128)(2,1)S(1)}, bf16[4,32,256]{2,1,0:T(8,128)(2,1)S(1)}, u32[]{:S(2)}, u32[]{:S(2)}) %collective-permute-start.9) | collective-permute-done | bytes 65568 | tf_op jit(solution)/shard_map/ppermute | solution.py:329
  37.6 1.2 %collective-permute-done.8 = bf16[320,256]{1,0:T(8,128)(2,1)S(1)} collective-permute-done((bf16[320,256]{1,0:T(8,128)(2,1)S(1)}, bf16[320,256]{1,0:T(8,128)(2,1)S(1)}, u32[]{:S(2)}, u32[]{:S(2)}) %collective-permute-start.8) | collective-permute-done | bytes 163872 | tf_op jit(solution)/shard_map/ppermute | solution.py:329
  39.0 1.6 %collective-permute-start.11 = (bf16[160,256]{1,0:T(8,128)(2,1)S(1)}, bf16[160,256]{1,0:T(8,128)(2,1)S(1)}, u32[]{:S(2)}, u32[]{:S(2)}) collective-permute-start(bf16[160,256]{1,0:T(8,128)(2,1)S(1)} %pad_maximum_fusion.3), channel_id=1, source_target_pairs={{0,4},{4,0},{8,12},{12,8},{16,20},{20,16},{24,28},{28,24},{1,5},{5... | collective-permute-start | bytes 245768 | tf_op jit(solution)/shard_map/ppermute | solution.py:329
  40.6 1.8 %collective-permute-start.13 = (bf16[2,64,256]{2,1,0:T(8,128)(2,1)S(1)}, bf16[2,64,256]{2,1,0:T(8,128)(2,1)S(1)}, u32[]{:S(2)}, u32[]{:S(2)}) collective-permute-start(bf16[2,64,256]{2,1,0:T(8,128)(2,1)S(1)} %get-tuple-element.139), channel_id=1, source_target_pairs={{0,8},{4,12},{8,0},{12,4},{16,24},{20,28},{24,16},{28,20},{1,9},{5... | collective-permute-start | bytes 196616 | tf_op jit(solution)/shard_map/ppermute | solution.py:329
  42.4 1.6 %collective-permute-start.14 = (bf16[512,256]{1,0:T(8,128)(2,1)S(1)}, bf16[512,256]{1,0:T(8,128)(2,1)S(1)}, u32[]{:S(2)}, u32[]{:S(2)}) collective-permute-start(bf16[512,256]{1,0:T(8,128)(2,1)S(1)} %slice.197), channel_id=1, source_target_pairs={{0,2},{1,3},{2,0},{3,1},{4,6},{5,7},{6,4},{7,5},{8,10},{9,11},{10,... | collective-permute-start | bytes 786440 | tf_op jit(solution)/shard_map/ppermute | solution.py:329
  44.0 1.3 %collective-permute-start.12 = (bf16[128,256]{1,0:T(8,128)(2,1)S(1)}, bf16[128,256]{1,0:T(8,128)(2,1)S(1)}, u32[]{:S(2)}, u32[]{:S(2)}) collective-permute-start(bf16[128,256]{1,0:T(8,128)(2,1)S(1)} %pad_maximum_fusion.4), channel_id=1, source_target_pairs={{0,8},{4,12},{8,0},{12,4},{16,24},{20,28},{24,16},{28,20},{1,9},{5... | collective-permute-start | bytes 196616 | tf_op jit(solution)/shard_map/ppermute | solution.py:329
  45.4 3.0 %collective-permute-done.12 = bf16[128,256]{1,0:T(8,128)(2,1)S(1)} collective-permute-done((bf16[128,256]{1,0:T(8,128)(2,1)S(1)}, bf16[128,256]{1,0:T(8,128)(2,1)S(1)}, u32[]{:S(2)}, u32[]{:S(2)}) %collective-permute-start.12) | collective-permute-done | bytes 65568 | tf_op jit(solution)/shard_map/ppermute | solution.py:329
  48.4 1.2 %collective-permute-start.16 = (bf16[1,128,256]{2,1,0:T(8,128)(2,1)S(1)}, bf16[1,128,256]{2,1,0:T(8,128)(2,1)S(1)}, u32[]{:S(2)}, u32[]{:S(2)}) collective-permute-start(bf16[1,128,256]{2,1,0:T(8,128)(2,1)S(1)} %get-tuple-element.137), channel_id=1, source_target_pairs={{0,4},{4,0},{8,12},{12,8},{16,20},{20,16},{24,28},{28,24},{1,5},{5... | collective-permute-start | bytes 196616 | tf_op jit(solution)/shard_map/ppermute | solution.py:329
  49.6 1.7 %collective-permute-start.17 = (bf16[112,256]{1,0:T(8,128)(2,1)S(1)}, bf16[112,256]{1,0:T(8,128)(2,1)S(1)}, u32[]{:S(2)}, u32[]{:S(2)}) collective-permute-start(bf16[112,256]{1,0:T(8,128)(2,1)S(1)} %pad_maximum_fusion.5), channel_id=1, source_target_pairs={{0,16},{4,20},{8,24},{12,28},{16,0},{20,4},{24,8},{28,12},{1,17},{... | collective-permute-start | bytes 172040 | tf_op jit(solution)/shard_map/ppermute | solution.py:329
  51.3 1.4 %collective-permute-done.16 = bf16[1,128,256]{2,1,0:T(8,128)(2,1)S(1)} collective-permute-done((bf16[1,128,256]{2,1,0:T(8,128)(2,1)S(1)}, bf16[1,128,256]{2,1,0:T(8,128)(2,1)S(1)}, u32[]{:S(2)}, u32[]{:S(2)}) %collective-permute-start.16) | collective-permute-done | bytes 65568 | tf_op jit(solution)/shard_map/ppermute | solution.py:329
  52.7 2.0 %collective-permute-done.17 = bf16[112,256]{1,0:T(8,128)(2,1)S(1)} collective-permute-done((bf16[112,256]{1,0:T(8,128)(2,1)S(1)}, bf16[112,256]{1,0:T(8,128)(2,1)S(1)}, u32[]{:S(2)}, u32[]{:S(2)}) %collective-permute-start.17) | collective-permute-done | bytes 57376 | tf_op jit(solution)/shard_map/ppermute | solution.py:329
  56.1 1.1 %finish.1 = (f32[256,256]{1,0:T(8,128)}, f32[16,256]{1,0:T(8,128)}, f32[168,256]{1,0:T(8,128)}) custom-call(s32[16,8]{1,0:T(8,128)S(1)} %bitcast.15, bf16[256,256]{1,0:T(8,128)(2,1)S(1)} %maximum_bitcast_fusion.returned, f32[84,256]{1,0:T(8,128)S(1)} %slice_add_fusion.1.mine, f32[84,256]{1,0:T(8,128)S(1)} %collective-permute-done.18.other, ...), custom_call_target="tpu_custom_call" | custom-call | flops 100000000 | bytes 4194304 | tf_op jit(solution)/shard_map/finish/pallas_call | solution.py:390
  (57 shorter events, 3.9 us)
Async XLA Ops:
  0.6 0.7 %copy-start.1 = (s32[1,8,2]{1,2,0:T(2,128)S(1)}, s32[1,8,2]{1,2,0:T(2,128)}, u32[]{:S(2)}) copy-start(s32[1,8,2]{1,2,0:T(2,128)} %param.18) | copy-start | bytes 196
  1.3 13.8 %collective-permute-start = (s32[1,2,8]{2,1,0:T(2,128)S(1)}, s32[1,2,8]{2,1,0:T(2,128)S(1)}, u32[]{:S(2)}, u32[]{:S(2)}) collective-permute-start(s32[1,2,8]{2,1,0:T(2,128)S(1)} %bitcast.9), channel_id=1, source_target_pairs={{0,8},{4,12},{8,0},{12,4},{16,24},{20,28},{24,16},{28,20},{1,9},{5... | collective-permute-start | bytes 200 | tf_op jit(solution)/shard_map/ppermute | solution.py:333
  4.3 10.8 %collective-permute-start.1 = (s32[1,2,8]{2,1,0:T(2,128)S(1)}, s32[1,2,8]{2,1,0:T(2,128)S(1)}, u32[]{:S(2)}, u32[]{:S(2)}) collective-permute-start(s32[1,2,8]{2,1,0:T(2,128)S(1)} %bitcast.10), channel_id=1, source_target_pairs={{0,16},{4,20},{8,24},{12,28},{16,0},{20,4},{24,8},{28,12},{1,17},{... | collective-permute-start | bytes 200 | tf_op jit(solution)/shard_map/ppermute | solution.py:333
  6.9 8.2 %collective-permute-start.2 = (s32[1,2,8]{2,1,0:T(2,128)S(1)}, s32[1,2,8]{2,1,0:T(2,128)S(1)}, u32[]{:S(2)}, u32[]{:S(2)}) collective-permute-start(s32[1,2,8]{2,1,0:T(2,128)S(1)} %bitcast.11), channel_id=1, source_target_pairs={{0,24},{4,28},{8,16},{12,20},{16,8},{20,12},{24,0},{28,4},{1,25},{... | collective-permute-start | bytes 200 | tf_op jit(solution)/shard_map/ppermute | solution.py:333
  6.9 8.6 %collective-permute-start.3 = (bf16[256,256]{1,0:T(8,128)(2,1)}, bf16[256,256]{1,0:T(8,128)(2,1)S(1)}, u32[]{:S(2)}, u32[]{:S(2)}) collective-permute-start(bf16[256,256]{1,0:T(8,128)(2,1)} %refs_4_.1), channel_id=1, source_target_pairs={{0,4},{4,0},{8,12},{12,8},{16,20},{20,16},{24,28},{28,24},{1,5},{5... | collective-permute-start | bytes 393224 | tf_op jit(solution)/shard_map/ppermute | solution.py:329
  9.3 6.2 %copy-start = (bf16[256,256]{1,0:T(8,128)(2,1)S(1)}, bf16[256,256]{1,0:T(8,128)(2,1)}, u32[]{:S(2)}) copy-start(bf16[256,256]{1,0:T(8,128)(2,1)} %refs_4_.1) | copy-start | bytes 393220
  15.2 15.7 %collective-permute-start.15 = (s32[4,2,8]{2,1,0:T(2,128)S(1)}, s32[4,2,8]{2,1,0:T(2,128)S(1)}, u32[]{:S(2)}, u32[]{:S(2)}) collective-permute-start(s32[4,2,8]{2,1,0:T(2,128)S(1)} %pad_add_fusion.1), channel_id=1, source_target_pairs={{0,4},{4,0},{8,12},{12,8},{16,20},{20,16},{24,28},{28,24},{1,5},{5... | collective-permute-start | bytes 776 | tf_op jit(solution)/shard_map/ppermute | solution.py:329
  16.2 8.7 %collective-permute-start.4 = (bf16[64,256]{1,0:T(8,128)(2,1)S(1)}, bf16[64,256]{1,0:T(8,128)(2,1)S(1)}, u32[]{:S(2)}, u32[]{:S(2)}) collective-permute-start(bf16[64,256]{1,0:T(8,128)(2,1)S(1)} %get-tuple-element.108), channel_id=1, source_target_pairs={{0,8},{4,12},{8,0},{12,4},{16,24},{20,28},{24,16},{28,20},{1,9},{5... | collective-permute-start | bytes 98312 | tf_op jit(solution)/shard_map/ppermute | solution.py:333
  17.2 7.8 %collective-permute-start.5 = (bf16[64,256]{1,0:T(8,128)(2,1)S(1)}, bf16[64,256]{1,0:T(8,128)(2,1)S(1)}, u32[]{:S(2)}, u32[]{:S(2)}) collective-permute-start(bf16[64,256]{1,0:T(8,128)(2,1)S(1)} %get-tuple-element.109), channel_id=1, source_target_pairs={{0,16},{4,20},{8,24},{12,28},{16,0},{20,4},{24,8},{28,12},{1,17},{... | collective-permute-start | bytes 98312 | tf_op jit(solution)/shard_map/ppermute | solution.py:333
  20.6 5.7 %collective-permute-start.6 = (bf16[64,256]{1,0:T(8,128)(2,1)S(1)}, bf16[64,256]{1,0:T(8,128)(2,1)S(1)}, u32[]{:S(2)}, u32[]{:S(2)}) collective-permute-start(bf16[64,256]{1,0:T(8,128)(2,1)S(1)} %get-tuple-element.110), channel_id=1, source_target_pairs={{0,24},{4,28},{8,16},{12,20},{16,8},{20,12},{24,0},{28,4},{1,25},{... | collective-permute-start | bytes 98312 | tf_op jit(solution)/shard_map/ppermute | solution.py:333
  30.8 1.6 %collective-permute-start.7 = (bf16[448,256]{1,0:T(8,128)(2,1)S(1)}, bf16[448,256]{1,0:T(8,128)(2,1)S(1)}, u32[]{:S(2)}, u32[]{:S(2)}) collective-permute-start(bf16[448,256]{1,0:T(8,128)(2,1)S(1)} %get-tuple-element.112), channel_id=1, source_target_pairs={{0,1},{1,0},{2,3},{3,2},{4,5},{5,4},{6,7},{7,6},{8,9},{9,8},{10,11... | collective-permute-start | bytes 688136 | tf_op jit(solution)/shard_map/ppermute | solution.py:329
  30.9 6.6 %collective-permute-start.9 = (bf16[4,32,256]{2,1,0:T(8,128)(2,1)S(1)}, bf16[4,32,256]{2,1,0:T(8,128)(2,1)S(1)}, u32[]{:S(2)}, u32[]{:S(2)}) collective-permute-start(bf16[4,32,256]{2,1,0:T(8,128)(2,1)S(1)} %bitcast.17), channel_id=1, source_target_pairs={{0,16},{4,20},{8,24},{12,28},{16,0},{20,4},{24,8},{28,12},{1,17},{... | collective-permute-start | bytes 196616 | tf_op jit(solution)/shard_map/ppermute | solution.py:329
  32.5 6.3 %collective-permute-start.8 = (bf16[320,256]{1,0:T(8,128)(2,1)S(1)}, bf16[320,256]{1,0:T(8,128)(2,1)S(1)}, u32[]{:S(2)}, u32[]{:S(2)}) collective-permute-start(bf16[320,256]{1,0:T(8,128)(2,1)S(1)} %pad_maximum_fusion), channel_id=1, source_target_pairs={{0,2},{1,3},{2,0},{3,1},{4,6},{5,7},{6,4},{7,5},{8,10},{9,11},{10,... | collective-permute-start | bytes 491528 | tf_op jit(solution)/shard_map/ppermute | solution.py:329
  36.0 2.9 %collective-permute-start.10 = (bf16[1024,256]{1,0:T(8,128)(2,1)S(1)}, bf16[1024,256]{1,0:T(8,128)(2,1)S(1)}, u32[]{:S(2)}, u32[]{:S(2)}) collective-permute-start(bf16[1024,256]{1,0:T(8,128)(2,1)S(1)} %get-tuple-element.118), channel_id=1, source_target_pairs={{0,1},{1,0},{2,3},{3,2},{4,5},{5,4},{6,7},{7,6},{8,9},{9,8},{10,11... | collective-permute-start | bytes 1572872 | tf_op jit(solution)/shard_map/ppermute | solution.py:329
  39.0 4.9 %collective-permute-start.11 = (bf16[160,256]{1,0:T(8,128)(2,1)S(1)}, bf16[160,256]{1,0:T(8,128)(2,1)S(1)}, u32[]{:S(2)}, u32[]{:S(2)}) collective-permute-start(bf16[160,256]{1,0:T(8,128)(2,1)S(1)} %pad_maximum_fusion.3), channel_id=1, source_target_pairs={{0,4},{4,0},{8,12},{12,8},{16,20},{20,16},{24,28},{28,24},{1,5},{5... | collective-permute-start | bytes 245768 | tf_op jit(solution)/shard_map/ppermute | solution.py:329
  40.6 4.7 %collective-permute-start.13 = (bf16[2,64,256]{2,1,0:T(8,128)(2,1)S(1)}, bf16[2,64,256]{2,1,0:T(8,128)(2,1)S(1)}, u32[]{:S(2)}, u32[]{:S(2)}) collective-permute-start(bf16[2,64,256]{2,1,0:T(8,128)(2,1)S(1)} %get-tuple-element.139), channel_id=1, source_target_pairs={{0,8},{4,12},{8,0},{12,4},{16,24},{20,28},{24,16},{28,20},{1,9},{5... | collective-permute-start | bytes 196616 | tf_op jit(solution)/shard_map/ppermute | solution.py:329
  42.4 7.1 %collective-permute-start.14 = (bf16[512,256]{1,0:T(8,128)(2,1)S(1)}, bf16[512,256]{1,0:T(8,128)(2,1)S(1)}, u32[]{:S(2)}, u32[]{:S(2)}) collective-permute-start(bf16[512,256]{1,0:T(8,128)(2,1)S(1)} %slice.197), channel_id=1, source_target_pairs={{0,2},{1,3},{2,0},{3,1},{4,6},{5,7},{6,4},{7,5},{8,10},{9,11},{10,... | collective-permute-start | bytes 786440 | tf_op jit(solution)/shard_map/ppermute | solution.py:329
  44.0 4.3 %collective-permute-start.12 = (bf16[128,256]{1,0:T(8,128)(2,1)S(1)}, bf16[128,256]{1,0:T(8,128)(2,1)S(1)}, u32[]{:S(2)}, u32[]{:S(2)}) collective-permute-start(bf16[128,256]{1,0:T(8,128)(2,1)S(1)} %pad_maximum_fusion.4), channel_id=1, source_target_pairs={{0,8},{4,12},{8,0},{12,4},{16,24},{20,28},{24,16},{28,20},{1,9},{5... | collective-permute-start | bytes 196616 | tf_op jit(solution)/shard_map/ppermute | solution.py:329
  48.4 4.3 %collective-permute-start.16 = (bf16[1,128,256]{2,1,0:T(8,128)(2,1)S(1)}, bf16[1,128,256]{2,1,0:T(8,128)(2,1)S(1)}, u32[]{:S(2)}, u32[]{:S(2)}) collective-permute-start(bf16[1,128,256]{2,1,0:T(8,128)(2,1)S(1)} %get-tuple-element.137), channel_id=1, source_target_pairs={{0,4},{4,0},{8,12},{12,8},{16,20},{20,16},{24,28},{28,24},{1,5},{5... | collective-permute-start | bytes 196616 | tf_op jit(solution)/shard_map/ppermute | solution.py:329
  49.6 5.1 %collective-permute-start.17 = (bf16[112,256]{1,0:T(8,128)(2,1)S(1)}, bf16[112,256]{1,0:T(8,128)(2,1)S(1)}, u32[]{:S(2)}, u32[]{:S(2)}) collective-permute-start(bf16[112,256]{1,0:T(8,128)(2,1)S(1)} %pad_maximum_fusion.5), channel_id=1, source_target_pairs={{0,16},{4,20},{8,24},{12,28},{16,0},{20,4},{24,8},{28,12},{1,17},{... | collective-permute-start | bytes 172040 | tf_op jit(solution)/shard_map/ppermute | solution.py:329
  54.8 1.4 %collective-permute-start.18 = (f32[84,256]{1,0:T(8,128)S(1)}, f32[84,256]{1,0:T(8,128)S(1)}, u32[]{:S(2)}, u32[]{:S(2)}) collective-permute-start(f32[84,256]{1,0:T(8,128)S(1)} %slice_add_fusion.1.mine), channel_id=1, source_target_pairs={{0,1},{1,0},{2,3},{3,2},{4,5},{5,4},{6,7},{7,6},{8,9},{9,8},{10,11... | collective-permute-start | bytes 258056 | tf_op jit(solution)/shard_map/ppermute | solution.py:329

commit v3 on v2

--- a/solution.py
+++ b/solution.py
@@ -100,7 +100,7 @@
         put_pos = flip(slot_row ^ (p * sizes.items + q), bits_of(sizes.peers * sizes.items)) if sizes.permute_hot else slot_row
     else:
         owner, request = (slot_row - sizes.hot_slots) // sizes.reqs, (slot_row - sizes.hot_slots) % sizes.reqs
-        put_pos = (owner ^ p) * sizes.reqs + request
+        put_pos = flip(owner ^ p, bits_of(sizes.peers)) * sizes.reqs + request
         slot_row = (owner ^ (p & ~1)) * sizes.reqs + request
     pick[:m, :] = one_hot(spread(column(slot_row), slots) == lax.broadcasted_iota(jnp.int32, (m, slots), 1))
     put[:, :m] = one_hot(put_pos == lax.broadcasted_iota(jnp.int32, (slots, m), 0))
@@ -210,7 +210,7 @@
 
     def run(m):
         prepare(sizes, True, m, p, q, chosen, user, slot, hour, user_tab, observed, state)
-        work(sizes, m, 0, IB // 2, q, state, table, hours_tab, user_terms, item_sums, grad_hour)
+        work(sizes, m, 0, IB // 4, q, state, table, hours_tab, user_terms, item_sums, grad_hour)
 
     in_size(number, sizes.hot_blocks, slot.shape[1], run)
 
@@ -232,7 +232,7 @@
     _, number = chosen_blocks(sizes, True, count[0], slot[...])
 
     def run(m):
-        work(sizes, m, IB // 2, IB, q, state, table, hours_tab, user_terms, item_sums, grad_hour)
+        work(sizes, m, IB // 4, IB, q, state, table, hours_tab, user_terms, item_sums, grad_hour)
 
     in_size(number, sizes.hot_blocks, slot.shape[1], run)
     chosen, number = chosen_blocks(sizes, False, count[0], slot[...])
@@ -261,7 +261,7 @@
     _, number = chosen_blocks(sizes, False, count[0], slot[...])
 
     def run(m):
-        work(sizes, m, 0, IB, q, state, table, hours_tab, user_terms, item_sums, grad_hour)
+        work(sizes, m, 0, IB, q, state, table, hours_tab, user_terms, item_sums, grad_hour, stack=8)
 
     in_size(number, sizes.cold_blocks, slot.shape[1], run)
 
@@ -316,8 +316,7 @@
     mask = jnp.where(lane == p, needs[...], 0).astype(F32)
     wanted = jnp.broadcast_to(jnp.sum(mask, axis=1, keepdims=True), (asked, 128)).astype(BF16)
     number = lax.broadcasted_iota(jnp.int32, (asked, rows), 1) // IB
-    source = flip(number // sizes.reqs, bits_of(sizes.peers)) * sizes.reqs + number % sizes.reqs
-    place = one_hot(source == lax.broadcasted_iota(jnp.int32, (asked, rows), 0))
+    place = one_hot(number == lax.broadcasted_iota(jnp.int32, (asked, rows), 0))
     block = lax.dot_general(wanted, place, (((0,), (0,)), ((), ())), preferred_element_type=F32)[:1].astype(jnp.int32)
     size = (cold_grad.shape[0], rows)
     row, column = lax.broadcasted_iota(jnp.int32, size, 0), lax.broadcasted_iota(jnp.int32, size, 1)
@@ -426,7 +425,7 @@
             observed_room,
             pltpu.SemaphoreType.DMA((7,)),
         ],
-        5 * 10**9,
+        10**8,
     )
     hours_tab, slot_row = hot_state[-4], hot_state[-2]
     served = call(
@@ -466,6 +465,11 @@
         5 * 10**9,
     )
     returned = returned.reshape(peers, reqs * IB, rank_size)
+    got = hop(send, "items", items, 0)
+    got, cold_terms = lax.optimization_barrier((got, cold_terms))
+    hot = keep[:split_hot] + got[:split_hot].astype(F32)
+    hour = keep[split_hot:] + got[split_hot : split_hot + high_rows].astype(F32)
+    hour += got[split_hot + high_rows :].astype(F32)
     send_user, user = call(
         users_kernel,
         (block_count,),
@@ -476,62 +480,47 @@
         10**9,
     )
 
-    got = hop(send, "items", items, 0)
-    hot = keep[:split_hot] + got[:split_hot].astype(F32)
-    hour = keep[split_hot:] + got[split_hot : split_hot + high_rows].astype(F32)
-    hour += got[split_hot + high_rows :].astype(F32)
     user += hop(send_user, "items", items, 0).astype(F32)
-
-    steps = [("items", items, bit) for bit in range(1, bits_of(items))]
-    steps += [("users", peers, bit) for bit in range(bits_of(peers))]
-
-    def send_back(returned, bit):
-        size = returned.shape[0] // 2
-        return jnp.concatenate([returned[:size], hop(returned[size:], "users", peers, bit)], axis=1)
-
-    bits = list(range(bits_of(peers)))
-    returned = send_back(returned, bits.pop())
-    first = bits_of(items) - 1
-    for place, step in enumerate(steps):
-        last = place == len(steps) - 1
-        rows = hot.shape[0] // 2
+    rows = hot.shape[0] // 4
+    high = lax.reduce_precision(hour, 8, 7)
+    whole = high.astype(BF16)
+    parts = [[hot[k * rows : (k + 1) * rows].astype(BF16), whole] for k in range(1, 4)]
+    size = returned.shape[0] // 2
+    parts[0].append(returned[size:].reshape(-1, rank_size))
+    changes = (items, 2, items + 2)
+    got = [
+        turn(jnp.concatenate(part, axis=0), ("users", "items"), peers * items, change)
+        for part, change in zip(parts, changes)
+    ]
+    back = got[0][rows + high_rows :]
+    returned = jnp.concatenate([returned[:size], back.reshape(returned[:size].shape)], axis=1)
+    got = [one[: rows + high_rows] for one in got]
+    hot = hot[:rows] + sum(one[:rows].astype(F32) for one in got)
+    by_user, by_item, by_both = [one[rows:].astype(F32) for one in got]
+    hour = (high + by_item) + (by_user + by_both)
+
+    last = bits_of(peers) - 1
+    for bit in range(1, bits_of(peers)):
+        rows, size = hot.shape[0] // 2, returned.shape[0] // 2
         high = lax.reduce_precision(hour, 8, 7)
-        parts = [hot[rows:].astype(BF16), high.astype(BF16)]
-        exact = step[0] == "items"
-        if exact:
-            parts.append((hour - high).astype(BF16))
-        else:
-            hour = high
+        parts = [hot[rows:].astype(BF16), high.astype(BF16), returned[size:].reshape(-1, rank_size)]
         parts = jnp.concatenate(parts, axis=0)
-        if place == first:
-            parts, user = lax.optimization_barrier((parts, user))
-        if place == first:
+        if bit == 1:
+            parts, user, needs = lax.optimization_barrier((parts, user, needs))
+        got = hop(parts, "users", peers, bit)
+        if bit == 1:
+            keep_user = user.shape[0] // 2
+            got_user = hop(user[keep_user:].astype(BF16), "items", items, 1)
             needs = jnp.stack([needs, hop(needs, "users", peers, 0)], axis=1)
-        got = hop(parts, *step)
-        if place == first:
-            for other in steps[:first]:
-                rows_user = user.shape[0] // 2
-                got_user = hop(user[rows_user:].astype(BF16), *other)
-                if other != steps[first - 1]:
-                    user = user[:rows_user] + got_user.astype(F32)
-        if place % 2 and bits:
-            returned = send_back(returned, bits.pop())
-        elif not last:
-            got, returned = lax.optimization_barrier((got, returned))
-        if place == len(steps) - 2:
+        if bit == last:
             got, got_user, needs = lax.optimization_barrier((got, got_user, needs))
-        if last:
-            got_hot = got[:rows]
-            hot = hot[:rows]
-            hour = hour + got[rows : rows + high_rows].astype(F32)
-            break
-        hot = hot[:rows] + got[:rows].astype(F32)
-        hour = hour + got[rows : rows + high_rows].astype(F32)
-        if exact:
-            hour = hour + got[rows + high_rows :].astype(F32)
-    while bits:
-        returned = send_back(returned, bits.pop())
-    user = user[:rows_user] + got_user.astype(F32)
+        back = got[rows + high_rows :]
+        returned = jnp.concatenate([returned[:size], back.reshape(returned[:size].shape)], axis=1)
+        hour = high + got[rows : rows + high_rows].astype(F32)
+        if bit < last:
+            hot = hot[:rows] + got[:rows].astype(F32)
+    hot, got_hot = hot[:rows], got[:rows]
+    user = user[:keep_user] + got_user.astype(F32)
     mine = hour[:half]
     other = hop(mine, "items", items, 0)
     if not permute_hot:

time: 57.4 us -> 53.7 us (0.936)
  starting transfers between devices: 23.2 us -> 20.6 us
  local copies, waits for them, and re-layouts: 0.77 us -> 0.11 us
    ppermute x13 -> x8, starting transfers between devices: 13.1 us -> 8.12 us  [hop(): return lax.ppermute(values, axis, [(i, i ^ 1 << bit) for i in range(size)])]
    ppermute x6 -> x9, starting transfers between devices: 10.1 us -> 12.5 us  [turn(): return lax.ppermute(values, axis, [(i, i ^ change) for i in range(size)])]
    ppermute x13 -> x8, waiting for transfers between devices: 10.8 us -> 9.86 us  [hop(): return lax.ppermute(values, axis, [(i, i ^ 1 << bit) for i in range(size)])]
    ppermute x6 -> x9, waiting for transfers between devices: 1.43 us -> 2.23 us  [turn(): return lax.ppermute(values, axis, [(i, i ^ change) for i in range(size)])]
    unnamed x4, local copies, waits for them, and re-layouts: 0.68 us -> 0.01 us
  transfers between devices with their start and end apart: 19 -> 17, of which waited for: 8 -> 8; matrix products, arithmetic and copies ran while one was open for 2% -> 2% of each run, Pallas kernels for 30% -> 23%
where the time goes in v3:
time: 53.7 us; the launch traced here: 53.5 us
  starting transfers between devices  20.6 us (38%)
  Pallas kernels  17.9 us (33%)
  waiting for transfers between devices  12.1 us (23%)
  between operations  1.59 us (3%)
  other arithmetic  1.24 us (2%)
    pallas_call x6, Pallas kernels, call(): pl.pallas_call(functools.partial(function, sizes), out_shape=out_shape, i...  17.9 us
    ppermute x9, starting transfers between devices, turn(): return lax.ppermute(values, axis, [(i, i ^ change) for i in range(size)])  12.5 us
    ppermute x8, waiting for transfers between devices, hop(): return lax.ppermute(values, axis, [(i, i ^ 1 << bit) for i in range(size)])  9.86 us
    ppermute x8, starting transfers between devices, hop(): return lax.ppermute(values, axis, [(i, i ^ 1 << bit) for i in range(size)])  8.12 us
    ppermute x9, waiting for transfers between devices, turn(): return lax.ppermute(values, axis, [(i, i ^ change) for i in range(size)])  2.23 us
  transfers between devices with their start and end apart: 17, of which 8 were waited for; matrix products, arithmetic and copies ran while one was open for 2% of the time, Pallas kernels for 23%

profile of v3, /device:TPU:0, one launch (start us, length us, event | category | flops | bytes accessed | tf_op | source)
XLA Modules:
  0.0 53.5 jit_solution(7181735193695607755)
XLA Ops:
  0.6 3.0 %collective-permute-start.3 = (bf16[256,256]{1,0:T(8,128)(2,1)}, bf16[256,256]{1,0:T(8,128)(2,1)S(1)}, u32[]{:S(2)}, u32[]{:S(2)}) collective-permute-start(bf16[256,256]{1,0:T(8,128)(2,1)} %refs_4_.1), channel_id=1, source_target_pairs={{0,4},{4,0},{8,12},{12,8},{16,20},{20,16},{24,28},{28,24},{1,5},{5... | collective-permute-start | bytes 393224 | tf_op jit(solution)/shard_map/ppermute | solution.py:328
  3.7 1.6 %collective-permute-start = (s32[1,2,8]{2,1,0:T(2,128)S(1)}, s32[1,2,8]{2,1,0:T(2,128)S(1)}, u32[]{:S(2)}, u32[]{:S(2)}) collective-permute-start(s32[1,2,8]{2,1,0:T(2,128)S(1)} %bitcast.15), channel_id=1, source_target_pairs={{0,8},{4,12},{8,0},{12,4},{16,24},{20,28},{24,16},{28,20},{1,9},{5... | collective-permute-start | bytes 200 | tf_op jit(solution)/shard_map/ppermute | solution.py:332
  5.3 2.6 %collective-permute-start.1 = (s32[1,2,8]{2,1,0:T(2,128)S(1)}, s32[1,2,8]{2,1,0:T(2,128)S(1)}, u32[]{:S(2)}, u32[]{:S(2)}) collective-permute-start(s32[1,2,8]{2,1,0:T(2,128)S(1)} %bitcast.16), channel_id=1, source_target_pairs={{0,16},{4,20},{8,24},{12,28},{16,0},{20,4},{24,8},{28,12},{1,17},{... | collective-permute-start | bytes 200 | tf_op jit(solution)/shard_map/ppermute | solution.py:332
  8.7 4.4 %first_kernel.1 = (f32[512,128]{1,0:T(8,128)S(1)}, f32[512,256]{1,0:T(8,128)S(1)}, f32[512,256]{1,0:T(8,128)S(1)}, bf16[512,32]{1,0:T(8,128)(2,1)S(1)}, bf16[32,...) custom-call(s32[1]{0:T(128)S(6)} %copy.15.count, ...), custom_call_target="tpu_custom_call" | custom-call | flops 100000000 | bytes 4194304 | tf_op jit(solution)/shard_map/first_kernel/pallas_call | solution.py:389
  13.2 0.6 %serve.1 = (bf16[64,256]{1,0:T(8,128)(2,1)S(1)}, bf16[64,256]{1,0:T(8,128)(2,1)S(1)}, bf16[64,256]{1,0:T(8,128)(2,1)S(1)}, bf16[64,256]{1,0:T(8,128)(2,1)S(1)}) custom-call(s32[1,2,8]{2,1,0:T(2,128)S(1)} %bitcast.18, s32[1,2,8]{2,1,0:T(2,128)S(1)} %collective-permute-done.refs_1_, s32[1,2,8]{2,1,0:T(2,128)S(1)} %collective-permute-done.1.refs_2_, ...), custom_call_target="tpu_custom_call" | custom-call | flops 1000000 | bytes 4194304 | tf_op jit(solution)/shard_map/serve/pallas_call | solution.py:389
  13.9 0.7 %collective-permute-start.4 = (bf16[64,256]{1,0:T(8,128)(2,1)S(1)}, bf16[64,256]{1,0:T(8,128)(2,1)S(1)}, u32[]{:S(2)}, u32[]{:S(2)}) collective-permute-start(bf16[64,256]{1,0:T(8,128)(2,1)S(1)} %get-tuple-element.107), channel_id=1, source_target_pairs={{0,8},{4,12},{8,0},{12,4},{16,24},{20,28},{24,16},{28,20},{1,9},{5... | collective-permute-start | bytes 98312 | tf_op jit(solution)/shard_map/ppermute | solution.py:332
  14.6 3.5 %collective-permute-start.5 = (bf16[64,256]{1,0:T(8,128)(2,1)S(1)}, bf16[64,256]{1,0:T(8,128)(2,1)S(1)}, u32[]{:S(2)}, u32[]{:S(2)}) collective-permute-start(bf16[64,256]{1,0:T(8,128)(2,1)S(1)} %get-tuple-element.108), channel_id=1, source_target_pairs={{0,16},{4,20},{8,24},{12,28},{16,0},{20,4},{24,8},{28,12},{1,17},{... | collective-permute-start | bytes 98312 | tf_op jit(solution)/shard_map/ppermute | solution.py:332
  18.3 5.8 %second_kernel.1 = (f32[512,128]{1,0:T(8,128)S(1)}, f32[512,256]{1,0:T(8,128)S(1)}, f32[512,256]{1,0:T(8,128)S(1)}, bf16[512,16]{1,0:T(8,128)(2,1)S(1)}, bf16[16...) custom-call(s32[1]{0:T(128)S(6)} %copy.15.count, ...), custom_call_target="tpu_custom_call" | custom-call | flops 5000000000 | bytes 4194304 | tf_op jit(solution)/shard_map/second_kernel/pallas_call | solution.py:389
  24.1 4.1 %third_kernel.1 = (bf16[448,256]{1,0:T(8,128)(2,1)S(1)}, f32[352,256]{1,0:T(8,128)S(1)}, bf16[256,256]{1,0:T(8,128)(2,1)S(1)}, f32[512,256]{1,0:T(8,128)S(1)}) custom-call(s32[1]{0:T(128)S(6)} %copy.15.count, s32[1,512]{1,0:T(1,128)S(1)} %get-tuple-element.96.slot, bf16[256,256]{1,0:T(8,128)(2,1)S(1)} %get-tuple-element.94.hours_tab, ...), custom_call_target="tpu_custom_call" | custom-call | flops 5000000000 | bytes 4194304 | tf_op jit(solution)/shard_map/third_kernel/pallas_call | solution.py:389
  28.3 1.4 %collective-permute-done.7 = bf16[448,256]{1,0:T(8,128)(2,1)S(1)} collective-permute-done((bf16[448,256]{1,0:T(8,128)(2,1)S(1)}, bf16[448,256]{1,0:T(8,128)(2,1)S(1)}, u32[]{:S(2)}, u32[]{:S(2)}) %collective-permute-start.7) | collective-permute-done | bytes 229408 | tf_op jit(solution)/shard_map/ppermute | solution.py:328
  29.9 0.7 %collective-permute-start.8 = (bf16[288,256]{1,0:T(8,128)(2,1)S(1)}, bf16[288,256]{1,0:T(8,128)(2,1)S(1)}, u32[]{:S(2)}, u32[]{:S(2)}) collective-permute-start(bf16[288,256]{1,0:T(8,128)(2,1)S(1)} %pad_maximum_fusion), channel_id=1, source_target_pairs={{0,4},{1,5},{2,6},{3,7},{4,0},{5,1},{6,2},{7,3},{8,12},{9,13},{10,... | collective-permute-start | bytes 442376 | tf_op jit(solution)/shard_map/ppermute | solution.py:332
  30.5 2.4 %collective-permute-start.10 = (bf16[160,256]{1,0:T(8,128)(2,1)S(1)}, bf16[160,256]{1,0:T(8,128)(2,1)S(1)}, u32[]{:S(2)}, u32[]{:S(2)}) collective-permute-start(bf16[160,256]{1,0:T(8,128)(2,1)S(1)} %get-tuple-element.142), channel_id=1, source_target_pairs={{0,6},{1,7},{2,4},{3,5},{4,2},{5,3},{6,0},{7,1},{8,14},{9,15},{10,... | collective-permute-start | bytes 245768 | tf_op jit(solution)/shard_map/ppermute | solution.py:332
  33.0 0.5 collective-permute-start.9
  33.5 1.9 %users_kernel.1 = (bf16[1024,256]{1,0:T(8,128)(2,1)S(1)}, f32[1024,256]{1,0:T(8,128)S(1)}) custom-call(s32[1]{0:T(128)S(6)} %copy.15.count, s32[1,512]{1,0:T(1,128)S(1)} %get-tuple-element.96.slot, s32[1,512]{1,0:T(1,128)S(1)} %get-tuple-element.89.user_pos.pos, f32[512,256]{1,0:T(8,128)S(1)} %get-tuple-element.115.terms, ...), custom_call_target="tpu_custom_call" | custom-call | flops 1000000000 | bytes 4194304 | tf_op jit(solution)/shard_map/users_kernel/pallas_call | solution.py:389
  35.5 1.2 %collective-permute-done.10 = bf16[160,256]{1,0:T(8,128)(2,1)S(1)} collective-permute-done((bf16[160,256]{1,0:T(8,128)(2,1)S(1)}, bf16[160,256]{1,0:T(8,128)(2,1)S(1)}, u32[]{:S(2)}, u32[]{:S(2)}) %collective-permute-start.10) | collective-permute-done | bytes 81952 | tf_op jit(solution)/shard_map/ppermute | solution.py:332
  36.7 0.9 %collective-permute-done.9 = bf16[160,256]{1,0:T(8,128)(2,1)S(1)} collective-permute-done((bf16[160,256]{1,0:T(8,128)(2,1)S(1)}, bf16[160,256]{1,0:T(8,128)(2,1)S(1)}, u32[]{:S(2)}, u32[]{:S(2)}) %collective-permute-start.9) | collective-permute-done | bytes 81952 | tf_op jit(solution)/shard_map/ppermute | solution.py:332
  38.4 1.5 %collective-permute-start.14 = (bf16[512,256]{1,0:T(8,128)(2,1)S(1)}, bf16[512,256]{1,0:T(8,128)(2,1)S(1)}, u32[]{:S(2)}, u32[]{:S(2)}) collective-permute-start(bf16[512,256]{1,0:T(8,128)(2,1)S(1)} %slice.220), channel_id=1, source_target_pairs={{0,2},{1,3},{2,0},{3,1},{4,6},{5,7},{6,4},{7,5},{8,10},{9,11},{10,... | collective-permute-start | bytes 786440 | tf_op jit(solution)/shard_map/ppermute | solution.py:328
  39.8 3.3 %collective-permute-done.12 = bf16[256,256]{1,0:T(8,128)(2,1)S(1)} collective-permute-done((bf16[256,256]{1,0:T(8,128)(2,1)S(1)}, bf16[256,256]{1,0:T(8,128)(2,1)S(1)}, u32[]{:S(2)}, u32[]{:S(2)}) %collective-permute-start.12) | collective-permute-done | bytes 131104 | tf_op jit(solution)/shard_map/ppermute | solution.py:328
  43.3 2.4 %collective-permute-start.13 = (bf16[240,256]{1,0:T(8,128)(2,1)S(1)}, bf16[240,256]{1,0:T(8,128)(2,1)S(1)}, u32[]{:S(2)}, u32[]{:S(2)}) collective-permute-start(bf16[240,256]{1,0:T(8,128)(2,1)S(1)} %pad_maximum_fusion.3), channel_id=1, source_target_pairs={{0,16},{4,20},{8,24},{12,28},{16,0},{20,4},{24,8},{28,12},{1,17},{... | collective-permute-start | bytes 368648 | tf_op jit(solution)/shard_map/ppermute | solution.py:328
  45.7 0.6 %collective-permute-start.15 = (s32[4,2,8]{2,1,0:T(2,128)S(1)}, s32[4,2,8]{2,1,0:T(2,128)S(1)}, u32[]{:S(2)}, u32[]{:S(2)}) collective-permute-start(s32[4,2,8]{2,1,0:T(2,128)S(1)} %pad_add_fusion.1), channel_id=1, source_target_pairs={{0,4},{4,0},{8,12},{12,8},{16,20},{20,16},{24,28},{28,24},{1,5},{5... | collective-permute-start | bytes 776 | tf_op jit(solution)/shard_map/ppermute | solution.py:328
  46.3 3.0 %collective-permute-done.15 = s32[4,2,8]{2,1,0:T(2,128)S(1)} collective-permute-done((s32[4,2,8]{2,1,0:T(2,128)S(1)}, s32[4,2,8]{2,1,0:T(2,128)S(1)}, u32[]{:S(2)}, u32[]{:S(2)}) %collective-permute-start.15) | collective-permute-done | bytes 288 | tf_op jit(solution)/shard_map/ppermute | solution.py:328
  49.3 1.7 %collective-permute-done.13 = bf16[240,256]{1,0:T(8,128)(2,1)S(1)} collective-permute-done((bf16[240,256]{1,0:T(8,128)(2,1)S(1)}, bf16[240,256]{1,0:T(8,128)(2,1)S(1)}, u32[]{:S(2)}, u32[]{:S(2)}) %collective-permute-start.13) | collective-permute-done | bytes 122912 | tf_op jit(solution)/shard_map/ppermute | solution.py:328
  51.1 0.8 %convert_add_fusion.1 = f32[512,256]{1,0:T(8,128)} fusion(bf16[512,256]{1,0:T(8,128)(2,1)S(1)} %collective-permute-done.14, f32[1024,256]{1,0:T(8,128)S(1)} %convert_add_fusion), kind=kLoop, calls=%fused_computation.2 | loop fusion | flops 262144 | bytes 1310720 | tf_op jit(solution)/shard_map/add | solution.py:523
  52.4 1.1 %finish.1 = (f32[256,256]{1,0:T(8,128)}, f32[16,256]{1,0:T(8,128)}, f32[168,256]{1,0:T(8,128)}) custom-call(s32[16,8]{1,0:T(8,128)S(1)} %bitcast.14, bf16[256,256]{1,0:T(8,128)(2,1)S(1)} %maximum_bitcast_fusion.returned, f32[84,256]{1,0:T(8,128)S(1)} %slice_add_fusion.mine, f32[84,256]{1,0:T(8,128)S(1)} %collective-permute-done.16.other, ...), custom_call_target="tpu_custom_call" | custom-call | flops 100000000 | bytes 4194304 | tf_op jit(solution)/shard_map/finish/pallas_call | solution.py:389
  (51 shorter events, 2.1 us)
Async XLA Ops:
  0.6 3.0 %copy-start.1 = (s32[1,8,2]{1,2,0:T(2,128)S(1)}, s32[1,8,2]{1,2,0:T(2,128)}, u32[]{:S(2)}) copy-start(s32[1,8,2]{1,2,0:T(2,128)} %param.18) | copy-start | bytes 196
  0.6 12.6 %collective-permute-start.3 = (bf16[256,256]{1,0:T(8,128)(2,1)}, bf16[256,256]{1,0:T(8,128)(2,1)S(1)}, u32[]{:S(2)}, u32[]{:S(2)}) collective-permute-start(bf16[256,256]{1,0:T(8,128)(2,1)} %refs_4_.1), channel_id=1, source_target_pairs={{0,4},{4,0},{8,12},{12,8},{16,20},{20,16},{24,28},{28,24},{1,5},{5... | collective-permute-start | bytes 393224 | tf_op jit(solution)/shard_map/ppermute | solution.py:328
  3.7 9.4 %collective-permute-start = (s32[1,2,8]{2,1,0:T(2,128)S(1)}, s32[1,2,8]{2,1,0:T(2,128)S(1)}, u32[]{:S(2)}, u32[]{:S(2)}) collective-permute-start(s32[1,2,8]{2,1,0:T(2,128)S(1)} %bitcast.15), channel_id=1, source_target_pairs={{0,8},{4,12},{8,0},{12,4},{16,24},{20,28},{24,16},{28,20},{1,9},{5... | collective-permute-start | bytes 200 | tf_op jit(solution)/shard_map/ppermute | solution.py:332
  5.3 7.9 %collective-permute-start.1 = (s32[1,2,8]{2,1,0:T(2,128)S(1)}, s32[1,2,8]{2,1,0:T(2,128)S(1)}, u32[]{:S(2)}, u32[]{:S(2)}) collective-permute-start(s32[1,2,8]{2,1,0:T(2,128)S(1)} %bitcast.16), channel_id=1, source_target_pairs={{0,16},{4,20},{8,24},{12,28},{16,0},{20,4},{24,8},{28,12},{1,17},{... | collective-permute-start | bytes 200 | tf_op jit(solution)/shard_map/ppermute | solution.py:332
  7.8 5.4 %collective-permute-start.2 = (s32[1,2,8]{2,1,0:T(2,128)S(1)}, s32[1,2,8]{2,1,0:T(2,128)S(1)}, u32[]{:S(2)}, u32[]{:S(2)}) collective-permute-start(s32[1,2,8]{2,1,0:T(2,128)S(1)} %bitcast.17), channel_id=1, source_target_pairs={{0,24},{4,28},{8,16},{12,20},{16,8},{20,12},{24,0},{28,4},{1,25},{... | collective-permute-start | bytes 200 | tf_op jit(solution)/shard_map/ppermute | solution.py:332
  8.7 4.5 %copy-start = (bf16[256,256]{1,0:T(8,128)(2,1)S(1)}, bf16[256,256]{1,0:T(8,128)(2,1)}, u32[]{:S(2)}) copy-start(bf16[256,256]{1,0:T(8,128)(2,1)} %refs_4_.1) | copy-start | bytes 393220
  13.9 10.2 %collective-permute-start.4 = (bf16[64,256]{1,0:T(8,128)(2,1)S(1)}, bf16[64,256]{1,0:T(8,128)(2,1)S(1)}, u32[]{:S(2)}, u32[]{:S(2)}) collective-permute-start(bf16[64,256]{1,0:T(8,128)(2,1)S(1)} %get-tuple-element.107), channel_id=1, source_target_pairs={{0,8},{4,12},{8,0},{12,4},{16,24},{20,28},{24,16},{28,20},{1,9},{5... | collective-permute-start | bytes 98312 | tf_op jit(solution)/shard_map/ppermute | solution.py:332
  14.6 9.5 %collective-permute-start.5 = (bf16[64,256]{1,0:T(8,128)(2,1)S(1)}, bf16[64,256]{1,0:T(8,128)(2,1)S(1)}, u32[]{:S(2)}, u32[]{:S(2)}) collective-permute-start(bf16[64,256]{1,0:T(8,128)(2,1)S(1)} %get-tuple-element.108), channel_id=1, source_target_pairs={{0,16},{4,20},{8,24},{12,28},{16,0},{20,4},{24,8},{28,12},{1,17},{... | collective-permute-start | bytes 98312 | tf_op jit(solution)/shard_map/ppermute | solution.py:332
  18.0 6.1 %collective-permute-start.6 = (bf16[64,256]{1,0:T(8,128)(2,1)S(1)}, bf16[64,256]{1,0:T(8,128)(2,1)S(1)}, u32[]{:S(2)}, u32[]{:S(2)}) collective-permute-start(bf16[64,256]{1,0:T(8,128)(2,1)S(1)} %get-tuple-element.109), channel_id=1, source_target_pairs={{0,24},{4,28},{8,16},{12,20},{16,8},{20,12},{24,0},{28,4},{1,25},{... | collective-permute-start | bytes 98312 | tf_op jit(solution)/shard_map/ppermute | solution.py:332
  28.2 1.6 %collective-permute-start.7 = (bf16[448,256]{1,0:T(8,128)(2,1)S(1)}, bf16[448,256]{1,0:T(8,128)(2,1)S(1)}, u32[]{:S(2)}, u32[]{:S(2)}) collective-permute-start(bf16[448,256]{1,0:T(8,128)(2,1)S(1)} %get-tuple-element.111), channel_id=1, source_target_pairs={{0,1},{1,0},{2,3},{3,2},{4,5},{5,4},{6,7},{7,6},{8,9},{9,8},{10,11... | collective-permute-start | bytes 688136 | tf_op jit(solution)/shard_map/ppermute | solution.py:328
  29.9 7.8 %collective-permute-start.8 = (bf16[288,256]{1,0:T(8,128)(2,1)S(1)}, bf16[288,256]{1,0:T(8,128)(2,1)S(1)}, u32[]{:S(2)}, u32[]{:S(2)}) collective-permute-start(bf16[288,256]{1,0:T(8,128)(2,1)S(1)} %pad_maximum_fusion), channel_id=1, source_target_pairs={{0,4},{1,5},{2,6},{3,7},{4,0},{5,1},{6,2},{7,3},{8,12},{9,13},{10,... | collective-permute-start | bytes 442376 | tf_op jit(solution)/shard_map/ppermute | solution.py:332
  30.5 6.2 %collective-permute-start.10 = (bf16[160,256]{1,0:T(8,128)(2,1)S(1)}, bf16[160,256]{1,0:T(8,128)(2,1)S(1)}, u32[]{:S(2)}, u32[]{:S(2)}) collective-permute-start(bf16[160,256]{1,0:T(8,128)(2,1)S(1)} %get-tuple-element.142), channel_id=1, source_target_pairs={{0,6},{1,7},{2,4},{3,5},{4,2},{5,3},{6,0},{7,1},{8,14},{9,15},{10,... | collective-permute-start | bytes 245768 | tf_op jit(solution)/shard_map/ppermute | solution.py:332
  33.0 4.7 %collective-permute-start.9 = (bf16[160,256]{1,0:T(8,128)(2,1)S(1)}, bf16[160,256]{1,0:T(8,128)(2,1)S(1)}, u32[]{:S(2)}, u32[]{:S(2)}) collective-permute-start(bf16[160,256]{1,0:T(8,128)(2,1)S(1)} %get-tuple-element.141), channel_id=1, source_target_pairs={{0,2},{1,3},{2,0},{3,1},{4,6},{5,7},{6,4},{7,5},{8,10},{9,11},{10,... | collective-permute-start | bytes 245768 | tf_op jit(solution)/shard_map/ppermute | solution.py:332
  35.4 2.4 %collective-permute-start.11 = (bf16[1024,256]{1,0:T(8,128)(2,1)S(1)}, bf16[1024,256]{1,0:T(8,128)(2,1)S(1)}, u32[]{:S(2)}, u32[]{:S(2)}) collective-permute-start(bf16[1024,256]{1,0:T(8,128)(2,1)S(1)} %get-tuple-element.118), channel_id=1, source_target_pairs={{0,1},{1,0},{2,3},{3,2},{4,5},{5,4},{6,7},{7,6},{8,9},{9,8},{10,11... | collective-permute-start | bytes 1572872 | tf_op jit(solution)/shard_map/ppermute | solution.py:328
  38.0 5.2 %collective-permute-start.12 = (bf16[256,256]{1,0:T(8,128)(2,1)S(1)}, bf16[256,256]{1,0:T(8,128)(2,1)S(1)}, u32[]{:S(2)}, u32[]{:S(2)}) collective-permute-start(bf16[256,256]{1,0:T(8,128)(2,1)S(1)} %pad_maximum_fusion.2), channel_id=1, source_target_pairs={{0,8},{4,12},{8,0},{12,4},{16,24},{20,28},{24,16},{28,20},{1,9},{5... | collective-permute-start | bytes 393224 | tf_op jit(solution)/shard_map/ppermute | solution.py:328
  38.4 12.6 %collective-permute-start.14 = (bf16[512,256]{1,0:T(8,128)(2,1)S(1)}, bf16[512,256]{1,0:T(8,128)(2,1)S(1)}, u32[]{:S(2)}, u32[]{:S(2)}) collective-permute-start(bf16[512,256]{1,0:T(8,128)(2,1)S(1)} %slice.220), channel_id=1, source_target_pairs={{0,2},{1,3},{2,0},{3,1},{4,6},{5,7},{6,4},{7,5},{8,10},{9,11},{10,... | collective-permute-start | bytes 786440 | tf_op jit(solution)/shard_map/ppermute | solution.py:328
  43.3 7.7 %collective-permute-start.13 = (bf16[240,256]{1,0:T(8,128)(2,1)S(1)}, bf16[240,256]{1,0:T(8,128)(2,1)S(1)}, u32[]{:S(2)}, u32[]{:S(2)}) collective-permute-start(bf16[240,256]{1,0:T(8,128)(2,1)S(1)} %pad_maximum_fusion.3), channel_id=1, source_target_pairs={{0,16},{4,20},{8,24},{12,28},{16,0},{20,4},{24,8},{28,12},{1,17},{... | collective-permute-start | bytes 368648 | tf_op jit(solution)/shard_map/ppermute | solution.py:328
  45.7 3.6 %collective-permute-start.15 = (s32[4,2,8]{2,1,0:T(2,128)S(1)}, s32[4,2,8]{2,1,0:T(2,128)S(1)}, u32[]{:S(2)}, u32[]{:S(2)}) collective-permute-start(s32[4,2,8]{2,1,0:T(2,128)S(1)} %pad_add_fusion.1), channel_id=1, source_target_pairs={{0,4},{4,0},{8,12},{12,8},{16,20},{20,16},{24,28},{28,24},{1,5},{5... | collective-permute-start | bytes 776 | tf_op jit(solution)/shard_map/ppermute | solution.py:328
  51.1 1.4 %collective-permute-start.16 = (f32[84,256]{1,0:T(8,128)S(1)}, f32[84,256]{1,0:T(8,128)S(1)}, u32[]{:S(2)}, u32[]{:S(2)}) collective-permute-start(f32[84,256]{1,0:T(8,128)S(1)} %slice_add_fusion.mine), channel_id=1, source_target_pairs={{0,1},{1,0},{2,3},{3,2},{4,5},{5,4},{6,7},{7,6},{8,9},{9,8},{10,11... | collective-permute-start | bytes 258056 | tf_op jit(solution)/shard_map/ppermute | solution.py:328

commit v4 on v3

--- a/solution.py
+++ b/solution.py
@@ -67,7 +67,7 @@
     return chosen, jnp.sum(chosen.astype(F32))
 
 
-def prepare(sizes, hot, m, p, q, chosen, user, slot, hour, user_tab, observed, out):
+def prepare(sizes, hot, m, p, q, chosen, user, slot, hour, user_tab, observed, out, users_here=None):
     obs, live_hour, user_rows, pick, put, user_pos = out
     blocks = slot.shape[1]
     users = user_tab.shape[0]
@@ -88,6 +88,8 @@
     obs[:m, :] = jnp.dot(order, 0.5 - observed[...], preferred_element_type=F32)
 
     user_col, hour_col = column(user_row), column(hour_row)
+    if users_here is not None:
+        users_here.wait()
     step = 512
     total = jnp.zeros((m, user_tab.shape[1]), F32)
     for k in range(0, users, step):
@@ -111,7 +113,7 @@
     live_hour[:m, :] = (used & ((lane_hour // HB) == spread(hour_col, 2 * HALF))).astype(F32)
 
 
-def work(sizes, m, first, last, q, state, table, hours_tab, user_terms, item_sums, grad_hour, stack=4):
+def work(sizes, m, first, last, q, state, table, hours_tab, user_terms, item_sums, grad_hour, before=None, stack=8):
     obs, live_hour, user_rows, pick, put, _ = state
     slots = pick.shape[1]
     parts = range(table.shape[0])
@@ -120,7 +122,7 @@
     tile = one_hot(used & ((cell & (HB - 1)) == (lane_hour & (HB - 1))))
     cell_item = lax.broadcasted_iota(jnp.int32, (m, IB * HB), 1) // HB
 
-    def one(group, carry):
+    def one(group, terms_before, hours_before):
         places = [group * stack + j for j in range(stack)]
         rows, cells = [], []
         for a in places:
@@ -137,11 +139,10 @@
         live = jnp.concatenate([live_hour[:m, :]] * stack, axis=0)
         residual = ((0.5 * jnp.tanh(half_model) + seen) * live).astype(BF16)
         weighted = jnp.dot(residual, hours_tab[...], preferred_element_type=F32)
-        grad_hour[...] += lax.dot_general(
-            residual, user_item, (((0,), (0,)), ((), ())), preferred_element_type=F32
-        )
+        hour_terms = lax.dot_general(residual, user_item, (((0,), (0,)), ((), ())), preferred_element_type=F32)
+        grad_hour[...] = hour_terms + hours_before
         into = put[:, :m]
-        total = user_terms[:m, :]
+        total = terms_before
         for j, a in enumerate(places):
             mine = weighted[j * m : j * m + m]
             total += mine * rows[j]
@@ -152,19 +153,29 @@
             for part in parts:
                 item_sums[part, pl.ds(a, slots, stride=IB), :] = sums[:, part * 128 : part * 128 + 128]
         user_terms[:m, :] = total
+
+    def next_one(group, carry):
+        one(group, user_terms[:m, :], grad_hour[...])
         return carry
 
-    lax.fori_loop(first // stack, last // stack, one, 0)
+    if before is not None and last - first == stack:
+        one(first // stack, *[0.0 if ref is None else ref[: size or ref.shape[0], :] for ref, size in zip(before, (m, None))])
+    else:
+        lax.fori_loop(first // stack, last // stack, next_one, 0)
 
 
 def in_size(number, small, whole, run):
-    pl.when(number <= small)(lambda: run(small))
-    pl.when(number > small)(lambda: run(whole))
+    small = small if isinstance(small, tuple) else (small,)
+    pl.when(number <= small[0])(lambda: run(small[0]))
+    for below, m in zip(small, small[1:]):
+        pl.when((number > below) & (number <= m))(functools.partial(run, m))
+    pl.when(number > small[-1])(lambda: run(whole))
 
 
 def serve(sizes, *refs):
     turns = sizes.peers // 2
     needs, (mine, theirs), outs, table = refs[: -turns - 3], refs[-turns - 3 : -turns - 1], refs[-turns - 1 : -1], refs[-1]
+    needs = [(need, k) for need in needs for k in range(need.shape[0])]
     p = lax.axis_index("users")
     rows = mine.shape[0]
     table[pl.ds(pl.multiple_of((p & 1) * rows, rows), rows), :] = mine[...]
@@ -173,7 +184,7 @@
         for which in range(2):
             for r in range(sizes.reqs):
                 owner = (p & ~1) + which
-                block = needs[m][0, r, owner] if len(needs) == turns else needs[0][m, r * sizes.peers + owner]
+                block = needs[m][0][needs[m][1], r, owner]
                 at = pl.multiple_of(which * rows + block * IB, IB)
                 to = (which * sizes.reqs + r) * IB
                 out[to : to + IB, :] = table[pl.ds(at, IB), :]
@@ -188,20 +199,17 @@
 
 def first_kernel(
     sizes, count, user_in, slot_in, hour_in, user_tab_in, hot_in, hour_factor_in, observed_in,
-    obs, live_hour, user_rows, pick, put, user_pos, user_terms, item_sums, grad_hour,
-    table, hours_tab, user, slot, hour,
+    obs, live_hour, user_rows, pick, put, user_pos, table, hours_tab, user, slot, hour,
     user_tab, hot, hour_factor, observed, sems,
 ):
     state = (obs, live_hour, user_rows, pick, put, user_pos)
     p, q = lax.axis_index("users"), lax.axis_index("items")
-    sources = (slot_in, user_in, hour_in, observed_in.at[0], user_tab_in, hour_factor_in, hot_in)
-    copies = start_copies(zip(sources, (slot, user, hour, observed, user_tab, hour_factor, hot)), sems)
-    user_terms[...] = jnp.zeros_like(user_terms)
-    grad_hour[...] = jnp.zeros_like(grad_hour)
+    sources = (slot_in, user_in, hour_in, observed_in.at[0], hour_factor_in, hot_in, user_tab_in)
+    copies = start_copies(zip(sources, (slot, user, hour, observed, hour_factor, hot, user_tab)), sems)
     for copy in copies[:3]:
         copy.wait()
     chosen, number = chosen_blocks(sizes, True, count[0], slot[...])
-    for copy in copies[3:]:
+    for copy in copies[3:-1]:
         copy.wait()
     load_table(table, hot)
     row_hour, used = hour_of(lax.broadcasted_iota(jnp.int32, (2 * HALF, sizes.hours), 0), q & 1, sizes.hours)
@@ -209,16 +217,30 @@
     hours_tab[...] = jnp.dot(hit, hour_factor[...], preferred_element_type=F32).astype(BF16)
 
     def run(m):
-        prepare(sizes, True, m, p, q, chosen, user, slot, hour, user_tab, observed, state)
-        work(sizes, m, 0, IB // 4, q, state, table, hours_tab, user_terms, item_sums, grad_hour)
+        prepare(sizes, True, m, p, q, chosen, user, slot, hour, user_tab, observed, state, copies[-1])
 
     in_size(number, sizes.hot_blocks, slot.shape[1], run)
+
+
+def half_kernel(
+    sizes, count, obs, live_hour, user_rows, pick, put, user_pos, table, hours_tab, slot,
+    user_terms, item_sums, grad_hour,
+):
+    state = (obs, live_hour, user_rows, pick, put, user_pos)
+    q = lax.axis_index("items")
+    _, number = chosen_blocks(sizes, True, count[0], slot[...])
+
+    def run(m):
+        before = (None, None)
+        work(sizes, m, 0, IB // 2, q, state, table, hours_tab, user_terms, item_sums, grad_hour, before)
+
+    in_size(number, (sizes.hot_blocks * 11 // 12, sizes.hot_blocks), slot.shape[1], run)
 
 
 def second_kernel(
     sizes, count, user_tab_in, observed_in,
-    obs, live_hour, user_rows, pick, put, user_pos, user_terms_in, item_sums_in, grad_hour_in,
-    table, hours_tab, user, slot, hour,
+    obs, live_hour, user_rows, pick, put, user_pos, table, hours_tab, user, slot, hour,
+    user_terms_in, item_sums_in, grad_hour_in,
     obs_2, live_hour_2, user_rows_2, pick_2, put_2, user_pos_2, user_terms, item_sums, grad_hour,
     user_tab, observed, sems,
 ):
@@ -226,15 +248,16 @@
     state_2 = (obs_2, live_hour_2, user_rows_2, pick_2, put_2, user_pos_2)
     p, q = lax.axis_index("users"), lax.axis_index("items")
     copies = start_copies(zip((observed_in.at[0], user_tab_in), (observed, user_tab)), sems)
-    user_terms[...] = user_terms_in[...]
     item_sums[...] = item_sums_in[...]
-    grad_hour[...] = grad_hour_in[...]
     _, number = chosen_blocks(sizes, True, count[0], slot[...])
 
     def run(m):
-        work(sizes, m, IB // 4, IB, q, state, table, hours_tab, user_terms, item_sums, grad_hour)
-
-    in_size(number, sizes.hot_blocks, slot.shape[1], run)
+        before = (user_terms_in, grad_hour_in)
+        work(sizes, m, IB // 2, IB, q, state, table, hours_tab, user_terms, item_sums, grad_hour, before)
+        if m < user_terms.shape[0]:
+            user_terms[m:, :] = jnp.zeros_like(user_terms[m:, :])
+
+    in_size(number, (sizes.hot_blocks * 11 // 12, sizes.hot_blocks), slot.shape[1], run)
     chosen, number = chosen_blocks(sizes, False, count[0], slot[...])
     for copy in copies:
         copy.wait()
@@ -261,9 +284,9 @@
     _, number = chosen_blocks(sizes, False, count[0], slot[...])
 
     def run(m):
-        work(sizes, m, 0, IB, q, state, table, hours_tab, user_terms, item_sums, grad_hour, stack=8)
-
-    in_size(number, sizes.cold_blocks, slot.shape[1], run)
+        work(sizes, m, 0, IB, q, state, table, hours_tab, user_terms, item_sums, grad_hour)
+
+    in_size(number, (sizes.cold_blocks // 4 * 3, sizes.cold_blocks), slot.shape[1], run)
 
     high_rows = padded(sizes.hours // 2)
     at = sizes.split_hot
@@ -304,13 +327,16 @@
     in_size(number, sizes.hot_blocks, slot.shape[1], hot)
 
 
-def finish(sizes, needs, returned, mine, other, hot, got, cold_grad, hot_grad, hour_grad):
-    p, q = lax.axis_index("users"), lax.axis_index("items")
-    hot_grad[...] = hot[...] + got[...].astype(F32)
+def last_hours(sizes, mine, other, hour_grad):
     half = mine.shape[0]
-    swap = (q & 1) == 1
+    swap = (lax.axis_index("items") & 1) == 1
     hour_grad[:half, :] = jnp.where(swap, other[...], mine[...])
     hour_grad[half:, :] = jnp.where(swap, mine[...], other[...])
+
+
+def last_rows(sizes, needs, returned, hot, got, cold_grad, hot_grad):
+    p = lax.axis_index("users")
+    hot_grad[...] = hot[...] + got[...].astype(F32)
     asked, rows = needs.shape[0], returned.shape[0]
     lane = lax.broadcasted_iota(jnp.int32, needs.shape, 1)
     mask = jnp.where(lane == p, needs[...], 0).astype(F32)
@@ -400,7 +426,7 @@
     turns = peers // 2
     theirs = hop(cold_factor, "users", peers, 0)
     need = jnp.transpose(need_rows, (0, 2, 1))
-    needs = [need] + [turn(need, "users", peers, 2 * m) for m in range(1, turns)]
+    needs = [need, hop(need, "users", peers, 1)]
 
     def room(*dims, dtype=F32):
         return pltpu.VMEM(dims, dtype)
@@ -414,10 +440,7 @@
         (block_count,),
         (block_user, block_slot, block_hour, user_factor, hot_factor, hour_factor, observed),
         (),
-        state_of(hot_slots)
-        + (shape(blocks, rank_size),)
-        + sums
-        + (shape(*table_of(hot_slots)), shape(2 * HALF, rank_size, dtype=BF16), row, row, row),
+        state_of(hot_slots) + (shape(*table_of(hot_slots)), shape(2 * HALF, rank_size, dtype=BF16), row, row, row),
         [
             users_room,
             room(*hot_factor.shape, dtype=BF16),
@@ -428,24 +451,29 @@
         10**8,
     )
     hours_tab, slot_row = hot_state[-4], hot_state[-2]
+    needs, hot_state, theirs = lax.optimization_barrier((needs, hot_state, theirs))
+    for bit in range(2, bits_of(peers)):
+        needs.append(hop(jnp.concatenate(needs, axis=0), "users", peers, bit))
+    terms = (shape(blocks, rank_size),) + sums
+    hot_sums = call(half_kernel, (block_count,), (), (*hot_state[:8], slot_row), terms, [], 3 * 10**9)
     served = call(
         serve,
-        needs if turns <= 8 else [jnp.concatenate(needs, axis=0).reshape(turns, -1)],
+        needs,
         (),
         (cold_factor, theirs),
         (shape(2 * reqs * IB, rank_size, dtype=BF16),) * turns,
         [room(2 * shard_len, rank_size, dtype=BF16)],
         10**6,
     )
-    hot_state, served = lax.optimization_barrier((hot_state, served))
+    hot_state, hot_sums, served = lax.optimization_barrier((hot_state, hot_sums, served))
     fetched = [served[0]] + [turn(served[m], "users", peers, 2 * m) for m in range(1, turns)]
     needs = jnp.concatenate(needs, axis=0)
     cold_state = call(
         second_kernel,
         (block_count,),
         (user_factor, observed),
-        hot_state,
-        state_of(cold_slots) + (shape(blocks, rank_size),) + sums,
+        (*hot_state, *hot_sums),
+        state_of(cold_slots) + terms,
         [users_room, observed_room, pltpu.SemaphoreType.DMA((2,))],
         5 * 10**9,
     )
@@ -513,27 +541,28 @@
             got_user = hop(user[keep_user:].astype(BF16), "items", items, 1)
             needs = jnp.stack([needs, hop(needs, "users", peers, 0)], axis=1)
         if bit == last:
-            got, got_user, needs = lax.optimization_barrier((got, got_user, needs))
+            user = user[:keep_user] + got_user.astype(F32)
+            got, user, needs = lax.optimization_barrier((got, user, needs))
         back = got[rows + high_rows :]
         returned = jnp.concatenate([returned[:size], back.reshape(returned[:size].shape)], axis=1)
         hour = high + got[rows : rows + high_rows].astype(F32)
         if bit < last:
             hot = hot[:rows] + got[:rows].astype(F32)
     hot, got_hot = hot[:rows], got[:rows]
-    user = user[:keep_user] + got_user.astype(F32)
     mine = hour[:half]
     other = hop(mine, "items", items, 0)
     if not permute_hot:
         hot, got_hot = jnp.zeros((IB, rank_size), F32), jnp.zeros((IB, rank_size), BF16)
-    cold_grad, hot, hour_grad = call(
-        finish,
+    cold_grad, hot = call(
+        last_rows,
         (),
         (),
-        (needs.reshape(-1, peers), returned.reshape(-1, rank_size), mine, other, hot, got_hot),
-        (shape(shard_len, rank_size), shape(hot.shape[0], rank_size), shape(hours, rank_size)),
+        (needs.reshape(-1, peers), returned.reshape(-1, rank_size), hot, got_hot),
+        (shape(shard_len, rank_size), shape(hot.shape[0], rank_size)),
         [],
         10**8,
     )
+    (hour_grad,) = call(last_hours, (), (), (mine, other), (shape(hours, rank_size),), [], 10**6)
     if not permute_hot:
         hot_whole = jnp.concatenate([hot_whole[part] for part in range(hot_whole.shape[0])], axis=1)
         hot = lax.psum_scatter(hot_whole, ("users", "items"), scatter_dimension=0, tiled=True)

time: 53.7 us -> 51.6 us (0.961)
  starting transfers between devices: 20.6 us -> 18.9 us
    ppermute x9 -> x6, starting transfers between devices: 12.5 us -> 8.07 us  [turn(): return lax.ppermute(values, axis, [(i, i ^ change) for i in range(size)])]
    ppermute x8 -> x10, starting transfers between devices: 8.12 us -> 10.8 us  [hop(): return lax.ppermute(values, axis, [(i, i ^ 1 << bit) for i in range(size)])]
    ppermute x8 -> x10, waiting for transfers between devices: 9.86 us -> 10.2 us  [hop(): return lax.ppermute(values, axis, [(i, i ^ 1 << bit) for i in range(size)])]
    pallas_call x6 -> x8, Pallas kernels: 17.9 us -> 17.6 us  [call(): pl.pallas_call(functools.partial(function, sizes), out_shape=out_shape, i...]
    ppermute x9 -> x6, waiting for transfers between devices: 2.23 us -> 2.15 us  [turn(): return lax.ppermute(values, axis, [(i, i ^ change) for i in range(size)])]
  transfers between devices with their start and end apart: 17 -> 16, of which waited for: 8 -> 7; matrix products, arithmetic and copies ran while one was open for 2% -> 2% of each run, Pallas kernels for 23% -> 25%
where the time goes in v4:
time: 51.6 us; the launch traced here: 51.8 us
  starting transfers between devices  18.9 us (37%)
  Pallas kernels  17.6 us (34%)
  waiting for transfers between devices  12.4 us (24%)
  between operations  1.64 us (3%)
  other arithmetic  1.25 us (2%)
    pallas_call x8, Pallas kernels, call(): pl.pallas_call(functools.partial(function, sizes), out_shape=out_shape, i...  17.6 us
    ppermute x10, starting transfers between devices, hop(): return lax.ppermute(values, axis, [(i, i ^ 1 << bit) for i in range(size)])  10.8 us
    ppermute x10, waiting for transfers between devices, hop(): return lax.ppermute(values, axis, [(i, i ^ 1 << bit) for i in range(size)])  10.2 us
    ppermute x6, starting transfers between devices, turn(): return lax.ppermute(values, axis, [(i, i ^ change) for i in range(size)])  8.07 us
    ppermute x6, waiting for transfers between devices, turn(): return lax.ppermute(values, axis, [(i, i ^ change) for i in range(size)])  2.15 us
  transfers between devices with their start and end apart: 16, of which 7 were waited for; matrix products, arithmetic and copies ran while one was open for 2% of the time, Pallas kernels for 25%

profile of v4, /device:TPU:0, one launch (start us, length us, event | category | flops | bytes accessed | tf_op | source)
XLA Modules:
  0.0 51.8 jit_solution(12704742852863288186)
XLA Ops:
  0.6 3.0 %collective-permute-start.1 = (bf16[256,256]{1,0:T(8,128)(2,1)}, bf16[256,256]{1,0:T(8,128)(2,1)S(1)}, u32[]{:S(2)}, u32[]{:S(2)}) collective-permute-start(bf16[256,256]{1,0:T(8,128)(2,1)} %refs_3_.1), channel_id=1, source_target_pairs={{0,4},{4,0},{8,12},{12,8},{16,20},{20,16},{24,28},{28,24},{1,5},{5... | collective-permute-start | bytes 393224 | tf_op jit(solution)/shard_map/ppermute | solution.py:354
  3.7 1.6 %collective-permute-start = (s32[1,2,8]{2,1,0:T(2,128)S(1)}, s32[1,2,8]{2,1,0:T(2,128)S(1)}, u32[]{:S(2)}, u32[]{:S(2)}) collective-permute-start(s32[1,2,8]{2,1,0:T(2,128)S(1)} %bitcast.14), channel_id=1, source_target_pairs={{0,8},{4,12},{8,0},{12,4},{16,24},{20,28},{24,16},{28,20},{1,9},{5... | collective-permute-start | bytes 200 | tf_op jit(solution)/shard_map/ppermute | solution.py:354
  5.9 2.7 %first_kernel.1 = (f32[512,128]{1,0:T(8,128)S(1)}, f32[512,256]{1,0:T(8,128)S(1)}, f32[512,256]{1,0:T(8,128)S(1)}, bf16[512,32]{1,0:T(8,128)(2,1)S(1)}, bf16[32,...) custom-call(s32[1]{0:T(128)S(6)} %copy.15.count, ...), custom_call_target="tpu_custom_call" | custom-call | flops 100000000 | bytes 4194304 | tf_op jit(solution)/shard_map/first_kernel/pallas_call | solution.py:415
  8.6 2.7 %collective-permute-start.2 = (s32[2,2,8]{2,1,0:T(2,128)S(1)}, s32[2,2,8]{2,1,0:T(2,128)S(1)}, u32[]{:S(2)}, u32[]{:S(2)}) collective-permute-start(s32[2,2,8]{2,1,0:T(2,128)S(1)} %pad_add_fusion.2), channel_id=1, source_target_pairs={{0,16},{4,20},{8,24},{12,28},{16,0},{20,4},{24,8},{28,12},{1,17},{... | collective-permute-start | bytes 392 | tf_op jit(solution)/shard_map/ppermute | solution.py:354
  11.3 2.9 %half_kernel.1 = (f32[512,256]{1,0:T(8,128)S(1)}, f32[2,512,128]{2,1,0:T(8,128)S(1)}, f32[256,256]{1,0:T(8,128)S(1)}) custom-call(s32[1]{0:T(128)S(6)} %copy.15.count, f32[512,128]{1,0:T(8,128)S(1)} %get-tuple-element.111.obs, f32[512,256]{1,0:T(8,128)S(1)} %get-tuple-element.112.live_hour, f32[512,256]{1,0:T(8,128)S(1)} %get-tuple-element.113.user_rows, ...), custom_call_target="tpu_custom_call" | custom-call | flops 3000000000 | bytes 4194304 | tf_op jit(solution)/shard_map/half_kernel/pallas_call | solution.py:415
  15.2 1.8 %collective-permute-start.4 = (bf16[64,256]{1,0:T(8,128)(2,1)S(1)}, bf16[64,256]{1,0:T(8,128)(2,1)S(1)}, u32[]{:S(2)}, u32[]{:S(2)}) collective-permute-start(bf16[64,256]{1,0:T(8,128)(2,1)S(1)} %get-tuple-element.135), channel_id=1, source_target_pairs={{0,16},{4,20},{8,24},{12,28},{16,0},{20,4},{24,8},{28,12},{1,17},{... | collective-permute-start | bytes 98312 | tf_op jit(solution)/shard_map/ppermute | solution.py:358
  17.0 2.3 %collective-permute-start.5 = (bf16[64,256]{1,0:T(8,128)(2,1)S(1)}, bf16[64,256]{1,0:T(8,128)(2,1)S(1)}, u32[]{:S(2)}, u32[]{:S(2)}) collective-permute-start(bf16[64,256]{1,0:T(8,128)(2,1)S(1)} %get-tuple-element.136), channel_id=1, source_target_pairs={{0,24},{4,28},{8,16},{12,20},{16,8},{20,12},{24,0},{28,4},{1,25},{... | collective-permute-start | bytes 98312 | tf_op jit(solution)/shard_map/ppermute | solution.py:358
  19.3 4.3 %second_kernel.1 = (f32[512,128]{1,0:T(8,128)S(1)}, f32[512,256]{1,0:T(8,128)S(1)}, f32[512,256]{1,0:T(8,128)S(1)}, bf16[512,16]{1,0:T(8,128)(2,1)S(1)}, bf16[16...) custom-call(s32[1]{0:T(128)S(6)} %copy.15.count, ...), custom_call_target="tpu_custom_call" | custom-call | flops 5000000000 | bytes 4194304 | tf_op jit(solution)/shard_map/second_kernel/pallas_call | solution.py:415
  23.7 3.3 %third_kernel.1 = (bf16[448,256]{1,0:T(8,128)(2,1)S(1)}, f32[352,256]{1,0:T(8,128)S(1)}, bf16[256,256]{1,0:T(8,128)(2,1)S(1)}, f32[512,256]{1,0:T(8,128)S(1)}) custom-call(s32[1]{0:T(128)S(6)} %copy.15.count, s32[1,512]{1,0:T(1,128)S(1)} %get-tuple-element.120.slot, bf16[256,256]{1,0:T(8,128)(2,1)S(1)} %get-tuple-element.118.hours_tab, ...), custom_call_target="tpu_custom_call" | custom-call | flops 5000000000 | bytes 4194304 | tf_op jit(solution)/shard_map/third_kernel/pallas_call | solution.py:415
  27.1 1.4 %collective-permute-done.6 = bf16[448,256]{1,0:T(8,128)(2,1)S(1)} collective-permute-done((bf16[448,256]{1,0:T(8,128)(2,1)S(1)}, bf16[448,256]{1,0:T(8,128)(2,1)S(1)}, u32[]{:S(2)}, u32[]{:S(2)}) %collective-permute-start.6) | collective-permute-done | bytes 229408 | tf_op jit(solution)/shard_map/ppermute | solution.py:354
  29.3 1.5 %collective-permute-start.8 = (bf16[160,256]{1,0:T(8,128)(2,1)S(1)}, bf16[160,256]{1,0:T(8,128)(2,1)S(1)}, u32[]{:S(2)}, u32[]{:S(2)}) collective-permute-start(bf16[160,256]{1,0:T(8,128)(2,1)S(1)} %get-tuple-element.167), channel_id=1, source_target_pairs={{0,2},{1,3},{2,0},{3,1},{4,6},{5,7},{6,4},{7,5},{8,10},{9,11},{10,... | collective-permute-start | bytes 245768 | tf_op jit(solution)/shard_map/ppermute | solution.py:358
  30.8 1.5 %collective-permute-start.9 = (bf16[160,256]{1,0:T(8,128)(2,1)S(1)}, bf16[160,256]{1,0:T(8,128)(2,1)S(1)}, u32[]{:S(2)}, u32[]{:S(2)}) collective-permute-start(bf16[160,256]{1,0:T(8,128)(2,1)S(1)} %get-tuple-element.168), channel_id=1, source_target_pairs={{0,6},{1,7},{2,4},{3,5},{4,2},{5,3},{6,0},{7,1},{8,14},{9,15},{10,... | collective-permute-start | bytes 245768 | tf_op jit(solution)/shard_map/ppermute | solution.py:358
  32.3 1.9 %users_kernel.1 = (bf16[1024,256]{1,0:T(8,128)(2,1)S(1)}, f32[1024,256]{1,0:T(8,128)S(1)}) custom-call(s32[1]{0:T(128)S(6)} %copy.15.count, s32[1,512]{1,0:T(1,128)S(1)} %get-tuple-element.120.slot, s32[1,512]{1,0:T(1,128)S(1)} %get-tuple-element.116.user_pos.pos, f32[512,256]{1,0:T(8,128)S(1)} %get-tuple-element.142.terms, ...), custom_call_target="tpu_custom_call" | custom-call | flops 1000000000 | bytes 4194304 | tf_op jit(solution)/shard_map/users_kernel/pallas_call | solution.py:415
  34.3 2.1 %collective-permute-done.9 = bf16[160,256]{1,0:T(8,128)(2,1)S(1)} collective-permute-done((bf16[160,256]{1,0:T(8,128)(2,1)S(1)}, bf16[160,256]{1,0:T(8,128)(2,1)S(1)}, u32[]{:S(2)}, u32[]{:S(2)}) %collective-permute-start.9) | collective-permute-done | bytes 81952 | tf_op jit(solution)/shard_map/ppermute | solution.py:358
  36.8 0.8 %collective-permute-start.14 = (s32[4,2,8]{2,1,0:T(2,128)S(1)}, s32[4,2,8]{2,1,0:T(2,128)S(1)}, u32[]{:S(2)}, u32[]{:S(2)}) collective-permute-start(s32[4,2,8]{2,1,0:T(2,128)S(1)} %pad_add_fusion.1), channel_id=1, source_target_pairs={{0,4},{4,0},{8,12},{12,8},{16,20},{20,16},{24,28},{28,24},{1,5},{5... | collective-permute-start | bytes 776 | tf_op jit(solution)/shard_map/ppermute | solution.py:354
  37.6 1.4 %collective-permute-start.13 = (bf16[512,256]{1,0:T(8,128)(2,1)S(1)}, bf16[512,256]{1,0:T(8,128)(2,1)S(1)}, u32[]{:S(2)}, u32[]{:S(2)}) collective-permute-start(bf16[512,256]{1,0:T(8,128)(2,1)S(1)} %slice.220), channel_id=1, source_target_pairs={{0,2},{1,3},{2,0},{3,1},{4,6},{5,7},{6,4},{7,5},{8,10},{9,11},{10,... | collective-permute-start | bytes 786440 | tf_op jit(solution)/shard_map/ppermute | solution.py:354
  39.0 1.5 %collective-permute-done.14 = s32[4,2,8]{2,1,0:T(2,128)S(1)} collective-permute-done((s32[4,2,8]{2,1,0:T(2,128)S(1)}, s32[4,2,8]{2,1,0:T(2,128)S(1)}, u32[]{:S(2)}, u32[]{:S(2)}) %collective-permute-start.14) | collective-permute-done | bytes 288 | tf_op jit(solution)/shard_map/ppermute | solution.py:354
  40.5 1.4 %collective-permute-done.11 = bf16[256,256]{1,0:T(8,128)(2,1)S(1)} collective-permute-done((bf16[256,256]{1,0:T(8,128)(2,1)S(1)}, bf16[256,256]{1,0:T(8,128)(2,1)S(1)}, u32[]{:S(2)}, u32[]{:S(2)}) %collective-permute-start.11) | collective-permute-done | bytes 131104 | tf_op jit(solution)/shard_map/ppermute | solution.py:354
  42.1 1.1 %collective-permute-start.12 = (bf16[240,256]{1,0:T(8,128)(2,1)S(1)}, bf16[240,256]{1,0:T(8,128)(2,1)S(1)}, u32[]{:S(2)}, u32[]{:S(2)}) collective-permute-start(bf16[240,256]{1,0:T(8,128)(2,1)S(1)} %pad_maximum_fusion.3), channel_id=1, source_target_pairs={{0,16},{4,20},{8,24},{12,28},{16,0},{20,4},{24,8},{28,12},{1,17},{... | collective-permute-start | bytes 368648 | tf_op jit(solution)/shard_map/ppermute | solution.py:354
  43.2 2.0 %collective-permute-done.13 = bf16[512,256]{1,0:T(8,128)(2,1)S(1)} collective-permute-done((bf16[512,256]{1,0:T(8,128)(2,1)S(1)}, bf16[512,256]{1,0:T(8,128)(2,1)S(1)}, u32[]{:S(2)}, u32[]{:S(2)}) %collective-permute-start.13) | collective-permute-done | bytes 262176 | tf_op jit(solution)/shard_map/ppermute | solution.py:354
  45.2 0.8 %convert_add_fusion.1 = f32[512,256]{1,0:T(8,128)} fusion(bf16[512,256]{1,0:T(8,128)(2,1)S(1)} %collective-permute-done.13, f32[1024,256]{1,0:T(8,128)S(1)} %convert_add_fusion), kind=kLoop, calls=%fused_computation.2 | loop fusion | flops 262144 | bytes 1310720 | tf_op jit(solution)/shard_map/add | solution.py:544
  46.0 3.7 %collective-permute-done.12 = bf16[240,256]{1,0:T(8,128)(2,1)S(1)} collective-permute-done((bf16[240,256]{1,0:T(8,128)(2,1)S(1)}, bf16[240,256]{1,0:T(8,128)(2,1)S(1)}, u32[]{:S(2)}, u32[]{:S(2)}) %collective-permute-start.12) | collective-permute-done | bytes 122912 | tf_op jit(solution)/shard_map/ppermute | solution.py:354
  49.9 1.1 %last_rows.1 = (f32[256,256]{1,0:T(8,128)}, f32[16,256]{1,0:T(8,128)}) custom-call(s32[16,8]{1,0:T(8,128)S(1)} %bitcast.18, bf16[256,256]{1,0:T(8,128)(2,1)S(1)} %maximum_bitcast_fusion.returned, f32[16,256]{1,0:T(8,128)S(1)} %slice.176.hot, bf16[16,256]{1,0:T(8,128)(2,1)S(1)} %slice.151.got), custom_call_target="tpu_custom_call" | custom-call | flops 100000000 | bytes 4194304 | tf_op jit(solution)/shard_map/last_rows/pallas_call | solution.py:415
  51.1 0.7 %last_hours.1 = f32[168,256]{1,0:T(8,128)} custom-call(f32[84,256]{1,0:T(8,128)S(1)} %slice_add_fusion.mine, f32[84,256]{1,0:T(8,128)S(1)} %collective-permute-done.15.other), custom_call_target="tpu_custom_call" | custom-call | flops 1000000 | bytes 4194304 | tf_op jit(solution)/shard_map/last_hours/pallas_call | solution.py:415
  (52 shorter events, 2.5 us)
Async XLA Ops:
  0.6 3.0 %copy-start.1 = (s32[1,8,2]{1,2,0:T(2,128)S(1)}, s32[1,8,2]{1,2,0:T(2,128)}, u32[]{:S(2)}) copy-start(s32[1,8,2]{1,2,0:T(2,128)} %param.18) | copy-start | bytes 196
  0.6 7.9 %collective-permute-start.1 = (bf16[256,256]{1,0:T(8,128)(2,1)}, bf16[256,256]{1,0:T(8,128)(2,1)S(1)}, u32[]{:S(2)}, u32[]{:S(2)}) collective-permute-start(bf16[256,256]{1,0:T(8,128)(2,1)} %refs_3_.1), channel_id=1, source_target_pairs={{0,4},{4,0},{8,12},{12,8},{16,20},{20,16},{24,28},{28,24},{1,5},{5... | collective-permute-start | bytes 393224 | tf_op jit(solution)/shard_map/ppermute | solution.py:354
  3.7 4.9 %collective-permute-start = (s32[1,2,8]{2,1,0:T(2,128)S(1)}, s32[1,2,8]{2,1,0:T(2,128)S(1)}, u32[]{:S(2)}, u32[]{:S(2)}) collective-permute-start(s32[1,2,8]{2,1,0:T(2,128)S(1)} %bitcast.14), channel_id=1, source_target_pairs={{0,8},{4,12},{8,0},{12,4},{16,24},{20,28},{24,16},{28,20},{1,9},{5... | collective-permute-start | bytes 200 | tf_op jit(solution)/shard_map/ppermute | solution.py:354
  8.6 5.6 %copy-start = (bf16[256,256]{1,0:T(8,128)(2,1)S(1)}, bf16[256,256]{1,0:T(8,128)(2,1)}, u32[]{:S(2)}) copy-start(bf16[256,256]{1,0:T(8,128)(2,1)} %refs_3_.1) | copy-start | bytes 393220
  8.6 5.6 %collective-permute-start.2 = (s32[2,2,8]{2,1,0:T(2,128)S(1)}, s32[2,2,8]{2,1,0:T(2,128)S(1)}, u32[]{:S(2)}, u32[]{:S(2)}) collective-permute-start(s32[2,2,8]{2,1,0:T(2,128)S(1)} %pad_add_fusion.2), channel_id=1, source_target_pairs={{0,16},{4,20},{8,24},{12,28},{16,0},{20,4},{24,8},{28,12},{1,17},{... | collective-permute-start | bytes 392 | tf_op jit(solution)/shard_map/ppermute | solution.py:354
  14.9 8.8 %collective-permute-start.3 = (bf16[64,256]{1,0:T(8,128)(2,1)S(1)}, bf16[64,256]{1,0:T(8,128)(2,1)S(1)}, u32[]{:S(2)}, u32[]{:S(2)}) collective-permute-start(bf16[64,256]{1,0:T(8,128)(2,1)S(1)} %get-tuple-element.134), channel_id=1, source_target_pairs={{0,8},{4,12},{8,0},{12,4},{16,24},{20,28},{24,16},{28,20},{1,9},{5... | collective-permute-start | bytes 98312 | tf_op jit(solution)/shard_map/ppermute | solution.py:358
  15.2 8.5 %collective-permute-start.4 = (bf16[64,256]{1,0:T(8,128)(2,1)S(1)}, bf16[64,256]{1,0:T(8,128)(2,1)S(1)}, u32[]{:S(2)}, u32[]{:S(2)}) collective-permute-start(bf16[64,256]{1,0:T(8,128)(2,1)S(1)} %get-tuple-element.135), channel_id=1, source_target_pairs={{0,16},{4,20},{8,24},{12,28},{16,0},{20,4},{24,8},{28,12},{1,17},{... | collective-permute-start | bytes 98312 | tf_op jit(solution)/shard_map/ppermute | solution.py:358
  17.0 6.7 %collective-permute-start.5 = (bf16[64,256]{1,0:T(8,128)(2,1)S(1)}, bf16[64,256]{1,0:T(8,128)(2,1)S(1)}, u32[]{:S(2)}, u32[]{:S(2)}) collective-permute-start(bf16[64,256]{1,0:T(8,128)(2,1)S(1)} %get-tuple-element.136), channel_id=1, source_target_pairs={{0,24},{4,28},{8,16},{12,20},{16,8},{20,12},{24,0},{28,4},{1,25},{... | collective-permute-start | bytes 98312 | tf_op jit(solution)/shard_map/ppermute | solution.py:358
  27.0 1.6 %collective-permute-start.6 = (bf16[448,256]{1,0:T(8,128)(2,1)S(1)}, bf16[448,256]{1,0:T(8,128)(2,1)S(1)}, u32[]{:S(2)}, u32[]{:S(2)}) collective-permute-start(bf16[448,256]{1,0:T(8,128)(2,1)S(1)} %get-tuple-element.138), channel_id=1, source_target_pairs={{0,1},{1,0},{2,3},{3,2},{4,5},{5,4},{6,7},{7,6},{8,9},{9,8},{10,11... | collective-permute-start | bytes 688136 | tf_op jit(solution)/shard_map/ppermute | solution.py:354
  28.6 7.8 %collective-permute-start.7 = (bf16[288,256]{1,0:T(8,128)(2,1)S(1)}, bf16[288,256]{1,0:T(8,128)(2,1)S(1)}, u32[]{:S(2)}, u32[]{:S(2)}) collective-permute-start(bf16[288,256]{1,0:T(8,128)(2,1)S(1)} %pad_maximum_fusion), channel_id=1, source_target_pairs={{0,4},{1,5},{2,6},{3,7},{4,0},{5,1},{6,2},{7,3},{8,12},{9,13},{10,... | collective-permute-start | bytes 442376 | tf_op jit(solution)/shard_map/ppermute | solution.py:358
  29.3 5.0 %collective-permute-start.8 = (bf16[160,256]{1,0:T(8,128)(2,1)S(1)}, bf16[160,256]{1,0:T(8,128)(2,1)S(1)}, u32[]{:S(2)}, u32[]{:S(2)}) collective-permute-start(bf16[160,256]{1,0:T(8,128)(2,1)S(1)} %get-tuple-element.167), channel_id=1, source_target_pairs={{0,2},{1,3},{2,0},{3,1},{4,6},{5,7},{6,4},{7,5},{8,10},{9,11},{10,... | collective-permute-start | bytes 245768 | tf_op jit(solution)/shard_map/ppermute | solution.py:358
  30.8 5.6 %collective-permute-start.9 = (bf16[160,256]{1,0:T(8,128)(2,1)S(1)}, bf16[160,256]{1,0:T(8,128)(2,1)S(1)}, u32[]{:S(2)}, u32[]{:S(2)}) collective-permute-start(bf16[160,256]{1,0:T(8,128)(2,1)S(1)} %get-tuple-element.168), channel_id=1, source_target_pairs={{0,6},{1,7},{2,4},{3,5},{4,2},{5,3},{6,0},{7,1},{8,14},{9,15},{10,... | collective-permute-start | bytes 245768 | tf_op jit(solution)/shard_map/ppermute | solution.py:358
  34.2 2.4 %collective-permute-start.10 = (bf16[1024,256]{1,0:T(8,128)(2,1)S(1)}, bf16[1024,256]{1,0:T(8,128)(2,1)S(1)}, u32[]{:S(2)}, u32[]{:S(2)}) collective-permute-start(bf16[1024,256]{1,0:T(8,128)(2,1)S(1)} %get-tuple-element.145), channel_id=1, source_target_pairs={{0,1},{1,0},{2,3},{3,2},{4,5},{5,4},{6,7},{7,6},{8,9},{9,8},{10,11... | collective-permute-start | bytes 1572872 | tf_op jit(solution)/shard_map/ppermute | solution.py:354
  36.7 5.2 %collective-permute-start.11 = (bf16[256,256]{1,0:T(8,128)(2,1)S(1)}, bf16[256,256]{1,0:T(8,128)(2,1)S(1)}, u32[]{:S(2)}, u32[]{:S(2)}) collective-permute-start(bf16[256,256]{1,0:T(8,128)(2,1)S(1)} %pad_maximum_fusion.2), channel_id=1, source_target_pairs={{0,8},{4,12},{8,0},{12,4},{16,24},{20,28},{24,16},{28,20},{1,9},{5... | collective-permute-start | bytes 393224 | tf_op jit(solution)/shard_map/ppermute | solution.py:354
  36.8 3.7 %collective-permute-start.14 = (s32[4,2,8]{2,1,0:T(2,128)S(1)}, s32[4,2,8]{2,1,0:T(2,128)S(1)}, u32[]{:S(2)}, u32[]{:S(2)}) collective-permute-start(s32[4,2,8]{2,1,0:T(2,128)S(1)} %pad_add_fusion.1), channel_id=1, source_target_pairs={{0,4},{4,0},{8,12},{12,8},{16,20},{20,16},{24,28},{28,24},{1,5},{5... | collective-permute-start | bytes 776 | tf_op jit(solution)/shard_map/ppermute | solution.py:354
  37.6 7.6 %collective-permute-start.13 = (bf16[512,256]{1,0:T(8,128)(2,1)S(1)}, bf16[512,256]{1,0:T(8,128)(2,1)S(1)}, u32[]{:S(2)}, u32[]{:S(2)}) collective-permute-start(bf16[512,256]{1,0:T(8,128)(2,1)S(1)} %slice.220), channel_id=1, source_target_pairs={{0,2},{1,3},{2,0},{3,1},{4,6},{5,7},{6,4},{7,5},{8,10},{9,11},{10,... | collective-permute-start | bytes 786440 | tf_op jit(solution)/shard_map/ppermute | solution.py:354
  42.1 7.7 %collective-permute-start.12 = (bf16[240,256]{1,0:T(8,128)(2,1)S(1)}, bf16[240,256]{1,0:T(8,128)(2,1)S(1)}, u32[]{:S(2)}, u32[]{:S(2)}) collective-permute-start(bf16[240,256]{1,0:T(8,128)(2,1)S(1)} %pad_maximum_fusion.3), channel_id=1, source_target_pairs={{0,16},{4,20},{8,24},{12,28},{16,0},{20,4},{24,8},{28,12},{1,17},{... | collective-permute-start | bytes 368648 | tf_op jit(solution)/shard_map/ppermute | solution.py:354
  49.8 1.4 %collective-permute-start.15 = (f32[84,256]{1,0:T(8,128)S(1)}, f32[84,256]{1,0:T(8,128)S(1)}, u32[]{:S(2)}, u32[]{:S(2)}) collective-permute-start(f32[84,256]{1,0:T(8,128)S(1)} %slice_add_fusion.mine), channel_id=1, source_target_pairs={{0,1},{1,0},{2,3},{3,2},{4,5},{5,4},{6,7},{7,6},{8,9},{9,8},{10,11... | collective-permute-start | bytes 258056 | tf_op jit(solution)/shard_map/ppermute | solution.py:354

commit v5 on v4

--- a/solution.py
+++ b/solution.py
@@ -35,11 +35,15 @@
     return out
 
 
+def first_hours(hours):
+    return (hours // HB + 1) // 2 * HB
+
+
 def hour_of(lane, split, hours):
-    half = hours // 2
-    inside = lane & (HALF - 1)
-    hour = ((lane >> 7) ^ split) * half + inside
-    return hour, inside < half
+    half = first_hours(hours)
+    side = (lane >= half).astype(jnp.int32)
+    hour = (side ^ split) * half + lane - side * half
+    return hour, (lane < 2 * half) & (hour < hours)
 
 
 def one_hot(mask):
@@ -117,10 +121,11 @@
     obs, live_hour, user_rows, pick, put, _ = state
     slots = pick.shape[1]
     parts = range(table.shape[0])
-    lane_hour, used = hour_of(lax.broadcasted_iota(jnp.int32, (IB * HB, 2 * HALF), 1), q & 1, sizes.hours)
+    used = 2 * first_hours(sizes.hours)
+    lane = lax.broadcasted_iota(jnp.int32, (IB * HB, 2 * HALF), 1)
     cell = lax.broadcasted_iota(jnp.int32, (IB * HB, 2 * HALF), 0)
-    tile = one_hot(used & ((cell & (HB - 1)) == (lane_hour & (HB - 1))))
-    cell_item = lax.broadcasted_iota(jnp.int32, (m, IB * HB), 1) // HB
+    tile = one_hot(((cell & (HB - 1)) == (lane & (HB - 1))) & (((cell // HB) & 1) == lane // HALF))
+    cell_pair = lax.broadcasted_iota(jnp.int32, (m, IB * HB), 1) // (2 * HB)
 
     def one(group, terms_before, hours_before):
         places = [group * stack + j for j in range(stack)]
@@ -129,17 +134,25 @@
             of_place = pl.ds(a, slots, stride=IB)
             choice = jnp.concatenate([table[part, of_place, :] for part in parts], axis=1).astype(BF16)
             rows.append(jnp.dot(pick[:m, :], choice, preferred_element_type=F32))
-            cells.append(jnp.where(cell_item == a, obs[:m, :], 0.0).astype(BF16))
+        for pair in range(stack // 2):
+            cells.append(jnp.where(cell_pair == group * (stack // 2) + pair, obs[:m, :], 0.0).astype(BF16))
         users_f = user_rows[:m, :]
         user_item = jnp.concatenate([(users_f * row).astype(BF16) for row in rows], axis=0)
         half_model = lax.dot_general(
             user_item, hours_tab[...] * jnp.asarray(0.5, BF16), (((1,), (1,)), ((), ())), preferred_element_type=F32
         )
-        seen = jnp.dot(jnp.concatenate(cells, axis=0), tile, preferred_element_type=F32)
+        pairs = jnp.dot(jnp.concatenate(cells, axis=0), tile, preferred_element_type=F32)
+        seen = []
+        for j in range(stack):
+            one_place = pairs[j // 2 * m : j // 2 * m + m, j % 2 * HALF : j % 2 * HALF + HALF]
+            seen.append(jnp.concatenate([one_place, one_place], axis=1))
+        seen = jnp.concatenate(seen, axis=0)
         live = jnp.concatenate([live_hour[:m, :]] * stack, axis=0)
         residual = ((0.5 * jnp.tanh(half_model) + seen) * live).astype(BF16)
         weighted = jnp.dot(residual, hours_tab[...], preferred_element_type=F32)
-        hour_terms = lax.dot_general(residual, user_item, (((0,), (0,)), ((), ())), preferred_element_type=F32)
+        hour_terms = lax.dot_general(
+            residual[:, :used], user_item, (((0,), (0,)), ((), ())), preferred_element_type=F32
+        )
         grad_hour[...] = hour_terms + hours_before
         into = put[:, :m]
         total = terms_before
@@ -288,7 +301,7 @@
 
     in_size(number, (sizes.cold_blocks // 4 * 3, sizes.cold_blocks), slot.shape[1], run)
 
-    high_rows = padded(sizes.hours // 2)
+    high_rows = padded(first_hours(sizes.hours))
     at = sizes.split_hot
     for part in range(table.shape[0]):
         lanes = slice(part * 128, part * 128 + 128)
@@ -297,7 +310,8 @@
             send[:at, lanes] = hot_sums[part, at : 2 * at, :].astype(BF16)
         cold_send[:, lanes] = item_sums[part].astype(BF16)
     keep[at : at + high_rows, :] = grad_hour[:high_rows, :]
-    other = grad_hour[HALF : HALF + high_rows, :]
+    half = first_hours(sizes.hours)
+    other = jnp.concatenate([grad_hour[half:, :], jnp.zeros((high_rows - half, grad_hour.shape[1]), F32)], axis=0)
     high = other.astype(BF16)
     send[at : at + high_rows, :] = high
     send[at + high_rows : at + 2 * high_rows, :] = (other - high.astype(F32)).astype(BF16)
@@ -330,8 +344,9 @@
 def last_hours(sizes, mine, other, hour_grad):
     half = mine.shape[0]
     swap = (lax.axis_index("items") & 1) == 1
+    rest = hour_grad.shape[0] - half
     hour_grad[:half, :] = jnp.where(swap, other[...], mine[...])
-    hour_grad[half:, :] = jnp.where(swap, mine[...], other[...])
+    hour_grad[half:, :] = jnp.where(swap, mine[:rest, :], other[:rest, :])
 
 
 def last_rows(sizes, needs, returned, hot, got, cold_grad, hot_grad):
@@ -381,7 +396,7 @@
     shard_len = cold_factor.shape[0]
     peers, items = lax.axis_size("users"), lax.axis_size("items")
     reqs = need_rows.shape[2]
-    half = hours // 2
+    half = first_hours(hours)
     blocks = block_user.shape[1]
     users = user_factor.shape[0]
     hot_slots, cold_slots = hot_rows // IB, peers * reqs
@@ -432,7 +447,7 @@
         return pltpu.VMEM(dims, dtype)
 
     row = shape(1, blocks, dtype=jnp.int32)
-    sums = (shape(*table_of(hot_slots)), shape(2 * HALF, rank_size))
+    sums = (shape(*table_of(hot_slots)), shape(2 * half, rank_size))
     users_room = room(*user_factor.shape, dtype=BF16)
     observed_room = room(*observed.shape[1:], dtype=BF16)
     hot_state = call(
@@ -489,7 +504,7 @@
             shape(cold_slots * IB, rank_size, dtype=BF16),
             shape(blocks, rank_size),
         ),
-        [room(*table_of(cold_slots)), room(*table_of(cold_slots)), room(2 * HALF, rank_size)],
+        [room(*table_of(cold_slots)), room(*table_of(cold_slots)), room(2 * half, rank_size)],
         5 * 10**9,
     )
     returned = returned.reshape(peers, reqs * IB, rank_size)

time: 51.6 us -> 50.8 us (0.984)
  Pallas kernels: 17.6 us -> 16.6 us
  waiting for transfers between devices: 12.4 us -> 11.5 us
    ppermute x10, waiting for transfers between devices: 10.2 us -> 8.97 us  [hop(): return lax.ppermute(values, axis, [(i, i ^ 1 << bit) for i in range(size)])]
    pallas_call x8, Pallas kernels: 17.6 us -> 16.6 us  [call(): pl.pallas_call(functools.partial(function, sizes), out_shape=out_shape, i...]
    ppermute x10, starting transfers between devices: 10.8 us -> 11.4 us  [hop(): return lax.ppermute(values, axis, [(i, i ^ 1 << bit) for i in range(size)])]
  transfers between devices with their start and end apart: 16 -> 16, of which waited for: 7 -> 8; matrix products, arithmetic and copies ran while one was open for 2% -> 2% of each run, Pallas kernels for 25% -> 24%
where the time goes in v5:
time: 50.8 us; the launch traced here: 50.6 us
  starting transfers between devices  19.4 us (38%)
  Pallas kernels  16.6 us (33%)
  waiting for transfers between devices  11.5 us (23%)
  between operations  1.64 us (3%)
  other arithmetic  1.24 us (2%)
    pallas_call x8, Pallas kernels, call(): pl.pallas_call(functools.partial(function, sizes), out_shape=out_shape, i...  16.6 us
    ppermute x10, starting transfers between devices, hop(): return lax.ppermute(values, axis, [(i, i ^ 1 << bit) for i in range(size)])  11.4 us
    ppermute x10, waiting for transfers between devices, hop(): return lax.ppermute(values, axis, [(i, i ^ 1 << bit) for i in range(size)])  8.97 us
    ppermute x6, starting transfers between devices, turn(): return lax.ppermute(values, axis, [(i, i ^ change) for i in range(size)])  8.07 us
    ppermute x6, waiting for transfers between devices, turn(): return lax.ppermute(values, axis, [(i, i ^ change) for i in range(size)])  2.57 us
  transfers between devices with their start and end apart: 16, of which 8 were waited for; matrix products, arithmetic and copies ran while one was open for 2% of the time, Pallas kernels for 24%

profile of v5, /device:TPU:0, one launch (start us, length us, event | category | flops | bytes accessed | tf_op | source)
XLA Modules:
  0.0 50.6 jit_solution(3194435422412239966)
XLA Ops:
  0.6 3.0 %collective-permute-start.1 = (bf16[256,256]{1,0:T(8,128)(2,1)}, bf16[256,256]{1,0:T(8,128)(2,1)S(1)}, u32[]{:S(2)}, u32[]{:S(2)}) collective-permute-start(bf16[256,256]{1,0:T(8,128)(2,1)} %refs_3_.1), channel_id=1, source_target_pairs={{0,4},{4,0},{8,12},{12,8},{16,20},{20,16},{24,28},{28,24},{1,5},{5... | collective-permute-start | bytes 393224 | tf_op jit(solution)/shard_map/ppermute | solution.py:369
  3.7 1.6 %collective-permute-start = (s32[1,2,8]{2,1,0:T(2,128)S(1)}, s32[1,2,8]{2,1,0:T(2,128)S(1)}, u32[]{:S(2)}, u32[]{:S(2)}) collective-permute-start(s32[1,2,8]{2,1,0:T(2,128)S(1)} %bitcast.14), channel_id=1, source_target_pairs={{0,8},{4,12},{8,0},{12,4},{16,24},{20,28},{24,16},{28,20},{1,9},{5... | collective-permute-start | bytes 200 | tf_op jit(solution)/shard_map/ppermute | solution.py:369
  5.9 2.7 %first_kernel.1 = (f32[512,128]{1,0:T(8,128)S(1)}, f32[512,256]{1,0:T(8,128)S(1)}, f32[512,256]{1,0:T(8,128)S(1)}, bf16[512,32]{1,0:T(8,128)(2,1)S(1)}, bf16[32,...) custom-call(s32[1]{0:T(128)S(6)} %copy.15.count, ...), custom_call_target="tpu_custom_call" | custom-call | flops 100000000 | bytes 4194304 | tf_op jit(solution)/shard_map/first_kernel/pallas_call | solution.py:430
  8.6 2.7 %collective-permute-start.2 = (s32[2,2,8]{2,1,0:T(2,128)S(1)}, s32[2,2,8]{2,1,0:T(2,128)S(1)}, u32[]{:S(2)}, u32[]{:S(2)}) collective-permute-start(s32[2,2,8]{2,1,0:T(2,128)S(1)} %pad_add_fusion.2), channel_id=1, source_target_pairs={{0,16},{4,20},{8,24},{12,28},{16,0},{20,4},{24,8},{28,12},{1,17},{... | collective-permute-start | bytes 392 | tf_op jit(solution)/shard_map/ppermute | solution.py:369
  11.3 2.5 %half_kernel.1 = (f32[512,256]{1,0:T(8,128)S(1)}, f32[2,512,128]{2,1,0:T(8,128)S(1)}, f32[176,256]{1,0:T(8,128)S(1)}) custom-call(s32[1]{0:T(128)S(6)} %copy.15.count, f32[512,128]{1,0:T(8,128)S(1)} %get-tuple-element.111.obs, f32[512,256]{1,0:T(8,128)S(1)} %get-tuple-element.112.live_hour, f32[512,256]{1,0:T(8,128)S(1)} %get-tuple-element.113.user_rows, ...), custom_call_target="tpu_custom_call" | custom-call | flops 3000000000 | bytes 4194304 | tf_op jit(solution)/shard_map/half_kernel/pallas_call | solution.py:430
  15.0 2.0 %collective-permute-start.4 = (bf16[64,256]{1,0:T(8,128)(2,1)S(1)}, bf16[64,256]{1,0:T(8,128)(2,1)S(1)}, u32[]{:S(2)}, u32[]{:S(2)}) collective-permute-start(bf16[64,256]{1,0:T(8,128)(2,1)S(1)} %get-tuple-element.135), channel_id=1, source_target_pairs={{0,16},{4,20},{8,24},{12,28},{16,0},{20,4},{24,8},{28,12},{1,17},{... | collective-permute-start | bytes 98312 | tf_op jit(solution)/shard_map/ppermute | solution.py:373
  17.0 1.9 %collective-permute-start.5 = (bf16[64,256]{1,0:T(8,128)(2,1)S(1)}, bf16[64,256]{1,0:T(8,128)(2,1)S(1)}, u32[]{:S(2)}, u32[]{:S(2)}) collective-permute-start(bf16[64,256]{1,0:T(8,128)(2,1)S(1)} %get-tuple-element.136), channel_id=1, source_target_pairs={{0,24},{4,28},{8,16},{12,20},{16,8},{20,12},{24,0},{28,4},{1,25},{... | collective-permute-start | bytes 98312 | tf_op jit(solution)/shard_map/ppermute | solution.py:373
  18.9 4.0 %second_kernel.1 = (f32[512,128]{1,0:T(8,128)S(1)}, f32[512,256]{1,0:T(8,128)S(1)}, f32[512,256]{1,0:T(8,128)S(1)}, bf16[512,16]{1,0:T(8,128)(2,1)S(1)}, bf16[16...) custom-call(s32[1]{0:T(128)S(6)} %copy.15.count, ...), custom_call_target="tpu_custom_call" | custom-call | flops 5000000000 | bytes 4194304 | tf_op jit(solution)/shard_map/second_kernel/pallas_call | solution.py:430
  23.0 3.1 %third_kernel.1 = (bf16[448,256]{1,0:T(8,128)(2,1)S(1)}, f32[352,256]{1,0:T(8,128)S(1)}, bf16[256,256]{1,0:T(8,128)(2,1)S(1)}, f32[512,256]{1,0:T(8,128)S(1)}) custom-call(s32[1]{0:T(128)S(6)} %copy.15.count, s32[1,512]{1,0:T(1,128)S(1)} %get-tuple-element.120.slot, bf16[256,256]{1,0:T(8,128)(2,1)S(1)} %get-tuple-element.118.hours_tab, ...), custom_call_target="tpu_custom_call" | custom-call | flops 5000000000 | bytes 4194304 | tf_op jit(solution)/shard_map/third_kernel/pallas_call | solution.py:430
  26.1 1.4 %collective-permute-done.6 = bf16[448,256]{1,0:T(8,128)(2,1)S(1)} collective-permute-done((bf16[448,256]{1,0:T(8,128)(2,1)S(1)}, bf16[448,256]{1,0:T(8,128)(2,1)S(1)}, u32[]{:S(2)}, u32[]{:S(2)}) %collective-permute-start.6) | collective-permute-done | bytes 229408 | tf_op jit(solution)/shard_map/ppermute | solution.py:369
  27.7 1.3 %collective-permute-start.7 = (bf16[288,256]{1,0:T(8,128)(2,1)S(1)}, bf16[288,256]{1,0:T(8,128)(2,1)S(1)}, u32[]{:S(2)}, u32[]{:S(2)}) collective-permute-start(bf16[288,256]{1,0:T(8,128)(2,1)S(1)} %pad_maximum_fusion), channel_id=1, source_target_pairs={{0,4},{1,5},{2,6},{3,7},{4,0},{5,1},{6,2},{7,3},{8,12},{9,13},{10,... | collective-permute-start | bytes 442376 | tf_op jit(solution)/shard_map/ppermute | solution.py:373
  29.0 1.6 %collective-permute-start.8 = (bf16[160,256]{1,0:T(8,128)(2,1)S(1)}, bf16[160,256]{1,0:T(8,128)(2,1)S(1)}, u32[]{:S(2)}, u32[]{:S(2)}) collective-permute-start(bf16[160,256]{1,0:T(8,128)(2,1)S(1)} %get-tuple-element.167), channel_id=1, source_target_pairs={{0,2},{1,3},{2,0},{3,1},{4,6},{5,7},{6,4},{7,5},{8,10},{9,11},{10,... | collective-permute-start | bytes 245768 | tf_op jit(solution)/shard_map/ppermute | solution.py:373
  30.6 0.8 %collective-permute-start.9 = (bf16[160,256]{1,0:T(8,128)(2,1)S(1)}, bf16[160,256]{1,0:T(8,128)(2,1)S(1)}, u32[]{:S(2)}, u32[]{:S(2)}) collective-permute-start(bf16[160,256]{1,0:T(8,128)(2,1)S(1)} %get-tuple-element.168), channel_id=1, source_target_pairs={{0,6},{1,7},{2,4},{3,5},{4,2},{5,3},{6,0},{7,1},{8,14},{9,15},{10,... | collective-permute-start | bytes 245768 | tf_op jit(solution)/shard_map/ppermute | solution.py:373
  31.3 1.9 %users_kernel.1 = (bf16[1024,256]{1,0:T(8,128)(2,1)S(1)}, f32[1024,256]{1,0:T(8,128)S(1)}) custom-call(s32[1]{0:T(128)S(6)} %copy.15.count, s32[1,512]{1,0:T(1,128)S(1)} %get-tuple-element.120.slot, s32[1,512]{1,0:T(1,128)S(1)} %get-tuple-element.116.user_pos.pos, f32[512,256]{1,0:T(8,128)S(1)} %get-tuple-element.142.terms, ...), custom_call_target="tpu_custom_call" | custom-call | flops 1000000000 | bytes 4194304 | tf_op jit(solution)/shard_map/users_kernel/pallas_call | solution.py:430
  34.1 1.8 %collective-permute-done.9 = bf16[160,256]{1,0:T(8,128)(2,1)S(1)} collective-permute-done((bf16[160,256]{1,0:T(8,128)(2,1)S(1)}, bf16[160,256]{1,0:T(8,128)(2,1)S(1)}, u32[]{:S(2)}, u32[]{:S(2)}) %collective-permute-start.9) | collective-permute-done | bytes 81952 | tf_op jit(solution)/shard_map/ppermute | solution.py:373
  36.3 0.9 %collective-permute-start.14 = (s32[4,2,8]{2,1,0:T(2,128)S(1)}, s32[4,2,8]{2,1,0:T(2,128)S(1)}, u32[]{:S(2)}, u32[]{:S(2)}) collective-permute-start(s32[4,2,8]{2,1,0:T(2,128)S(1)} %pad_add_fusion.1), channel_id=1, source_target_pairs={{0,4},{4,0},{8,12},{12,8},{16,20},{20,16},{24,28},{28,24},{1,5},{5... | collective-permute-start | bytes 776 | tf_op jit(solution)/shard_map/ppermute | solution.py:369
  37.2 1.5 %collective-permute-start.13 = (bf16[512,256]{1,0:T(8,128)(2,1)S(1)}, bf16[512,256]{1,0:T(8,128)(2,1)S(1)}, u32[]{:S(2)}, u32[]{:S(2)}) collective-permute-start(bf16[512,256]{1,0:T(8,128)(2,1)S(1)} %slice.220), channel_id=1, source_target_pairs={{0,2},{1,3},{2,0},{3,1},{4,6},{5,7},{6,4},{7,5},{8,10},{9,11},{10,... | collective-permute-start | bytes 786440 | tf_op jit(solution)/shard_map/ppermute | solution.py:369
  38.7 1.3 %collective-permute-done.14 = s32[4,2,8]{2,1,0:T(2,128)S(1)} collective-permute-done((s32[4,2,8]{2,1,0:T(2,128)S(1)}, s32[4,2,8]{2,1,0:T(2,128)S(1)}, u32[]{:S(2)}, u32[]{:S(2)}) %collective-permute-start.14) | collective-permute-done | bytes 288 | tf_op jit(solution)/shard_map/ppermute | solution.py:369
  40.0 1.3 %collective-permute-done.11 = bf16[256,256]{1,0:T(8,128)(2,1)S(1)} collective-permute-done((bf16[256,256]{1,0:T(8,128)(2,1)S(1)}, bf16[256,256]{1,0:T(8,128)(2,1)S(1)}, u32[]{:S(2)}, u32[]{:S(2)}) %collective-permute-start.11) | collective-permute-done | bytes 131104 | tf_op jit(solution)/shard_map/ppermute | solution.py:369
  41.4 1.5 %collective-permute-start.12 = (bf16[240,256]{1,0:T(8,128)(2,1)S(1)}, bf16[240,256]{1,0:T(8,128)(2,1)S(1)}, u32[]{:S(2)}, u32[]{:S(2)}) collective-permute-start(bf16[240,256]{1,0:T(8,128)(2,1)S(1)} %pad_maximum_fusion.3), channel_id=1, source_target_pairs={{0,16},{4,20},{8,24},{12,28},{16,0},{20,4},{24,8},{28,12},{1,17},{... | collective-permute-start | bytes 368648 | tf_op jit(solution)/shard_map/ppermute | solution.py:369
  42.8 2.1 %collective-permute-done.13 = bf16[512,256]{1,0:T(8,128)(2,1)S(1)} collective-permute-done((bf16[512,256]{1,0:T(8,128)(2,1)S(1)}, bf16[512,256]{1,0:T(8,128)(2,1)S(1)}, u32[]{:S(2)}, u32[]{:S(2)}) %collective-permute-start.13) | collective-permute-done | bytes 262176 | tf_op jit(solution)/shard_map/ppermute | solution.py:369
  44.9 0.8 %convert_add_fusion.1 = f32[512,256]{1,0:T(8,128)} fusion(bf16[512,256]{1,0:T(8,128)(2,1)S(1)} %collective-permute-done.13, f32[1024,256]{1,0:T(8,128)S(1)} %convert_add_fusion), kind=kLoop, calls=%fused_computation.2 | loop fusion | flops 262144 | bytes 1310720 | tf_op jit(solution)/shard_map/add | solution.py:559
  45.8 2.7 %collective-permute-done.12 = bf16[240,256]{1,0:T(8,128)(2,1)S(1)} collective-permute-done((bf16[240,256]{1,0:T(8,128)(2,1)S(1)}, bf16[240,256]{1,0:T(8,128)(2,1)S(1)}, u32[]{:S(2)}, u32[]{:S(2)}) %collective-permute-start.12) | collective-permute-done | bytes 122912 | tf_op jit(solution)/shard_map/ppermute | solution.py:369
  48.7 1.1 %last_rows.1 = (f32[256,256]{1,0:T(8,128)}, f32[16,256]{1,0:T(8,128)}) custom-call(s32[16,8]{1,0:T(8,128)S(1)} %bitcast.18, bf16[256,256]{1,0:T(8,128)(2,1)S(1)} %maximum_bitcast_fusion.returned, f32[16,256]{1,0:T(8,128)S(1)} %slice.176.hot, bf16[16,256]{1,0:T(8,128)(2,1)S(1)} %slice.151.got), custom_call_target="tpu_custom_call" | custom-call | flops 100000000 | bytes 4194304 | tf_op jit(solution)/shard_map/last_rows/pallas_call | solution.py:430
  (52 shorter events, 3.6 us)
Async XLA Ops:
  0.6 3.0 %copy-start.1 = (s32[1,8,2]{1,2,0:T(2,128)S(1)}, s32[1,8,2]{1,2,0:T(2,128)}, u32[]{:S(2)}) copy-start(s32[1,8,2]{1,2,0:T(2,128)} %param.18) | copy-start | bytes 196
  0.6 7.9 %collective-permute-start.1 = (bf16[256,256]{1,0:T(8,128)(2,1)}, bf16[256,256]{1,0:T(8,128)(2,1)S(1)}, u32[]{:S(2)}, u32[]{:S(2)}) collective-permute-start(bf16[256,256]{1,0:T(8,128)(2,1)} %refs_3_.1), channel_id=1, source_target_pairs={{0,4},{4,0},{8,12},{12,8},{16,20},{20,16},{24,28},{28,24},{1,5},{5... | collective-permute-start | bytes 393224 | tf_op jit(solution)/shard_map/ppermute | solution.py:369
  3.7 4.9 %collective-permute-start = (s32[1,2,8]{2,1,0:T(2,128)S(1)}, s32[1,2,8]{2,1,0:T(2,128)S(1)}, u32[]{:S(2)}, u32[]{:S(2)}) collective-permute-start(s32[1,2,8]{2,1,0:T(2,128)S(1)} %bitcast.14), channel_id=1, source_target_pairs={{0,8},{4,12},{8,0},{12,4},{16,24},{20,28},{24,16},{28,20},{1,9},{5... | collective-permute-start | bytes 200 | tf_op jit(solution)/shard_map/ppermute | solution.py:369
  8.6 5.2 %copy-start = (bf16[256,256]{1,0:T(8,128)(2,1)S(1)}, bf16[256,256]{1,0:T(8,128)(2,1)}, u32[]{:S(2)}) copy-start(bf16[256,256]{1,0:T(8,128)(2,1)} %refs_3_.1) | copy-start | bytes 393220
  8.6 5.2 %collective-permute-start.2 = (s32[2,2,8]{2,1,0:T(2,128)S(1)}, s32[2,2,8]{2,1,0:T(2,128)S(1)}, u32[]{:S(2)}, u32[]{:S(2)}) collective-permute-start(s32[2,2,8]{2,1,0:T(2,128)S(1)} %pad_add_fusion.2), channel_id=1, source_target_pairs={{0,16},{4,20},{8,24},{12,28},{16,0},{20,4},{24,8},{28,12},{1,17},{... | collective-permute-start | bytes 392 | tf_op jit(solution)/shard_map/ppermute | solution.py:369
  14.5 8.5 %collective-permute-start.3 = (bf16[64,256]{1,0:T(8,128)(2,1)S(1)}, bf16[64,256]{1,0:T(8,128)(2,1)S(1)}, u32[]{:S(2)}, u32[]{:S(2)}) collective-permute-start(bf16[64,256]{1,0:T(8,128)(2,1)S(1)} %get-tuple-element.134), channel_id=1, source_target_pairs={{0,8},{4,12},{8,0},{12,4},{16,24},{20,28},{24,16},{28,20},{1,9},{5... | collective-permute-start | bytes 98312 | tf_op jit(solution)/shard_map/ppermute | solution.py:373
  15.0 7.9 %collective-permute-start.4 = (bf16[64,256]{1,0:T(8,128)(2,1)S(1)}, bf16[64,256]{1,0:T(8,128)(2,1)S(1)}, u32[]{:S(2)}, u32[]{:S(2)}) collective-permute-start(bf16[64,256]{1,0:T(8,128)(2,1)S(1)} %get-tuple-element.135), channel_id=1, source_target_pairs={{0,16},{4,20},{8,24},{12,28},{16,0},{20,4},{24,8},{28,12},{1,17},{... | collective-permute-start | bytes 98312 | tf_op jit(solution)/shard_map/ppermute | solution.py:373
  17.0 6.0 %collective-permute-start.5 = (bf16[64,256]{1,0:T(8,128)(2,1)S(1)}, bf16[64,256]{1,0:T(8,128)(2,1)S(1)}, u32[]{:S(2)}, u32[]{:S(2)}) collective-permute-start(bf16[64,256]{1,0:T(8,128)(2,1)S(1)} %get-tuple-element.136), channel_id=1, source_target_pairs={{0,24},{4,28},{8,16},{12,20},{16,8},{20,12},{24,0},{28,4},{1,25},{... | collective-permute-start | bytes 98312 | tf_op jit(solution)/shard_map/ppermute | solution.py:373
  26.0 1.6 %collective-permute-start.6 = (bf16[448,256]{1,0:T(8,128)(2,1)S(1)}, bf16[448,256]{1,0:T(8,128)(2,1)S(1)}, u32[]{:S(2)}, u32[]{:S(2)}) collective-permute-start(bf16[448,256]{1,0:T(8,128)(2,1)S(1)} %get-tuple-element.138), channel_id=1, source_target_pairs={{0,1},{1,0},{2,3},{3,2},{4,5},{5,4},{6,7},{7,6},{8,9},{9,8},{10,11... | collective-permute-start | bytes 688136 | tf_op jit(solution)/shard_map/ppermute | solution.py:369
  27.7 8.2 %collective-permute-start.7 = (bf16[288,256]{1,0:T(8,128)(2,1)S(1)}, bf16[288,256]{1,0:T(8,128)(2,1)S(1)}, u32[]{:S(2)}, u32[]{:S(2)}) collective-permute-start(bf16[288,256]{1,0:T(8,128)(2,1)S(1)} %pad_maximum_fusion), channel_id=1, source_target_pairs={{0,4},{1,5},{2,6},{3,7},{4,0},{5,1},{6,2},{7,3},{8,12},{9,13},{10,... | collective-permute-start | bytes 442376 | tf_op jit(solution)/shard_map/ppermute | solution.py:373
  29.0 5.1 %collective-permute-start.8 = (bf16[160,256]{1,0:T(8,128)(2,1)S(1)}, bf16[160,256]{1,0:T(8,128)(2,1)S(1)}, u32[]{:S(2)}, u32[]{:S(2)}) collective-permute-start(bf16[160,256]{1,0:T(8,128)(2,1)S(1)} %get-tuple-element.167), channel_id=1, source_target_pairs={{0,2},{1,3},{2,0},{3,1},{4,6},{5,7},{6,4},{7,5},{8,10},{9,11},{10,... | collective-permute-start | bytes 245768 | tf_op jit(solution)/shard_map/ppermute | solution.py:373
  30.6 5.3 %collective-permute-start.9 = (bf16[160,256]{1,0:T(8,128)(2,1)S(1)}, bf16[160,256]{1,0:T(8,128)(2,1)S(1)}, u32[]{:S(2)}, u32[]{:S(2)}) collective-permute-start(bf16[160,256]{1,0:T(8,128)(2,1)S(1)} %get-tuple-element.168), channel_id=1, source_target_pairs={{0,6},{1,7},{2,4},{3,5},{4,2},{5,3},{6,0},{7,1},{8,14},{9,15},{10,... | collective-permute-start | bytes 245768 | tf_op jit(solution)/shard_map/ppermute | solution.py:373
  33.3 2.8 %collective-permute-start.10 = (bf16[1024,256]{1,0:T(8,128)(2,1)S(1)}, bf16[1024,256]{1,0:T(8,128)(2,1)S(1)}, u32[]{:S(2)}, u32[]{:S(2)}) collective-permute-start(bf16[1024,256]{1,0:T(8,128)(2,1)S(1)} %get-tuple-element.145), channel_id=1, source_target_pairs={{0,1},{1,0},{2,3},{3,2},{4,5},{5,4},{6,7},{7,6},{8,9},{9,8},{10,11... | collective-permute-start | bytes 1572872 | tf_op jit(solution)/shard_map/ppermute | solution.py:369
  36.2 5.0 %collective-permute-start.11 = (bf16[256,256]{1,0:T(8,128)(2,1)S(1)}, bf16[256,256]{1,0:T(8,128)(2,1)S(1)}, u32[]{:S(2)}, u32[]{:S(2)}) collective-permute-start(bf16[256,256]{1,0:T(8,128)(2,1)S(1)} %pad_maximum_fusion.2), channel_id=1, source_target_pairs={{0,8},{4,12},{8,0},{12,4},{16,24},{20,28},{24,16},{28,20},{1,9},{5... | collective-permute-start | bytes 393224 | tf_op jit(solution)/shard_map/ppermute | solution.py:369
  36.3 3.7 %collective-permute-start.14 = (s32[4,2,8]{2,1,0:T(2,128)S(1)}, s32[4,2,8]{2,1,0:T(2,128)S(1)}, u32[]{:S(2)}, u32[]{:S(2)}) collective-permute-start(s32[4,2,8]{2,1,0:T(2,128)S(1)} %pad_add_fusion.1), channel_id=1, source_target_pairs={{0,4},{4,0},{8,12},{12,8},{16,20},{20,16},{24,28},{28,24},{1,5},{5... | collective-permute-start | bytes 776 | tf_op jit(solution)/shard_map/ppermute | solution.py:369
  37.2 7.7 %collective-permute-start.13 = (bf16[512,256]{1,0:T(8,128)(2,1)S(1)}, bf16[512,256]{1,0:T(8,128)(2,1)S(1)}, u32[]{:S(2)}, u32[]{:S(2)}) collective-permute-start(bf16[512,256]{1,0:T(8,128)(2,1)S(1)} %slice.220), channel_id=1, source_target_pairs={{0,2},{1,3},{2,0},{3,1},{4,6},{5,7},{6,4},{7,5},{8,10},{9,11},{10,... | collective-permute-start | bytes 786440 | tf_op jit(solution)/shard_map/ppermute | solution.py:369
  41.4 7.2 %collective-permute-start.12 = (bf16[240,256]{1,0:T(8,128)(2,1)S(1)}, bf16[240,256]{1,0:T(8,128)(2,1)S(1)}, u32[]{:S(2)}, u32[]{:S(2)}) collective-permute-start(bf16[240,256]{1,0:T(8,128)(2,1)S(1)} %pad_maximum_fusion.3), channel_id=1, source_target_pairs={{0,16},{4,20},{8,24},{12,28},{16,0},{20,4},{24,8},{28,12},{1,17},{... | collective-permute-start | bytes 368648 | tf_op jit(solution)/shard_map/ppermute | solution.py:369
  48.6 1.4 %collective-permute-start.15 = (f32[88,256]{1,0:T(8,128)S(1)}, f32[88,256]{1,0:T(8,128)S(1)}, u32[]{:S(2)}, u32[]{:S(2)}) collective-permute-start(f32[88,256]{1,0:T(8,128)S(1)} %slice_add_fusion.mine), channel_id=1, source_target_pairs={{0,1},{1,0},{2,3},{3,2},{4,5},{5,4},{6,7},{7,6},{8,9},{9,8},{10,11... | collective-permute-start | bytes 270344 | tf_op jit(solution)/shard_map/ppermute | solution.py:369

commit v6 on v5

--- a/solution.py
+++ b/solution.py
@@ -117,7 +117,7 @@
     live_hour[:m, :] = (used & ((lane_hour // HB) == spread(hour_col, 2 * HALF))).astype(F32)
 
 
-def work(sizes, m, first, last, q, state, table, hours_tab, user_terms, item_sums, grad_hour, before=None, stack=8):
+def work(sizes, m, first, last, q, state, table, hours_tab, user_terms, item_sums, grad_hour, before=None, stack=8, fine=True):
     obs, live_hour, user_rows, pick, put, _ = state
     slots = pick.shape[1]
     parts = range(table.shape[0])
@@ -161,8 +161,10 @@
             total += mine * rows[j]
             terms = mine * users_f
             high = terms.astype(BF16)
-            low = (terms - high.astype(F32)).astype(BF16)
-            sums = jnp.dot(into, high, preferred_element_type=F32) + jnp.dot(into, low, preferred_element_type=F32)
+            sums = jnp.dot(into, high, preferred_element_type=F32)
+            if fine:
+                low = (terms - high.astype(F32)).astype(BF16)
+                sums += jnp.dot(into, low, preferred_element_type=F32)
             for part in parts:
                 item_sums[part, pl.ds(a, slots, stride=IB), :] = sums[:, part * 128 : part * 128 + 128]
         user_terms[:m, :] = total
@@ -297,7 +299,7 @@
     _, number = chosen_blocks(sizes, False, count[0], slot[...])
 
     def run(m):
-        work(sizes, m, 0, IB, q, state, table, hours_tab, user_terms, item_sums, grad_hour)
+        work(sizes, m, 0, IB, q, state, table, hours_tab, user_terms, item_sums, grad_hour, fine=False)
 
     in_size(number, (sizes.cold_blocks // 4 * 3, sizes.cold_blocks), slot.shape[1], run)
 
@@ -512,7 +514,7 @@
     got, cold_terms = lax.optimization_barrier((got, cold_terms))
     hot = keep[:split_hot] + got[:split_hot].astype(F32)
     hour = keep[split_hot:] + got[split_hot : split_hot + high_rows].astype(F32)
-    hour += got[split_hot + high_rows :].astype(F32)
+    hour = (hour + got[split_hot + high_rows :].astype(F32))[:half]
     send_user, user = call(
         users_kernel,
         (block_count,),
@@ -535,9 +537,9 @@
         turn(jnp.concatenate(part, axis=0), ("users", "items"), peers * items, change)
         for part, change in zip(parts, changes)
     ]
-    back = got[0][rows + high_rows :]
+    back = got[0][rows + half :]
     returned = jnp.concatenate([returned[:size], back.reshape(returned[:size].shape)], axis=1)
-    got = [one[: rows + high_rows] for one in got]
+    got = [one[: rows + half] for one in got]
     hot = hot[:rows] + sum(one[:rows].astype(F32) for one in got)
     by_user, by_item, by_both = [one[rows:].astype(F32) for one in got]
     hour = (high + by_item) + (by_user + by_both)
@@ -558,9 +560,9 @@
         if bit == last:
             user = user[:keep_user] + got_user.astype(F32)
             got, user, needs = lax.optimization_barrier((got, user, needs))
-        back = got[rows + high_rows :]
+        back = got[rows + half :]
         returned = jnp.concatenate([returned[:size], back.reshape(returned[:size].shape)], axis=1)
-        hour = high + got[rows : rows + high_rows].astype(F32)
+        hour = high + got[rows : rows + half].astype(F32)
         if bit < last:
             hot = hot[:rows] + got[:rows].astype(F32)
     hot, got_hot = hot[:rows], got[:rows]

time: 50.8 us -> 50.3 us (level)
  no operation moved by 1% of the time
where the time goes in v6:
time: 50.3 us; the launch traced here: 50.1 us
  starting transfers between devices  19.4 us (39%)
  Pallas kernels  16.3 us (32%)
  waiting for transfers between devices  11.4 us (23%)
  between operations  1.64 us (3%)
  other arithmetic  1.21 us (2%)
    pallas_call x8, Pallas kernels, call(): pl.pallas_call(functools.partial(function, sizes), out_shape=out_shape, i...  16.3 us
    ppermute x10, starting transfers between devices, hop(): return lax.ppermute(values, axis, [(i, i ^ 1 << bit) for i in range(size)])  11.3 us
    ppermute x10, waiting for transfers between devices, hop(): return lax.ppermute(values, axis, [(i, i ^ 1 << bit) for i in range(size)])  8.9 us
    ppermute x6, starting transfers between devices, turn(): return lax.ppermute(values, axis, [(i, i ^ change) for i in range(size)])  8.07 us
    ppermute x6, waiting for transfers between devices, turn(): return lax.ppermute(values, axis, [(i, i ^ change) for i in range(size)])  2.52 us
  transfers between devices with their start and end apart: 16, of which 8 were waited for; matrix products, arithmetic and copies ran while one was open for 2% of the time, Pallas kernels for 24%

profile of v6, /device:TPU:0, one launch (start us, length us, event | category | flops | bytes accessed | tf_op | source)
XLA Modules:
  0.0 50.1 jit_solution(3240842964320369507)
XLA Ops:
  0.6 3.0 %collective-permute-start.1 = (bf16[256,256]{1,0:T(8,128)(2,1)}, bf16[256,256]{1,0:T(8,128)(2,1)S(1)}, u32[]{:S(2)}, u32[]{:S(2)}) collective-permute-start(bf16[256,256]{1,0:T(8,128)(2,1)} %refs_3_.1), channel_id=1, source_target_pairs={{0,4},{4,0},{8,12},{12,8},{16,20},{20,16},{24,28},{28,24},{1,5},{5... | collective-permute-start | bytes 393224 | tf_op jit(solution)/shard_map/ppermute | solution.py:371
  3.7 1.6 %collective-permute-start = (s32[1,2,8]{2,1,0:T(2,128)S(1)}, s32[1,2,8]{2,1,0:T(2,128)S(1)}, u32[]{:S(2)}, u32[]{:S(2)}) collective-permute-start(s32[1,2,8]{2,1,0:T(2,128)S(1)} %bitcast.14), channel_id=1, source_target_pairs={{0,8},{4,12},{8,0},{12,4},{16,24},{20,28},{24,16},{28,20},{1,9},{5... | collective-permute-start | bytes 200 | tf_op jit(solution)/shard_map/ppermute | solution.py:371
  5.9 2.7 %first_kernel.1 = (f32[512,128]{1,0:T(8,128)S(1)}, f32[512,256]{1,0:T(8,128)S(1)}, f32[512,256]{1,0:T(8,128)S(1)}, bf16[512,32]{1,0:T(8,128)(2,1)S(1)}, bf16[32,...) custom-call(s32[1]{0:T(128)S(6)} %copy.15.count, ...), custom_call_target="tpu_custom_call" | custom-call | flops 100000000 | bytes 4194304 | tf_op jit(solution)/shard_map/first_kernel/pallas_call | solution.py:432
  8.6 2.7 %collective-permute-start.2 = (s32[2,2,8]{2,1,0:T(2,128)S(1)}, s32[2,2,8]{2,1,0:T(2,128)S(1)}, u32[]{:S(2)}, u32[]{:S(2)}) collective-permute-start(s32[2,2,8]{2,1,0:T(2,128)S(1)} %pad_add_fusion.2), channel_id=1, source_target_pairs={{0,16},{4,20},{8,24},{12,28},{16,0},{20,4},{24,8},{28,12},{1,17},{... | collective-permute-start | bytes 392 | tf_op jit(solution)/shard_map/ppermute | solution.py:371
  11.3 2.5 %half_kernel.1 = (f32[512,256]{1,0:T(8,128)S(1)}, f32[2,512,128]{2,1,0:T(8,128)S(1)}, f32[176,256]{1,0:T(8,128)S(1)}) custom-call(s32[1]{0:T(128)S(6)} %copy.15.count, f32[512,128]{1,0:T(8,128)S(1)} %get-tuple-element.111.obs, f32[512,256]{1,0:T(8,128)S(1)} %get-tuple-element.112.live_hour, f32[512,256]{1,0:T(8,128)S(1)} %get-tuple-element.113.user_rows, ...), custom_call_target="tpu_custom_call" | custom-call | flops 3000000000 | bytes 4194304 | tf_op jit(solution)/shard_map/half_kernel/pallas_call | solution.py:432
  15.0 2.0 %collective-permute-start.4 = (bf16[64,256]{1,0:T(8,128)(2,1)S(1)}, bf16[64,256]{1,0:T(8,128)(2,1)S(1)}, u32[]{:S(2)}, u32[]{:S(2)}) collective-permute-start(bf16[64,256]{1,0:T(8,128)(2,1)S(1)} %get-tuple-element.135), channel_id=1, source_target_pairs={{0,16},{4,20},{8,24},{12,28},{16,0},{20,4},{24,8},{28,12},{1,17},{... | collective-permute-start | bytes 98312 | tf_op jit(solution)/shard_map/ppermute | solution.py:375
  17.0 1.9 %collective-permute-start.5 = (bf16[64,256]{1,0:T(8,128)(2,1)S(1)}, bf16[64,256]{1,0:T(8,128)(2,1)S(1)}, u32[]{:S(2)}, u32[]{:S(2)}) collective-permute-start(bf16[64,256]{1,0:T(8,128)(2,1)S(1)} %get-tuple-element.136), channel_id=1, source_target_pairs={{0,24},{4,28},{8,16},{12,20},{16,8},{20,12},{24,0},{28,4},{1,25},{... | collective-permute-start | bytes 98312 | tf_op jit(solution)/shard_map/ppermute | solution.py:375
  18.9 4.0 %second_kernel.1 = (f32[512,128]{1,0:T(8,128)S(1)}, f32[512,256]{1,0:T(8,128)S(1)}, f32[512,256]{1,0:T(8,128)S(1)}, bf16[512,16]{1,0:T(8,128)(2,1)S(1)}, bf16[16...) custom-call(s32[1]{0:T(128)S(6)} %copy.15.count, ...), custom_call_target="tpu_custom_call" | custom-call | flops 5000000000 | bytes 4194304 | tf_op jit(solution)/shard_map/second_kernel/pallas_call | solution.py:432
  23.0 2.8 %third_kernel.1 = (bf16[448,256]{1,0:T(8,128)(2,1)S(1)}, f32[352,256]{1,0:T(8,128)S(1)}, bf16[256,256]{1,0:T(8,128)(2,1)S(1)}, f32[512,256]{1,0:T(8,128)S(1)}) custom-call(s32[1]{0:T(128)S(6)} %copy.15.count, s32[1,512]{1,0:T(1,128)S(1)} %get-tuple-element.120.slot, bf16[256,256]{1,0:T(8,128)(2,1)S(1)} %get-tuple-element.118.hours_tab, ...), custom_call_target="tpu_custom_call" | custom-call | flops 5000000000 | bytes 4194304 | tf_op jit(solution)/shard_map/third_kernel/pallas_call | solution.py:432
  25.9 1.4 %collective-permute-done.6 = bf16[448,256]{1,0:T(8,128)(2,1)S(1)} collective-permute-done((bf16[448,256]{1,0:T(8,128)(2,1)S(1)}, bf16[448,256]{1,0:T(8,128)(2,1)S(1)}, u32[]{:S(2)}, u32[]{:S(2)}) %collective-permute-start.6) | collective-permute-done | bytes 229408 | tf_op jit(solution)/shard_map/ppermute | solution.py:371
  27.4 1.3 %collective-permute-start.7 = (bf16[280,256]{1,0:T(8,128)(2,1)S(1)}, bf16[280,256]{1,0:T(8,128)(2,1)S(1)}, u32[]{:S(2)}, u32[]{:S(2)}) collective-permute-start(bf16[280,256]{1,0:T(8,128)(2,1)S(1)} %pad_maximum_fusion), channel_id=1, source_target_pairs={{0,4},{1,5},{2,6},{3,7},{4,0},{5,1},{6,2},{7,3},{8,12},{9,13},{10,... | collective-permute-start | bytes 430088 | tf_op jit(solution)/shard_map/ppermute | solution.py:375
  28.7 1.6 %collective-permute-start.8 = (bf16[152,256]{1,0:T(8,128)(2,1)S(1)}, bf16[152,256]{1,0:T(8,128)(2,1)S(1)}, u32[]{:S(2)}, u32[]{:S(2)}) collective-permute-start(bf16[152,256]{1,0:T(8,128)(2,1)S(1)} %get-tuple-element.167), channel_id=1, source_target_pairs={{0,2},{1,3},{2,0},{3,1},{4,6},{5,7},{6,4},{7,5},{8,10},{9,11},{10,... | collective-permute-start | bytes 233480 | tf_op jit(solution)/shard_map/ppermute | solution.py:375
  30.3 0.8 %collective-permute-start.9 = (bf16[152,256]{1,0:T(8,128)(2,1)S(1)}, bf16[152,256]{1,0:T(8,128)(2,1)S(1)}, u32[]{:S(2)}, u32[]{:S(2)}) collective-permute-start(bf16[152,256]{1,0:T(8,128)(2,1)S(1)} %get-tuple-element.168), channel_id=1, source_target_pairs={{0,6},{1,7},{2,4},{3,5},{4,2},{5,3},{6,0},{7,1},{8,14},{9,15},{10,... | collective-permute-start | bytes 233480 | tf_op jit(solution)/shard_map/ppermute | solution.py:375
  31.0 1.9 %users_kernel.1 = (bf16[1024,256]{1,0:T(8,128)(2,1)S(1)}, f32[1024,256]{1,0:T(8,128)S(1)}) custom-call(s32[1]{0:T(128)S(6)} %copy.15.count, s32[1,512]{1,0:T(1,128)S(1)} %get-tuple-element.120.slot, s32[1,512]{1,0:T(1,128)S(1)} %get-tuple-element.116.user_pos.pos, f32[512,256]{1,0:T(8,128)S(1)} %get-tuple-element.142.terms, ...), custom_call_target="tpu_custom_call" | custom-call | flops 1000000000 | bytes 4194304 | tf_op jit(solution)/shard_map/users_kernel/pallas_call | solution.py:432
  33.7 1.9 %collective-permute-done.9 = bf16[152,256]{1,0:T(8,128)(2,1)S(1)} collective-permute-done((bf16[152,256]{1,0:T(8,128)(2,1)S(1)}, bf16[152,256]{1,0:T(8,128)(2,1)S(1)}, u32[]{:S(2)}, u32[]{:S(2)}) %collective-permute-start.9) | collective-permute-done | bytes 77856 | tf_op jit(solution)/shard_map/ppermute | solution.py:375
  35.9 0.8 %collective-permute-start.14 = (s32[4,2,8]{2,1,0:T(2,128)S(1)}, s32[4,2,8]{2,1,0:T(2,128)S(1)}, u32[]{:S(2)}, u32[]{:S(2)}) collective-permute-start(s32[4,2,8]{2,1,0:T(2,128)S(1)} %pad_add_fusion.1), channel_id=1, source_target_pairs={{0,4},{4,0},{8,12},{12,8},{16,20},{20,16},{24,28},{28,24},{1,5},{5... | collective-permute-start | bytes 776 | tf_op jit(solution)/shard_map/ppermute | solution.py:371
  36.8 1.4 %collective-permute-start.13 = (bf16[512,256]{1,0:T(8,128)(2,1)S(1)}, bf16[512,256]{1,0:T(8,128)(2,1)S(1)}, u32[]{:S(2)}, u32[]{:S(2)}) collective-permute-start(bf16[512,256]{1,0:T(8,128)(2,1)S(1)} %slice.225), channel_id=1, source_target_pairs={{0,2},{1,3},{2,0},{3,1},{4,6},{5,7},{6,4},{7,5},{8,10},{9,11},{10,... | collective-permute-start | bytes 786440 | tf_op jit(solution)/shard_map/ppermute | solution.py:371
  38.2 1.4 %collective-permute-done.14 = s32[4,2,8]{2,1,0:T(2,128)S(1)} collective-permute-done((s32[4,2,8]{2,1,0:T(2,128)S(1)}, s32[4,2,8]{2,1,0:T(2,128)S(1)}, u32[]{:S(2)}, u32[]{:S(2)}) %collective-permute-start.14) | collective-permute-done | bytes 288 | tf_op jit(solution)/shard_map/ppermute | solution.py:371
  39.6 1.2 %collective-permute-done.11 = bf16[248,256]{1,0:T(8,128)(2,1)S(1)} collective-permute-done((bf16[248,256]{1,0:T(8,128)(2,1)S(1)}, bf16[248,256]{1,0:T(8,128)(2,1)S(1)}, u32[]{:S(2)}, u32[]{:S(2)}) %collective-permute-start.11) | collective-permute-done | bytes 127008 | tf_op jit(solution)/shard_map/ppermute | solution.py:371
  41.0 1.5 %collective-permute-start.12 = (bf16[232,256]{1,0:T(8,128)(2,1)S(1)}, bf16[232,256]{1,0:T(8,128)(2,1)S(1)}, u32[]{:S(2)}, u32[]{:S(2)}) collective-permute-start(bf16[232,256]{1,0:T(8,128)(2,1)S(1)} %pad_maximum_fusion.3), channel_id=1, source_target_pairs={{0,16},{4,20},{8,24},{12,28},{16,0},{20,4},{24,8},{28,12},{1,17},{... | collective-permute-start | bytes 356360 | tf_op jit(solution)/shard_map/ppermute | solution.py:371
  42.5 2.1 %collective-permute-done.13 = bf16[512,256]{1,0:T(8,128)(2,1)S(1)} collective-permute-done((bf16[512,256]{1,0:T(8,128)(2,1)S(1)}, bf16[512,256]{1,0:T(8,128)(2,1)S(1)}, u32[]{:S(2)}, u32[]{:S(2)}) %collective-permute-start.13) | collective-permute-done | bytes 262176 | tf_op jit(solution)/shard_map/ppermute | solution.py:371
  44.6 0.8 %convert_add_fusion.1 = f32[512,256]{1,0:T(8,128)} fusion(bf16[512,256]{1,0:T(8,128)(2,1)S(1)} %collective-permute-done.13, f32[1024,256]{1,0:T(8,128)S(1)} %convert_add_fusion), kind=kLoop, calls=%fused_computation.2 | loop fusion | flops 262144 | bytes 1310720 | tf_op jit(solution)/shard_map/add | solution.py:561
  45.5 2.6 %collective-permute-done.12 = bf16[232,256]{1,0:T(8,128)(2,1)S(1)} collective-permute-done((bf16[232,256]{1,0:T(8,128)(2,1)S(1)}, bf16[232,256]{1,0:T(8,128)(2,1)S(1)}, u32[]{:S(2)}, u32[]{:S(2)}) %collective-permute-start.12) | collective-permute-done | bytes 118816 | tf_op jit(solution)/shard_map/ppermute | solution.py:371
  48.2 1.1 %last_rows.1 = (f32[256,256]{1,0:T(8,128)}, f32[16,256]{1,0:T(8,128)}) custom-call(s32[16,8]{1,0:T(8,128)S(1)} %bitcast.18, bf16[256,256]{1,0:T(8,128)(2,1)S(1)} %maximum_bitcast_fusion.returned, f32[16,256]{1,0:T(8,128)S(1)} %slice.179.hot, bf16[16,256]{1,0:T(8,128)(2,1)S(1)} %slice.152.got), custom_call_target="tpu_custom_call" | custom-call | flops 100000000 | bytes 4194304 | tf_op jit(solution)/shard_map/last_rows/pallas_call | solution.py:432
  (53 shorter events, 3.4 us)
Async XLA Ops:
  0.6 3.0 %copy-start.1 = (s32[1,8,2]{1,2,0:T(2,128)S(1)}, s32[1,8,2]{1,2,0:T(2,128)}, u32[]{:S(2)}) copy-start(s32[1,8,2]{1,2,0:T(2,128)} %param.18) | copy-start | bytes 196
  0.6 7.9 %collective-permute-start.1 = (bf16[256,256]{1,0:T(8,128)(2,1)}, bf16[256,256]{1,0:T(8,128)(2,1)S(1)}, u32[]{:S(2)}, u32[]{:S(2)}) collective-permute-start(bf16[256,256]{1,0:T(8,128)(2,1)} %refs_3_.1), channel_id=1, source_target_pairs={{0,4},{4,0},{8,12},{12,8},{16,20},{20,16},{24,28},{28,24},{1,5},{5... | collective-permute-start | bytes 393224 | tf_op jit(solution)/shard_map/ppermute | solution.py:371
  3.7 4.9 %collective-permute-start = (s32[1,2,8]{2,1,0:T(2,128)S(1)}, s32[1,2,8]{2,1,0:T(2,128)S(1)}, u32[]{:S(2)}, u32[]{:S(2)}) collective-permute-start(s32[1,2,8]{2,1,0:T(2,128)S(1)} %bitcast.14), channel_id=1, source_target_pairs={{0,8},{4,12},{8,0},{12,4},{16,24},{20,28},{24,16},{28,20},{1,9},{5... | collective-permute-start | bytes 200 | tf_op jit(solution)/shard_map/ppermute | solution.py:371
  8.6 5.2 %copy-start = (bf16[256,256]{1,0:T(8,128)(2,1)S(1)}, bf16[256,256]{1,0:T(8,128)(2,1)}, u32[]{:S(2)}) copy-start(bf16[256,256]{1,0:T(8,128)(2,1)} %refs_3_.1) | copy-start | bytes 393220
  8.6 5.2 %collective-permute-start.2 = (s32[2,2,8]{2,1,0:T(2,128)S(1)}, s32[2,2,8]{2,1,0:T(2,128)S(1)}, u32[]{:S(2)}, u32[]{:S(2)}) collective-permute-start(s32[2,2,8]{2,1,0:T(2,128)S(1)} %pad_add_fusion.2), channel_id=1, source_target_pairs={{0,16},{4,20},{8,24},{12,28},{16,0},{20,4},{24,8},{28,12},{1,17},{... | collective-permute-start | bytes 392 | tf_op jit(solution)/shard_map/ppermute | solution.py:371
  14.5 8.5 %collective-permute-start.3 = (bf16[64,256]{1,0:T(8,128)(2,1)S(1)}, bf16[64,256]{1,0:T(8,128)(2,1)S(1)}, u32[]{:S(2)}, u32[]{:S(2)}) collective-permute-start(bf16[64,256]{1,0:T(8,128)(2,1)S(1)} %get-tuple-element.134), channel_id=1, source_target_pairs={{0,8},{4,12},{8,0},{12,4},{16,24},{20,28},{24,16},{28,20},{1,9},{5... | collective-permute-start | bytes 98312 | tf_op jit(solution)/shard_map/ppermute | solution.py:375
  15.0 7.9 %collective-permute-start.4 = (bf16[64,256]{1,0:T(8,128)(2,1)S(1)}, bf16[64,256]{1,0:T(8,128)(2,1)S(1)}, u32[]{:S(2)}, u32[]{:S(2)}) collective-permute-start(bf16[64,256]{1,0:T(8,128)(2,1)S(1)} %get-tuple-element.135), channel_id=1, source_target_pairs={{0,16},{4,20},{8,24},{12,28},{16,0},{20,4},{24,8},{28,12},{1,17},{... | collective-permute-start | bytes 98312 | tf_op jit(solution)/shard_map/ppermute | solution.py:375
  17.0 6.0 %collective-permute-start.5 = (bf16[64,256]{1,0:T(8,128)(2,1)S(1)}, bf16[64,256]{1,0:T(8,128)(2,1)S(1)}, u32[]{:S(2)}, u32[]{:S(2)}) collective-permute-start(bf16[64,256]{1,0:T(8,128)(2,1)S(1)} %get-tuple-element.136), channel_id=1, source_target_pairs={{0,24},{4,28},{8,16},{12,20},{16,8},{20,12},{24,0},{28,4},{1,25},{... | collective-permute-start | bytes 98312 | tf_op jit(solution)/shard_map/ppermute | solution.py:375
  25.7 1.6 %collective-permute-start.6 = (bf16[448,256]{1,0:T(8,128)(2,1)S(1)}, bf16[448,256]{1,0:T(8,128)(2,1)S(1)}, u32[]{:S(2)}, u32[]{:S(2)}) collective-permute-start(bf16[448,256]{1,0:T(8,128)(2,1)S(1)} %get-tuple-element.138), channel_id=1, source_target_pairs={{0,1},{1,0},{2,3},{3,2},{4,5},{5,4},{6,7},{7,6},{8,9},{9,8},{10,11... | collective-permute-start | bytes 688136 | tf_op jit(solution)/shard_map/ppermute | solution.py:371
  27.4 8.2 %collective-permute-start.7 = (bf16[280,256]{1,0:T(8,128)(2,1)S(1)}, bf16[280,256]{1,0:T(8,128)(2,1)S(1)}, u32[]{:S(2)}, u32[]{:S(2)}) collective-permute-start(bf16[280,256]{1,0:T(8,128)(2,1)S(1)} %pad_maximum_fusion), channel_id=1, source_target_pairs={{0,4},{1,5},{2,6},{3,7},{4,0},{5,1},{6,2},{7,3},{8,12},{9,13},{10,... | collective-permute-start | bytes 430088 | tf_op jit(solution)/shard_map/ppermute | solution.py:375
  28.7 5.0 %collective-permute-start.8 = (bf16[152,256]{1,0:T(8,128)(2,1)S(1)}, bf16[152,256]{1,0:T(8,128)(2,1)S(1)}, u32[]{:S(2)}, u32[]{:S(2)}) collective-permute-start(bf16[152,256]{1,0:T(8,128)(2,1)S(1)} %get-tuple-element.167), channel_id=1, source_target_pairs={{0,2},{1,3},{2,0},{3,1},{4,6},{5,7},{6,4},{7,5},{8,10},{9,11},{10,... | collective-permute-start | bytes 233480 | tf_op jit(solution)/shard_map/ppermute | solution.py:375
  30.3 5.3 %collective-permute-start.9 = (bf16[152,256]{1,0:T(8,128)(2,1)S(1)}, bf16[152,256]{1,0:T(8,128)(2,1)S(1)}, u32[]{:S(2)}, u32[]{:S(2)}) collective-permute-start(bf16[152,256]{1,0:T(8,128)(2,1)S(1)} %get-tuple-element.168), channel_id=1, source_target_pairs={{0,6},{1,7},{2,4},{3,5},{4,2},{5,3},{6,0},{7,1},{8,14},{9,15},{10,... | collective-permute-start | bytes 233480 | tf_op jit(solution)/shard_map/ppermute | solution.py:375
  33.0 2.7 %collective-permute-start.10 = (bf16[1024,256]{1,0:T(8,128)(2,1)S(1)}, bf16[1024,256]{1,0:T(8,128)(2,1)S(1)}, u32[]{:S(2)}, u32[]{:S(2)}) collective-permute-start(bf16[1024,256]{1,0:T(8,128)(2,1)S(1)} %get-tuple-element.145), channel_id=1, source_target_pairs={{0,1},{1,0},{2,3},{3,2},{4,5},{5,4},{6,7},{7,6},{8,9},{9,8},{10,11... | collective-permute-start | bytes 1572872 | tf_op jit(solution)/shard_map/ppermute | solution.py:371
  35.8 5.0 %collective-permute-start.11 = (bf16[248,256]{1,0:T(8,128)(2,1)S(1)}, bf16[248,256]{1,0:T(8,128)(2,1)S(1)}, u32[]{:S(2)}, u32[]{:S(2)}) collective-permute-start(bf16[248,256]{1,0:T(8,128)(2,1)S(1)} %pad_maximum_fusion.2), channel_id=1, source_target_pairs={{0,8},{4,12},{8,0},{12,4},{16,24},{20,28},{24,16},{28,20},{1,9},{5... | collective-permute-start | bytes 380936 | tf_op jit(solution)/shard_map/ppermute | solution.py:371
  35.9 3.7 %collective-permute-start.14 = (s32[4,2,8]{2,1,0:T(2,128)S(1)}, s32[4,2,8]{2,1,0:T(2,128)S(1)}, u32[]{:S(2)}, u32[]{:S(2)}) collective-permute-start(s32[4,2,8]{2,1,0:T(2,128)S(1)} %pad_add_fusion.1), channel_id=1, source_target_pairs={{0,4},{4,0},{8,12},{12,8},{16,20},{20,16},{24,28},{28,24},{1,5},{5... | collective-permute-start | bytes 776 | tf_op jit(solution)/shard_map/ppermute | solution.py:371
  36.8 7.8 %collective-permute-start.13 = (bf16[512,256]{1,0:T(8,128)(2,1)S(1)}, bf16[512,256]{1,0:T(8,128)(2,1)S(1)}, u32[]{:S(2)}, u32[]{:S(2)}) collective-permute-start(bf16[512,256]{1,0:T(8,128)(2,1)S(1)} %slice.225), channel_id=1, source_target_pairs={{0,2},{1,3},{2,0},{3,1},{4,6},{5,7},{6,4},{7,5},{8,10},{9,11},{10,... | collective-permute-start | bytes 786440 | tf_op jit(solution)/shard_map/ppermute | solution.py:371
  41.0 7.1 %collective-permute-start.12 = (bf16[232,256]{1,0:T(8,128)(2,1)S(1)}, bf16[232,256]{1,0:T(8,128)(2,1)S(1)}, u32[]{:S(2)}, u32[]{:S(2)}) collective-permute-start(bf16[232,256]{1,0:T(8,128)(2,1)S(1)} %pad_maximum_fusion.3), channel_id=1, source_target_pairs={{0,16},{4,20},{8,24},{12,28},{16,0},{20,4},{24,8},{28,12},{1,17},{... | collective-permute-start | bytes 356360 | tf_op jit(solution)/shard_map/ppermute | solution.py:371
  48.1 1.4 %collective-permute-start.15 = (f32[88,256]{1,0:T(8,128)S(1)}, f32[88,256]{1,0:T(8,128)S(1)}, u32[]{:S(2)}, u32[]{:S(2)}) collective-permute-start(f32[88,256]{1,0:T(8,128)S(1)} %convert_add_fusion.3.mine), channel_id=1, source_target_pairs={{0,1},{1,0},{2,3},{3,2},{4,5},{5,4},{6,7},{7,6},{8,9},{9,8},{10,11... | collective-permute-start | bytes 270344 | tf_op jit(solution)/shard_map/ppermute | solution.py:371
